TPU v7x, 256 devices: a whole 4x4x8 slice. The times are simulated.
256 devices in a mesh: expert: 32 (over z, x), dp: 8 (over y, core).
Axes of the slice: x: 4, y: 4, z: 8, core: 2. Of those that a mesh axis runs over, the one named last changes fastest.
Arguments:
- upper_out: float32 [32768, 2048], P(('expert', 'dp')), may hold values from -3 to 3
- lower_out: bfloat16 [32768, 2048], P(('expert', 'dp')), may hold values from -6 to 6
- upper_cot: bfloat16 [32768, 2048], P(('expert', 'dp')), may hold values from -6 to 6
- lower_cot: bfloat16 [32768, 2048], P(('expert', 'dp')), may hold values from -3 to 3
- gate_up_weight: bfloat16 [32, 2048, 1408], P('expert', 'dp'), may hold values from -0.125 to 0.125
- down_weight: bfloat16 [32, 2048, 704], P('expert', 'dp'), may hold values from -0.21875 to 0.21875
- router_weight: float32 [2048, 32], replicated, may hold values from -0.125 to 0.125
- expert_ids: int32 [32768, 2], P(('expert', 'dp')), may hold values from 0 to 31, all different within a row; in each aligned block of 128 rows (0 to 127, 128 to 255, ...) at most 9 rows name the same one
- keep_mask: int32 [32768, 2], P(('expert', 'dp')), may hold values 0 or 1
Outputs:
- upper_input: float32 [32768, 2048], P(('expert', 'dp'))
- lower_grad: float32 [32768, 2048], P(('expert', 'dp'))
- gate_up_grad: bfloat16 [32, 2048, 1408], P('expert', 'dp')
- down_grad: bfloat16 [32, 2048, 704], P('expert', 'dp')
- router_grad: float32 [2048, 32], replicated
Inputs may be any that keep to these rules, and one draw needn't show every extreme that they name: `expert_ids`: each row names 2 different experts. Within the rows of one device (aligned blocks of 128 rows) no expert is named by more than 9 rows, a bound that some block reaches.
All inputs are finite; a program needn't handle non-finite values. No bound on the sum of `keep_mask` on one device may be relied on, other than what follows from the above.
Results may differ from a plain program's by a relative error of at most 0.017.
Values may be sent and summed in bfloat16 or wider, within the bound.
No kernel may reach another device: no remote copies, remote signals or barrier semaphores. Data moves between devices by JAX's collectives and lax.ppermute only.
A program may use at most 128 MiB of HBM per device.

v0:
```python
import jax
import jax.numpy as jnp
from jax import lax
from jax.sharding import PartitionSpec as P

residual_scale = 128.0 ** (-0.5)
highest = lax.Precision.HIGHEST
contract_last = (((1,), (1,)), ((), ()))
contract_first = (((0,), (0,)), ((), ()))


def body(
    upper_out,
    lower_out,
    upper_cot,
    lower_cot,
    gate_up_weight,
    down_weight,
    router_weight,
    expert_ids,
    keep_mask,
):
    tokens, features = lower_out.shape
    experts = router_weight.shape[1]
    top_count = expert_ids.shape[1]
    capacity = (tokens * top_count * 9 + 8 * experts - 1) // (8 * experts)
    assign = tokens * top_count
    slots = experts * capacity
    hidden_units = down_weight.shape[2]
    gate_up_local = gate_up_weight[0]
    down_local = down_weight[0]
    expert_range = jnp.arange(experts, dtype=jnp.int32)
    flat_ids = expert_ids.reshape(assign)
    flat_kept = keep_mask.reshape(assign)
    onehot = (flat_ids[:, None] == expert_range).astype(jnp.int32)
    slot_rank = jnp.sum(onehot * (jnp.cumsum(onehot, axis=0) - 1), axis=1)
    slot_pos = flat_ids * capacity + slot_rank
    slot_src = (
        jnp.full((slots,), assign, jnp.int32).at[slot_pos].set(jnp.arange(assign, dtype=jnp.int32))
    )
    kept_ext = jnp.concatenate([flat_kept, jnp.zeros((1,), jnp.int32)])
    slot_tok = jnp.where(kept_ext[slot_src] > 0, slot_src // top_count, tokens)
    logits = jnp.dot(lower_out.astype(jnp.float32), router_weight, precision=highest)
    pair_hot = (expert_ids[:, :, None] == expert_range).astype(jnp.float32)
    chosen = jnp.sum(pair_hot * logits[:, None, :], axis=2)
    first_share = jax.nn.sigmoid(chosen[:, 0] - chosen[:, 1])
    weight = jnp.stack([first_share, 1.0 - first_share], axis=1) * keep_mask.astype(jnp.float32)
    weight_ext = jnp.concatenate([weight.reshape(assign), jnp.zeros((1,), jnp.float32)])
    slot_weight = weight_ext[slot_src]
    lower_ext = jnp.concatenate([lower_out, jnp.zeros((1, features), jnp.bfloat16)], axis=0)
    send_rows = lower_ext[slot_tok].reshape(experts, capacity, features)
    cot_ext = jnp.concatenate([upper_cot, jnp.zeros((1, features), jnp.bfloat16)], axis=0)
    send_cot = (
        cot_ext[slot_tok].astype(jnp.float32) * (residual_scale * slot_weight)[:, None]
    ).astype(jnp.bfloat16)
    send_cot = send_cot.reshape(experts, capacity, features)
    gate_up, down = (
        lax.all_gather(gate_up_local, "dp", axis=0, tiled=True),
        lax.all_gather(down_local, "dp", axis=0, tiled=True),
    )
    arrived = lax.all_to_all(send_rows, "expert", split_axis=0, concat_axis=0, tiled=True)
    row_block = arrived.reshape(slots, features)
    projected = jnp.dot(row_block, gate_up, preferred_element_type=jnp.float32)
    gate_part = projected[:, :hidden_units]
    up_part = projected[:, hidden_units:]
    gate_sig = jax.nn.sigmoid(gate_part)
    activated = gate_part * gate_sig
    hidden = (activated * up_part).astype(jnp.bfloat16)
    outputs = lax.dot_general(
        hidden, down, contract_last, preferred_element_type=jnp.float32
    ).astype(jnp.bfloat16)
    outputs, saved = (outputs, (gate_part, up_part, gate_sig, activated, hidden))
    out_back = lax.all_to_all(
        outputs.reshape(experts, capacity, features),
        "expert",
        split_axis=0,
        concat_axis=0,
        tiled=True,
    )
    grads = lax.all_to_all(send_cot, "expert", split_axis=0, concat_axis=0, tiled=True).reshape(
        slots, features
    )
    gate_part, up_part, gate_sig, activated, hidden = saved
    down_part = lax.dot_general(grads, hidden, contract_first, preferred_element_type=jnp.float32)
    hidden_grad = jnp.dot(grads, down, preferred_element_type=jnp.float32)
    gate_grad = hidden_grad * up_part * (gate_sig * (1.0 + gate_part * (1.0 - gate_sig)))
    up_grad = hidden_grad * activated
    joined = jnp.concatenate([gate_grad, up_grad], axis=1).astype(jnp.bfloat16)
    gate_up_part = lax.dot_general(
        row_block, joined, contract_first, preferred_element_type=jnp.float32
    )
    rows_grad = lax.dot_general(
        joined, gate_up, contract_last, preferred_element_type=jnp.float32
    ).astype(jnp.bfloat16)
    rows_grad, gate_up_part, down_part = (rows_grad, gate_up_part, down_part)
    rows_back = lax.all_to_all(
        rows_grad.reshape(experts, capacity, features),
        "expert",
        split_axis=0,
        concat_axis=0,
        tiled=True,
    )
    out_assign = (
        out_back.reshape(slots, features)[slot_pos]
        .astype(jnp.float32)
        .reshape(tokens, top_count, features)
    )
    back_assign = (
        rows_back.reshape(slots, features)[slot_pos]
        .astype(jnp.float32)
        .reshape(tokens, top_count, features)
    )
    mixed = jnp.sum(weight[:, :, None] * out_assign, axis=1)
    upper_input = upper_out - residual_scale * mixed
    share_grad = (
        residual_scale
        * keep_mask.astype(jnp.float32)
        * jnp.sum(upper_cot.astype(jnp.float32)[:, None, :] * out_assign, axis=2)
    )
    diff_grad = (share_grad[:, 0] - share_grad[:, 1]) * first_share * (1.0 - first_share)
    logit_grad = diff_grad[:, None] * (pair_hot[:, 0] - pair_hot[:, 1])
    lower_grad = (
        lower_cot.astype(jnp.float32)
        + jnp.sum(back_assign, axis=1)
        + jnp.dot(logit_grad, router_weight.T, precision=highest)
    )
    router_term = jnp.dot(lower_out.astype(jnp.float32).T, logit_grad, precision=highest)
    router_grad = lax.psum(router_term, ("expert", "dp"))
    gate_up_sum, down_sum = (
        lax.psum_scatter(
            gate_up_part.astype(jnp.bfloat16), "dp", scatter_dimension=0, tiled=True
        ).astype(jnp.float32),
        lax.psum_scatter(
            down_part.astype(jnp.bfloat16), "dp", scatter_dimension=0, tiled=True
        ).astype(jnp.float32),
    )
    return (
        upper_input,
        lower_grad,
        gate_up_sum.astype(jnp.bfloat16)[None],
        down_sum.astype(jnp.bfloat16)[None],
        router_grad,
    )


def solution(mesh):
    placed = (
        P(("expert", "dp"), None),
        P(("expert", "dp"), None),
        P(("expert", "dp"), None),
        P(("expert", "dp"), None),
        P("expert", "dp", None),
        P("expert", "dp", None),
        P(),
        P(("expert", "dp"), None),
        P(("expert", "dp"), None),
    )
    return jax.shard_map(
        body,
        mesh=mesh,
        in_specs=placed,
        out_specs=(
            P(("expert", "dp"), None),
            P(("expert", "dp"), None),
            P("expert", "dp", None),
            P("expert", "dp", None),
            P(),
        ),
        check_vma=False,
    )
```

profile of v0, /device:TPU:2, one launch (start us, length us, event | category | flops | bytes accessed | tf_op | source)
XLA Modules:
  0.0 572.6 jit_solution(3335142089802895782)
XLA Ops:
  7.2 0.7 all-gather.5.cloned.1.call-update
  7.9 0.8 copy.62
  9.0 0.7 broadcast_multiply_fusion.1
  10.8 0.8 copy.60
  11.7 1.1 concatenate.16
  12.9 1.4 scatter_custom_fusion
  14.3 2.4 gather_fusion
  16.8 2.4 gather_fusion.1
  19.3 1.6 reshape.125
  20.8 11.7 %all-to-all-start = ((bf16[32,9,2048]{2,1,0:T(8,128)(2,1)}), bf16[32,9,2048]{2,1,0:T(8,128)(2,1)S(1)}, u32[]{:S(2)}, u32[]{:S(2)}) async-start(bf16[32,9,2048]{2,1,0:T(8,128)(2,1)} %reshape.125), calls=%async_computation | async-start | bytes 4194304 | tf_op jit(solution)/shard_map/all_to_all | solution.py:61
  32.7 0.7 all-gather.7.cloned.1.call-update
  33.4 3.0 gather_fusion.3
  36.4 3.4 reshape.134
  40.5 0.6 copy-done.9
  41.3 2.4 gather_fusion.4
  43.9 3.8 multiply_convert_fusion
  47.7 34.1 %all-to-all-done = bf16[32,9,2048]{2,1,0:T(8,128)(2,1)S(1)} async-done(((bf16[32,9,2048]{2,1,0:T(8,128)(2,1)}), bf16[32,9,2048]{2,1,0:T(8,128)(2,1)S(1)}, u32[]{:S(2)}, u32[]{:S(2)}) %all-to-all-start) | async-done | bytes 1179680 | tf_op jit(solution)/shard_map/all_to_all | solution.py:61
  81.8 6.9 %all-to-all-start.2 = ((bf16[32,9,2048]{2,1,0:T(8,128)(2,1)}), bf16[32,9,2048]{2,1,0:T(8,128)(2,1)}, u32[]{:S(2)}, u32[]{:S(2)}) async-start(bf16[32,9,2048]{2,1,0:T(8,128)(2,1)} %multiply_convert_fusion), calls=%async_computation.2 | async-start | bytes 4194304 | tf_op jit(solution)/shard_map/all_to_all | solution.py:80
  88.8 1.4 reshape.126
  90.2 47.2 %all-to-all-done.2 = bf16[32,9,2048]{2,1,0:T(8,128)(2,1)} async-done(((bf16[32,9,2048]{2,1,0:T(8,128)(2,1)}), bf16[32,9,2048]{2,1,0:T(8,128)(2,1)}, u32[]{:S(2)}, u32[]{:S(2)}) %all-to-all-start.2) | async-done | bytes 1179680 | tf_op jit(solution)/shard_map/all_to_all | solution.py:80
  137.4 1.8 reshape.130
  139.2 6.2 %fusion.2 = f32[288,1408]{1,0:T(8,128)} fusion(bf16[288,2048]{1,0:T(8,128)(2,1)S(1)} %copy-done.5, bf16[1,2048,1408]{2,1,0:T(8,128)(2,1)} %all-gather.5.cloned.1.call-done), kind=kOutput, calls=%fused_computation.10 | convolution fusion | flops 1660944384 | bytes 8568832 | tf_op jit(solution)/shard_map/dot_general | solution.py:63
  145.4 4.6 multiply_convert_fusion.2
  150.1 0.8 copy-done.16
  150.8 1.1 fusion.8
  151.9 1.6 reshape.127
  153.5 6.6 %all-to-all-start.1 = ((bf16[32,9,2048]{2,1,0:T(8,128)(2,1)}), bf16[32,9,2048]{2,1,0:T(8,128)(2,1)S(1)}, u32[]{:S(2)}, u32[]{:S(2)}) async-start(bf16[32,9,2048]{2,1,0:T(8,128)(2,1)} %reshape.127), calls=%async_computation.1 | async-start | bytes 4194304 | tf_op jit(solution)/shard_map/all_to_all | solution.py:73
  160.3 1.1 convert_element_type.82
  162.0 47.0 %all-to-all-done.1 = bf16[32,9,2048]{2,1,0:T(8,128)(2,1)S(1)} async-done(((bf16[32,9,2048]{2,1,0:T(8,128)(2,1)}), bf16[32,9,2048]{2,1,0:T(8,128)(2,1)S(1)}, u32[]{:S(2)}, u32[]{:S(2)}) %all-to-all-start.1) | async-done | bytes 1179680 | tf_op jit(solution)/shard_map/all_to_all | solution.py:73
  209.5 2.3 gather_fusion.2
  211.8 2.4 reshape.133
  214.3 6.2 %multiply_reduce_fusion = (f32[128,2]{1,0:T(8,128)S(1)}, f32[128,2048]{1,0:T(8,128)}) fusion(f32[128,2,2048]{2,1,0:T(2,128)S(1)} %reshape.133, f32[128,2048]{1,0:T(8,128)} %convert_element_type.82, f32[128,2]{1,0:T(8,128)S(1)} %copy-done.10), kind=kLoop, calls=%fused_computation.22 | loop fusion | flops 1834752 | bytes 4196352 | tf_op jit(solution)/shard_map/reduce_sum | solution.py:118
  220.6 1.0 convolution_bitcast_fusion
  221.7 4.6 convolution_convert_fusion.1
  226.4 1.2 copy-done.6
  227.8 5.5 convolution_convert_fusion
  233.3 4.7 fusion.11
  238.5 53.5 %all_to_all.20 = bf16[32,9,2048]{2,1,0:T(8,128)(2,1)} all-to-all(bf16[32,9,2048]{2,1,0:T(8,128)(2,1)S(1)} %reshape.131), channel_id=1, replica_groups=mesh['expert'=32,'dp'=8] {'expert'}, dimensions={0} | all-to-all | bytes 2359296 | tf_op jit(solution)/shard_map/all_to_all | solution.py:96
  292.0 1.8 reshape.132
  293.8 1.4 gather_fusion.5
  295.2 1.3 reshape.135
  296.6 2.8 reduce_sum.51
  299.4 3.2 convolution_add_fusion
  302.6 1.1 multiply_subtract_fusion
  303.7 175.5 %all-reduce.4.cloned.1.call-done = f32[2048,32]{0,1:T(8,128)} async-done(((f32[2048,32]{0,1:T(8,128)}), f32[2048,32]{0,1:T(8,128)}) %all-reduce.4.cloned.1.call-update) | async-done | bytes 262160 | tf_op jit(solution)/shard_map/psum | solution.py:128
  479.2 39.4 %reduce-scatter.5.cloned.1.call-done = bf16[256,704]{0,1:T(8,128)(2,1)} async-done(((bf16[2048,704]{0,1:T(8,128)(2,1)}), bf16[256,704]{0,1:T(8,128)(2,1)}) %reduce-scatter.5.cloned.1.call-update) | async-done | bytes 360464 | tf_op jit(solution)/shard_map/reduce_scatter | solution.py:133
  518.6 45.8 %reduce-scatter.3.cloned.1.call-done = bf16[256,1408]{1,0:T(8,128)(2,1)} async-done(((bf16[2048,1408]{1,0:T(8,128)(2,1)}), bf16[256,1408]{1,0:T(8,128)(2,1)}) %reduce-scatter.3.cloned.1.call-update) | async-done | bytes 720912 | tf_op jit(solution)/shard_map/reduce_scatter | solution.py:130
  564.4 1.7 copy.70
  (82 shorter events, 5.2 us)
Async XLA Ops:
  7.2 32.6 %copy-start = (f32[2048,32]{0,1:T(8,128)S(1)}, f32[2048,32]{0,1:T(8,128)}, u32[]{:S(2)}) copy-start(f32[2048,32]{0,1:T(8,128)} %param.15) | copy-start | bytes 786436
  7.2 132.0 %all-gather.5.cloned.1.call-start = ((), (), s32[]{:S(2)}) async-start(), calls=%async_computation.9 | async-start | bytes 6488064 | tf_op jit(solution)/shard_map/all_gather | solution.py:58
  20.8 12.5 %copy-start.4 = (bf16[128,2048]{1,0:T(8,128)(2,1)S(1)}, bf16[128,2048]{1,0:T(8,128)(2,1)}, u32[]{:S(2)}) copy-start(bf16[128,2048]{1,0:T(8,128)(2,1)} %param.11) | copy-start | bytes 1572868
  20.8 61.0 %all-to-all-start = ((bf16[32,9,2048]{2,1,0:T(8,128)(2,1)}), bf16[32,9,2048]{2,1,0:T(8,128)(2,1)S(1)}, u32[]{:S(2)}, u32[]{:S(2)}) async-start(bf16[32,9,2048]{2,1,0:T(8,128)(2,1)} %reshape.125), calls=%async_computation | async-start | bytes 4194304 | tf_op jit(solution)/shard_map/all_to_all | solution.py:61
  32.6 112.8 %all-gather.7.cloned.1.call-start = ((), (), s32[]{:S(2)}) async-start(), calls=%async_computation.10 | async-start | bytes 3244032 | tf_op jit(solution)/shard_map/all_gather | solution.py:59
  36.4 3.4 copy-start.1
  36.4 4.0 copy-start.13
  36.4 4.0 copy-start.14
  40.5 0.6 copy-start.9
  81.8 55.5 %all-to-all-start.2 = ((bf16[32,9,2048]{2,1,0:T(8,128)(2,1)}), bf16[32,9,2048]{2,1,0:T(8,128)(2,1)}, u32[]{:S(2)}, u32[]{:S(2)}) async-start(bf16[32,9,2048]{2,1,0:T(8,128)(2,1)} %multiply_convert_fusion), calls=%async_computation.2 | async-start | bytes 4194304 | tf_op jit(solution)/shard_map/all_to_all | solution.py:80
  90.2 49.0 %copy-start.5 = (bf16[288,2048]{1,0:T(8,128)(2,1)S(1)}, bf16[288,2048]{1,0:T(8,128)(2,1)}, u32[]{:S(2)}) copy-start(bf16[288,2048]{1,0:T(8,128)(2,1)} %reshape.126) | copy-start | bytes 3538948
  139.2 6.3 %copy-start.7 = (bf16[288,2048]{1,0:T(8,128)(2,1)}, bf16[288,2048]{1,0:T(8,128)(2,1)S(1)}, u32[]{:S(2)}) copy-start(bf16[288,2048]{1,0:T(8,128)(2,1)S(1)} %reshape.130) | copy-start | bytes 3538948
  145.4 5.4 copy-start.15
  150.0 0.8 copy-start.16
  153.5 55.5 %all-to-all-start.1 = ((bf16[32,9,2048]{2,1,0:T(8,128)(2,1)}), bf16[32,9,2048]{2,1,0:T(8,128)(2,1)S(1)}, u32[]{:S(2)}, u32[]{:S(2)}) async-start(bf16[32,9,2048]{2,1,0:T(8,128)(2,1)} %reshape.127), calls=%async_computation.1 | async-start | bytes 4194304 | tf_op jit(solution)/shard_map/all_to_all | solution.py:73
  160.1 319.1 %all-reduce.4.cloned.1.call-start = ((), (), s32[]{:S(2)}) async-start(), calls=%async_computation.8 | async-start | bytes 524288 | tf_op jit(solution)/shard_map/psum | solution.py:128
  211.8 2.4 copy-start.10
  214.3 6.3 %copy-start.2 = (bf16[128,2048]{1,0:T(8,128)(2,1)S(1)}, bf16[128,2048]{1,0:T(8,128)(2,1)}, u32[]{:S(2)}) copy-start(bf16[128,2048]{1,0:T(8,128)(2,1)} %param.10) | copy-start | bytes 1572868
  214.3 6.3 %copy-start.11 = (f32[128,2,32]{0,2,1:T(8,128)S(1)}, f32[128,2,32]{0,2,1:T(8,128)}, u32[]{:S(2)}) copy-start(f32[128,2,32]{0,2,1:T(8,128)} %fusion.17) | copy-start | bytes 98308
  214.3 7.4 %copy-start.17 = (bf16[288,704]{1,0:T(8,128)(2,1)S(1)}, bf16[288,704]{1,0:T(8,128)(2,1)}, u32[]{:S(2)}) copy-start(bf16[288,704]{1,0:T(8,128)(2,1)} %copy-done.16) | copy-start | bytes 1216516
  221.6 297.0 %reduce-scatter.5.cloned.1.call-start = ((), (), s32[]{:S(2)}) async-start(), calls=%async_computation.7 | async-start | bytes 3244032 | tf_op jit(solution)/shard_map/reduce_scatter | solution.py:133
  226.3 1.3 copy-start.6
  226.3 1.4 copy-start.18
  226.3 1.5 copy-start.19
  226.4 338.0 %reduce-scatter.3.cloned.1.call-start = ((), (), s32[]{:S(2)}) async-start(), calls=%async_computation.6 | async-start | bytes 6488064 | tf_op jit(solution)/shard_map/reduce_scatter | solution.py:130
  296.6 2.8 copy-start.12
  299.3 3.3 copy-start.3
  299.4 3.2 copy-start.8
Sparse Core Ops, SparseCore 0:
  9.8 44.2 all-gather.4
  56.0 33.1 all-gather.6
  221.8 257.3 all-reduce.3
  482.2 36.3 reduce-scatter.4
  521.6 42.7 reduce-scatter.2
where the time goes:
time: 573 us
  waiting for transfers between devices  390 us (68%)
  blocking collectives  53.5 us (9%)
  local copies, waits for them, and re-layouts  40.2 us (7%)
  matrix products  31.5 us (5%)
  starting transfers between devices  25.6 us (4%)
  other arithmetic  17.1 us (3%)
  between operations  14.2 us (2%)
    psum x1, waiting for transfers between devices, body(): router_grad = lax.psum(router_term, ('expert', 'dp'))  175 us
    all_to_all x1, blocking collectives, body(): lax.all_to_all(rows_grad.reshape(experts, capacity, features), 'expert',...  53.5 us
    all_to_all x1, waiting for transfers between devices, body(): lax.all_to_all(send_cot, 'expert', split_axis=0, concat_axis=0, tiled=True)  47.2 us
    all_to_all x1, waiting for transfers between devices, body(): lax.all_to_all(outputs.reshape(experts, capacity, features), 'expert', sp...  47 us
    reduce_scatter x1, waiting for transfers between devices, body(): lax.psum_scatter(gate_up_part.astype(jnp.bfloat16), 'dp', scatter_dimensi...  45.8 us
    reduce_scatter x1, waiting for transfers between devices, body(): lax.psum_scatter(down_part.astype(jnp.bfloat16), 'dp', scatter_dimension=...  39.4 us
    all_to_all x1, waiting for transfers between devices, body(): lax.all_to_all(send_rows, 'expert', split_axis=0, concat_axis=0, tiled=True)  34.1 us
    all_to_all x1, starting transfers between devices, body(): lax.all_to_all(send_rows, 'expert', split_axis=0, concat_axis=0, tiled=True)  11.7 us
  transfers between devices with their start and end apart: 8, of which 6 were waited for; matrix products, arithmetic and copies ran while one was open for 11% of the time, Pallas kernels for 0%

commit v1 on v0

v1 whole, which is shorter than its diff:
```python
import jax
import jax.numpy as jnp
from jax import lax
from jax.sharding import PartitionSpec as P

residual_scale = 128.0 ** (-0.5)
highest = lax.Precision.HIGHEST
contract_last = (((1,), (1,)), ((), ()))
contract_first = (((0,), (0,)), ((), ()))
f32, bf16 = jnp.float32, jnp.bfloat16
fold = 8


def exchange(array):
    return lax.all_to_all(array, "expert", split_axis=0, concat_axis=0, tiled=True)


def pack(rows, experts, extra=()):
    features = rows.shape[1]
    main = experts * fold
    parts = [rows[:main].reshape(experts, fold, features)]
    for start in range(main, rows.shape[0], experts):
        parts.append(rows[start : start + experts].reshape(experts, fold, features // fold))
    return jnp.concatenate([*parts, *extra], axis=2)


def unpack(block, features):
    experts, _, width = block.shape
    rows = [block[:, :, :features].reshape(experts * fold, features)]
    for start in range(features, width - features // fold + 1, features // fold):
        rows.append(block[:, :, start : start + features // fold].reshape(experts, features))
    return jnp.concatenate(rows, axis=0)


def body(
    upper_out,
    lower_out,
    upper_cot,
    lower_cot,
    gate_up_weight,
    down_weight,
    router_weight,
    expert_ids,
    keep_mask,
):
    tokens, features = lower_out.shape
    experts = router_weight.shape[1]
    hidden_units = down_weight.shape[2]
    main = experts * fold
    slots = main + experts
    gate_up = lax.all_gather(gate_up_weight[0], "dp", axis=0, tiled=True)
    down = lax.all_gather(down_weight[0], "dp", axis=0, tiled=True)

    expert_range = jnp.arange(experts, dtype=jnp.int32)
    hot = [(expert_ids[:, k, None] == expert_range).astype(f32) for k in range(2)]
    earlier = (
        jnp.arange(tokens, dtype=jnp.int32)[:, None] > jnp.arange(tokens, dtype=jnp.int32)
    ).astype(bf16)
    counts = jnp.dot(earlier, (hot[0] + hot[1]).astype(bf16), preferred_element_type=f32)
    place = []
    for k in range(2):
        rank = jnp.sum(hot[k] * counts, axis=1).astype(jnp.int32)
        slot = jnp.where(rank < fold, expert_ids[:, k] * fold + rank, main + expert_ids[:, k])
        place.append(slot[:, None] == jnp.arange(slots, dtype=jnp.int32))
    kept = keep_mask.astype(f32)
    used = jnp.where(place[0], kept[:, :1], 0.0) + jnp.where(place[1], kept[:, 1:], 0.0)
    used = used.astype(bf16)
    rows = lax.dot_general(used, lower_out, contract_first, preferred_element_type=f32)
    arrived = exchange(pack(rows.astype(bf16), experts))

    logits = jnp.dot(lower_out.astype(f32), router_weight, precision=highest)
    gap = jnp.sum((hot[0] - hot[1]) * logits, axis=1)
    share = jax.nn.sigmoid(gap)
    rest = 1.0 - share
    weights = (share * kept[:, 0], rest * kept[:, 1])
    mix = jnp.where(place[0], weights[0][:, None], 0.0) + jnp.where(
        place[1], weights[1][:, None], 0.0
    )
    slot_weight = jnp.sum(mix, axis=0)
    cot_rows = lax.dot_general(used, upper_cot, contract_first, preferred_element_type=f32)
    cot_rows = (cot_rows * (residual_scale * slot_weight)[:, None]).astype(bf16)
    partner = jnp.sum(
        jnp.where(place[0], expert_ids[:, 1:].astype(f32), 0.0)
        + jnp.where(place[1], expert_ids[:, :1].astype(f32), 0.0),
        axis=0,
    )
    other = jnp.sum(
        jnp.where(place[0], rest[:, None], 0.0) + jnp.where(place[1], share[:, None], 0.0), axis=0
    )
    other_high = lax.reduce_precision(other, 8, 7)
    facts = jnp.stack([partner, other_high, other - other_high], axis=1).astype(bf16)
    facts = jnp.concatenate(
        [
            facts[:main].reshape(experts, fold, 3),
            jnp.broadcast_to(facts[main:, None, :], (experts, fold, 3)),
        ],
        axis=2,
    )
    facts = jnp.pad(facts, ((0, 0), (0, 0), (0, 122)))
    cot_arrived = exchange(pack(cot_rows, experts, (facts,)))

    row_block = unpack(arrived, features)
    projected = jnp.dot(row_block, gate_up, preferred_element_type=f32)
    gate_part = projected[:, :hidden_units]
    up_part = projected[:, hidden_units:]
    gate_sig = jax.nn.sigmoid(gate_part)
    activated = gate_part * gate_sig
    hidden = (activated * up_part).astype(bf16)
    outputs = lax.dot_general(hidden, down, contract_last, preferred_element_type=f32).astype(bf16)

    grads = unpack(cot_arrived[:, :, : features + features // fold], features)
    facts = cot_arrived[:, :, features + features // fold :]
    facts = jnp.concatenate([facts[:, :, :3].reshape(main, 3), facts[:, 0, 3:6]], axis=0)
    facts = facts.astype(f32)
    inner = jnp.sum(grads.astype(f32) * outputs.astype(f32), axis=1)
    change = inner * (facts[:, 1] + facts[:, 2])
    own = lax.axis_index("expert")
    sign = (expert_range == own).astype(f32) - (
        facts[:, 0].astype(jnp.int32)[:, None] == expert_range
    ).astype(f32)
    logit_grad = change[:, None] * sign
    router_part = lax.dot_general(
        logit_grad, row_block.astype(f32), contract_first, precision=highest
    )
    out_back = exchange(
        pack(jnp.concatenate([outputs, router_part.astype(bf16)], axis=0), experts)
    )

    hidden_grad = jnp.dot(grads, down, preferred_element_type=f32)
    gate_grad = hidden_grad * up_part * (gate_sig * (1.0 + gate_part * (1.0 - gate_sig)))
    up_grad = hidden_grad * activated
    joined = jnp.concatenate([gate_grad, up_grad], axis=1).astype(bf16)
    down_part = lax.dot_general(grads, hidden, contract_first, preferred_element_type=f32)
    gate_up_part = lax.dot_general(row_block, joined, contract_first, preferred_element_type=f32)
    both = jnp.concatenate([gate_up_part.astype(bf16), down_part.astype(bf16)], axis=1)
    both = lax.psum_scatter(both, "dp", scatter_dimension=0, tiled=True)
    rows_grad = lax.dot_general(joined, gate_up, contract_last, preferred_element_type=f32)
    rows_grad = rows_grad + jnp.dot(logit_grad, router_weight.T, precision=highest)
    rows_back = exchange(pack(rows_grad.astype(bf16), experts))

    out_rows = unpack(out_back, features)
    router_row = jnp.sum(out_rows[slots:].astype(f32), axis=0)
    router_row = jnp.sum(lax.all_gather(router_row.reshape(fold, -1), "dp"), axis=0)
    router_all = exchange(jnp.broadcast_to(router_row, (experts, *router_row.shape)))
    router_grad = router_all.reshape(experts, features).T
    mixed = jnp.dot(mix, out_rows[:slots].astype(f32), precision=highest)
    upper_input = upper_out - residual_scale * mixed
    back = jnp.dot(
        (place[0] | place[1]).astype(bf16), unpack(rows_back, features), preferred_element_type=f32
    )
    lower_grad = lower_cot.astype(f32) + back
    return (
        upper_input,
        lower_grad,
        both[None, :, : 2 * hidden_units],
        both[None, :, 2 * hidden_units :],
        router_grad,
    )


def solution(mesh):
    blocks = P(("expert", "dp"), None)
    split = P("expert", "dp", None)
    return jax.shard_map(
        body,
        mesh=mesh,
        in_specs=(blocks, blocks, blocks, blocks, split, split, P(), blocks, blocks),
        out_specs=(blocks, blocks, split, split, P()),
        check_vma=False,
    )
```

time: 573 us -> 244 us (0.43)
  waiting for transfers between devices: 390 us -> 121 us
  blocking collectives: 53.5 us -> 13.3 us
  local copies, waits for them, and re-layouts: 40.2 us -> 10.9 us
  starting transfers between devices: 25.6 us -> 35.4 us
  other arithmetic: 17.1 us -> 10.7 us
    psum x1 -> x0, waiting for transfers between devices: 175 us -> none  [body(): router_grad = lax.psum(router_term, ('expert', 'dp'))]
    reduce_scatter x2 -> x1, waiting for transfers between devices: 85.2 us -> 0.01 us  [body(): both = lax.psum_scatter(both, 'dp', scatter_dimension=0, tiled=True)]
    all_to_all x1 -> x0, blocking collectives: 53.5 us -> none  [body(): lax.all_to_all(rows_grad.reshape(experts, capacity, features), 'expert',...]
    gather x6 -> x0, local copies, waits for them, and re-layouts: 14 us -> none  [the longest x1 2.96 us: body(): cot_ext[slot_tok].astype(jnp.float32)]
    all_gather x0 -> x1, blocking collectives: none -> 13.3 us  [body(): lax.all_gather(router_row.reshape(fold, -1), 'dp')]
    all_to_all x3 -> x5, starting transfers between devices: 25.2 us -> 35.1 us  [exchange(): lax.all_to_all(array, 'expert', split_axis=0, concat_axis=0, tiled=True)]
    all_to_all x3 -> x5, waiting for transfers between devices: 128 us -> 119 us  [exchange(): lax.all_to_all(array, 'expert', split_axis=0, concat_axis=0, tiled=True)]
    concatenate x2 -> x6, other arithmetic: 0.02 us -> 8.8 us  [the longest x4 4.61 us: pack(): return jnp.concatenate([*parts, *extra], axis=2)]
  transfers between devices with their start and end apart: 8 -> 8, of which waited for: 6 -> 5; matrix products, arithmetic and copies ran while one was open for 11% -> 16% of each run, Pallas kernels for 0% -> 0%
where the time goes in v1:
time: 244 us; the launch traced here: 241 us
  waiting for transfers between devices  121 us (50%)
  matrix products  36.3 us (15%)
  starting transfers between devices  35.4 us (15%)
  between operations  14.3 us (6%)
  blocking collectives  13.3 us (5%)
  local copies, waits for them, and re-layouts  10.9 us (4%)
  other arithmetic  10.7 us (4%)
    all_to_all x5, waiting for transfers between devices, exchange(): lax.all_to_all(array, 'expert', split_axis=0, concat_axis=0, tiled=True)  119 us
    all_to_all x5, starting transfers between devices, exchange(): lax.all_to_all(array, 'expert', split_axis=0, concat_axis=0, tiled=True)  35.1 us
    all_gather x1, blocking collectives, body(): lax.all_gather(router_row.reshape(fold, -1), 'dp')  13.3 us
    dot_general x1, matrix products, body(): projected = jnp.dot(row_block, gate_up, preferred_element_type=f32)  5.79 us
  transfers between devices with their start and end apart: 8, of which 5 were waited for; matrix products, arithmetic and copies ran while one was open for 16% of the time, Pallas kernels for 0%

profile of v1, /device:TPU:2, one launch (start us, length us, event | category | flops | bytes accessed | tf_op | source)
XLA Modules:
  0.0 241.4 jit_solution(13970101376191744542)
XLA Ops:
  7.2 0.7 all-gather.6.cloned.1.call-update
  7.9 0.7 convert_element_type.121
  8.6 0.8 slice_bitcast_fusion.14
  9.4 0.2 select_reduce_fusion.1
  9.5 1.6 fusion.22
  11.1 0.8 convert_bitcast_fusion.1
  11.9 0.5 convolution_convert_fusion.2
  12.5 1.1 pad_maximum_fusion.2
  13.6 11.6 %all-to-all-start = ((bf16[32,8,2304]{2,1,0:T(8,128)(2,1)}), bf16[32,8,2304]{2,1,0:T(8,128)(2,1)S(1)}, u32[]{:S(2)}, u32[]{:S(2)}) async-start(bf16[32,8,2304]{2,1,0:T(8,128)(2,1)} %pad_maximum_fusion.2), calls=%async_computation | async-start | bytes 2359296 | tf_op jit(solution)/shard_map/all_to_all | solution.py:15
  25.3 0.7 all-gather.8.cloned.1.call-update
  26.0 0.3 fusion.25
  26.6 0.2 copy.38
  26.7 0.5 fusion.8
  27.3 1.1 fusion.15
  28.5 27.7 %all-to-all-done = bf16[32,8,2304]{2,1,0:T(8,128)(2,1)S(1)} async-done(((bf16[32,8,2304]{2,1,0:T(8,128)(2,1)}), bf16[32,8,2304]{2,1,0:T(8,128)(2,1)S(1)}, u32[]{:S(2)}, u32[]{:S(2)}) %all-to-all-start) | async-done | bytes 1179680 | tf_op jit(solution)/shard_map/all_to_all | solution.py:15
  56.1 5.6 %all-to-all-start.1 = ((bf16[32,8,2432]{2,1,0:T(8,128)(2,1)}), bf16[32,8,2432]{2,1,0:T(8,128)(2,1)S(1)}, u32[]{:S(2)}, u32[]{:S(2)}) async-start(bf16[32,8,2432]{2,1,0:T(8,128)(2,1)} %fusion.15), calls=%async_computation.1 | async-start | bytes 2490368 | tf_op jit(solution)/shard_map/all_to_all | solution.py:15
  61.7 0.2 reduce-scatter.2.cloned.1.call-start
  62.0 1.1 slice_bitcast_fusion.6
  63.1 29.3 %all-to-all-done.1 = bf16[32,8,2432]{2,1,0:T(8,128)(2,1)S(1)} async-done(((bf16[32,8,2432]{2,1,0:T(8,128)(2,1)}), bf16[32,8,2432]{2,1,0:T(8,128)(2,1)S(1)}, u32[]{:S(2)}, u32[]{:S(2)}) %all-to-all-start.1) | async-done | bytes 1245216 | tf_op jit(solution)/shard_map/all_to_all | solution.py:15
  92.4 1.1 slice_bitcast_fusion.3
  93.5 5.8 %fusion.2 = f32[288,1408]{1,0:T(8,128)} fusion(bf16[1,2048,1408]{2,1,0:T(8,128)(2,1)} %all-gather.6.cloned.1.call-done, bf16[32,2048]{1,0:T(8,128)(2,1)S(1)} %bitcast.127, bf16[256,2048]{1,0:T(8,128)(2,1)S(1)} %copy-done.2), kind=kOutput, calls=%fused_computation.4 | convolution fusion | flops 1663303680 | bytes 8568832 | tf_op jit(solution)/shard_map/dot_general | solution.py:103
  99.3 4.0 %multiply_convert_fusion.1 = (bf16[288,704]{1,0:T(8,128)(2,1)S(1)}, bf16[288,704]{1,0:T(8,128)(2,1)S(1)}, bf16[288,704]{1,0:T(8,128)(2,1)S(1)}) fusion(f32[288,1408]{1,0:T(8,128)} %fusion.2, bf16[1,2048,704]{1,2,0:T(8,128)(2,1)} %all-gather.8.cloned.1.call-done, bf16[32,2048]{1,0:T(8,128)(2,1)S(1)} %bitcast.130, bf16[256,2048]{1,0:T(8,128)(2,1)} %slice_bitcast_fusion.3), kind=kOutput, calls=%fused_computation.47 | convolution fusion | flops 835872768 | bytes 6901760 | tf_op jit(solution)/shard_map/dot_general | solution.py:129
  103.3 1.7 convolution_convert_fusion.1
  105.1 4.2 %convolution_convert_fusion = bf16[2048,1408]{0,1:T(8,128)(2,1)S(1)} fusion(bf16[288,704]{1,0:T(8,128)(2,1)S(1)} %get-tuple-element.33, bf16[288,704]{1,0:T(8,128)(2,1)S(1)} %get-tuple-element.32, bf16[32,2048]{1,0:T(8,128)(2,1)S(1)} %bitcast.128, bf16[256,2048]{1,0:T(8,128)(2,1)S(1)} %copy-done.2), kind=kOutput, calls=%fused_computation.1 | convolution fusion | flops 1667809280 | bytes 7757824 | tf_op jit(solution)/shard_map/dot_general | solution.py:134
  109.3 4.2 %pad_maximum_fusion = bf16[2048,2112]{0,1:T(8,128)(2,1)} fusion(bf16[2048,704]{0,1:T(8,128)(2,1)S(1)} %convolution_convert_fusion.1, bf16[2048,1408]{0,1:T(8,128)(2,1)S(1)} %convolution_convert_fusion), kind=kLoop, calls=%fused_computation | loop fusion | flops 17301504 | bytes 17301504 | tf_op jit(solution)/shard_map/concatenate | solution.py:135
  113.8 0.9 copy-done.4
  114.7 3.2 %multiply_reduce_fusion = (f32[288]{0:T(512)S(1)}, bf16[288,2048]{1,0:T(8,128)(2,1)S(1)}) fusion(bf16[32,2048]{1,0:T(8,128)(2,1)S(1)} %bitcast.132, bf16[256,2048]{1,0:T(8,128)(2,1)S(1)} %copy-done.4, bf16[288,704]{1,0:T(8,128)(2,1)} %copy-done.10, bf16[1,2048,704]{1,2,0:T(8,128)(2,1)} %all-gather.8.cloned.1.call-done), kind=kOutput, calls=%fused_computation.22 | convolution fusion | flops 835190528 | bytes 5649536 | tf_op jit(solution)/shard_map/dot_general | solution.py:109
  118.0 4.7 %fusion = f32[288,2048]{1,0:T(8,128)S(1)} fusion(bf16[1,2048,1408]{2,1,0:T(8,128)(2,1)} %all-gather.6.cloned.1.call-done, bf16[288,704]{1,0:T(8,128)(2,1)S(1)} %copy-done.9, bf16[288,704]{1,0:T(8,128)(2,1)S(1)} %copy-done.7), kind=kOutput, calls=%fused_computation.2 | convolution fusion | flops 1662566400 | bytes 8937472 | tf_op jit(solution)/shard_map/dot_general | solution.py:137
  122.7 2.2 fusion.12
  125.0 1.1 pad_maximum_fusion.5
  126.1 6.0 %all-to-all-start.3 = ((bf16[32,8,2304]{2,1,0:T(8,128)(2,1)}), bf16[32,8,2304]{2,1,0:T(8,128)(2,1)S(1)}, u32[]{:S(2)}, u32[]{:S(2)}) async-start(bf16[32,8,2304]{2,1,0:T(8,128)(2,1)} %pad_maximum_fusion.5), calls=%async_computation.3 | async-start | bytes 2359296 | tf_op jit(solution)/shard_map/all_to_all | solution.py:15
  132.1 2.2 convolution_convert_fusion.3
  134.5 1.2 pad_maximum_fusion.1
  135.7 25.2 %all-to-all-done.3 = bf16[32,8,2304]{2,1,0:T(8,128)(2,1)S(1)} async-done(((bf16[32,8,2304]{2,1,0:T(8,128)(2,1)}), bf16[32,8,2304]{2,1,0:T(8,128)(2,1)S(1)}, u32[]{:S(2)}, u32[]{:S(2)}) %all-to-all-start.3) | async-done | bytes 1179680 | tf_op jit(solution)/shard_map/all_to_all | solution.py:15
  160.9 6.0 %all-to-all-start.2 = ((bf16[32,8,2560]{2,1,0:T(8,128)(2,1)}), bf16[32,8,2560]{2,1,0:T(8,128)(2,1)S(1)}, u32[]{:S(2)}, u32[]{:S(2)}) async-start(bf16[32,8,2560]{2,1,0:T(8,128)(2,1)} %pad_maximum_fusion.1), calls=%async_computation.2 | async-start | bytes 2621440 | tf_op jit(solution)/shard_map/all_to_all | solution.py:15
  167.0 0.1 slice_bitcast_fusion
  167.1 2.5 %convolution_add_fusion.1 = f32[128,2048]{1,0:T(8,128)} fusion(bf16[32,2048]{1,0:T(8,128)(2,1)S(1)} %bitcast.134, bf16[256,2048]{1,0:T(8,128)(2,1)S(1)} %slice_bitcast_fusion, bf16[128,2048]{1,0:T(8,128)(2,1)} %param.12, s32[128]{0:T(128)S(1)} %get-tuple-element.42, s32[128]{0:T(128)S(1)} %get-tuple-element.41), kind=kOutput, calls=%fused_computation.19 | convolution fusion | flops 153989120 | bytes 2753536 | tf_op jit(solution)/shard_map/dot_general | solution.py:148
  169.6 28.7 %all-to-all-done.2 = bf16[32,8,2560]{2,1,0:T(8,128)(2,1)S(1)} async-done(((bf16[32,8,2560]{2,1,0:T(8,128)(2,1)}), bf16[32,8,2560]{2,1,0:T(8,128)(2,1)S(1)}, u32[]{:S(2)}, u32[]{:S(2)}) %all-to-all-start.2) | async-done | bytes 1310752 | tf_op jit(solution)/shard_map/all_to_all | solution.py:15
  198.4 13.3 %all-gather.2 = f32[64,256]{1,0:T(8,128)S(1)} all-gather(f32[8,256]{1,0:T(8,128)S(1)} %convert_reduce_fusion), channel_id=4, replica_groups=mesh['expert'=32,'dp'=8] {'dp'}, dimensions={0}, use_global_device_ids=true | all-gather | bytes 73728 | tf_op jit(solution)/shard_map/all_gather | solution.py:143
  211.6 0.7 broadcast_in_dim.116
  212.4 6.0 %all-to-all-start.4 = ((f32[32,8,256]{2,1,0:T(8,128)}), f32[32,8,256]{2,1,0:T(8,128)S(1)}, u32[]{:S(2)}, u32[]{:S(2)}) async-start(f32[32,8,256]{2,1,0:T(8,128)} %broadcast_in_dim.116), calls=%async_computation.5 | async-start | bytes 524288 | tf_op jit(solution)/shard_map/all_to_all | solution.py:15
  218.4 0.1 slice_bitcast_fusion.2
  218.5 3.2 %fusion.14 = f32[128,2048]{1,0:T(8,128)} fusion(f32[128,2048]{1,0:T(8,128)} %param.9, bf16[32,2048]{1,0:T(8,128)(2,1)S(1)} %bitcast.113, bf16[256,2048]{1,0:T(8,128)(2,1)S(1)} %slice_bitcast_fusion.2, f32[128]{0:T(128)S(1)} %get-tuple-element.38, s32[128]{0:T(128)S(1)} %get-tuple-element.42, f32[128]{0:T(128)S(1)} %get-tuple-element.37, ...), kind=kOutput, calls=%fused_computation.21 | convolution fusion | flops 909037568 | bytes 3278848 | tf_op jit(solution)/shard_map/dot_general | solution.py:146
  221.8 8.3 %all-to-all-done.4 = f32[32,8,256]{2,1,0:T(8,128)S(1)} async-done(((f32[32,8,256]{2,1,0:T(8,128)}), f32[32,8,256]{2,1,0:T(8,128)S(1)}, u32[]{:S(2)}, u32[]{:S(2)}) %all-to-all-start.4) | async-done | bytes 262176 | tf_op jit(solution)/shard_map/all_to_all | solution.py:15
  230.1 0.8 copy.48
  230.9 1.2 slice_bitcast_fusion.8
  232.0 1.1 copy.36
  233.1 1.7 slice_bitcast_fusion.9
  (69 shorter events, 1.4 us)
Async XLA Ops:
  7.2 2.4 copy-start
  7.2 86.3 %all-gather.6.cloned.1.call-start = ((), (), s32[]{:S(2)}) async-start(), calls=%async_computation.7 | async-start | bytes 6488064 | tf_op jit(solution)/shard_map/all_gather | solution.py:51
  12.5 14.2 %copy-start.5 = (bf16[128,2048]{1,0:T(8,128)(2,1)S(1)}, bf16[128,2048]{1,0:T(8,128)(2,1)}, u32[]{:S(2)}) copy-start(bf16[128,2048]{1,0:T(8,128)(2,1)} %param.11) | copy-start | bytes 1572868
  13.6 42.5 %all-to-all-start = ((bf16[32,8,2304]{2,1,0:T(8,128)(2,1)}), bf16[32,8,2304]{2,1,0:T(8,128)(2,1)S(1)}, u32[]{:S(2)}, u32[]{:S(2)}) async-start(bf16[32,8,2304]{2,1,0:T(8,128)(2,1)} %pad_maximum_fusion.2), calls=%async_computation | async-start | bytes 2359296 | tf_op jit(solution)/shard_map/all_to_all | solution.py:15
  25.3 74.0 %all-gather.8.cloned.1.call-start = ((), (), s32[]{:S(2)}) async-start(), calls=%async_computation.8 | async-start | bytes 3244032 | tf_op jit(solution)/shard_map/all_gather | solution.py:52
  56.1 36.2 %all-to-all-start.1 = ((bf16[32,8,2432]{2,1,0:T(8,128)(2,1)}), bf16[32,8,2432]{2,1,0:T(8,128)(2,1)S(1)}, u32[]{:S(2)}, u32[]{:S(2)}) async-start(bf16[32,8,2432]{2,1,0:T(8,128)(2,1)} %fusion.15), calls=%async_computation.1 | async-start | bytes 2490368 | tf_op jit(solution)/shard_map/all_to_all | solution.py:15
  61.7 169.1 %reduce-scatter.2.cloned.1.call-start = ((), (), s32[]{:S(2)}) async-start(), calls=%async_computation.6 | async-start | bytes 9732096 | tf_op jit(solution)/shard_map/reduce_scatter | solution.py:136
  63.1 30.4 %copy-start.2 = (bf16[256,2048]{1,0:T(8,128)(2,1)S(1)}, bf16[256,2048]{1,0:T(8,128)(2,1)}, u32[]{:S(2)}) copy-start(bf16[256,2048]{1,0:T(8,128)(2,1)} %slice_bitcast_fusion.6) | copy-start | bytes 3145732
  99.3 4.0 %copy-start.3 = (bf16[256,2048]{1,0:T(8,128)(2,1)S(1)}, bf16[256,2048]{1,0:T(8,128)(2,1)}, u32[]{:S(2)}) copy-start(bf16[256,2048]{1,0:T(8,128)(2,1)} %slice_bitcast_fusion.3) | copy-start | bytes 3145732
  103.3 1.8 copy-start.10
  103.3 1.8 copy-start.6
  103.3 1.8 copy-start.8
  113.5 1.2 copy-start.4
  114.7 3.3 %copy-start.7 = (bf16[288,704]{1,0:T(8,128)(2,1)S(1)}, bf16[288,704]{1,0:T(8,128)(2,1)}, u32[]{:S(2)}) copy-start(bf16[288,704]{1,0:T(8,128)(2,1)} %copy-done.6) | copy-start | bytes 1216516
  114.7 3.3 %copy-start.9 = (bf16[288,704]{1,0:T(8,128)(2,1)S(1)}, bf16[288,704]{1,0:T(8,128)(2,1)}, u32[]{:S(2)}) copy-start(bf16[288,704]{1,0:T(8,128)(2,1)} %copy-done.8) | copy-start | bytes 1216516
  118.0 4.7 %copy-start.1 = (f32[2048,32]{0,1:T(8,128)S(1)}, f32[2048,32]{0,1:T(8,128)}, u32[]{:S(2)}) copy-start(f32[2048,32]{0,1:T(8,128)} %param.15) | copy-start | bytes 786436
  126.1 34.8 %all-to-all-start.3 = ((bf16[32,8,2304]{2,1,0:T(8,128)(2,1)}), bf16[32,8,2304]{2,1,0:T(8,128)(2,1)S(1)}, u32[]{:S(2)}, u32[]{:S(2)}) async-start(bf16[32,8,2304]{2,1,0:T(8,128)(2,1)} %pad_maximum_fusion.5), calls=%async_computation.3 | async-start | bytes 2359296 | tf_op jit(solution)/shard_map/all_to_all | solution.py:15
  160.9 37.4 %all-to-all-start.2 = ((bf16[32,8,2560]{2,1,0:T(8,128)(2,1)}), bf16[32,8,2560]{2,1,0:T(8,128)(2,1)S(1)}, u32[]{:S(2)}, u32[]{:S(2)}) async-start(bf16[32,8,2560]{2,1,0:T(8,128)(2,1)} %pad_maximum_fusion.1), calls=%async_computation.2 | async-start | bytes 2621440 | tf_op jit(solution)/shard_map/all_to_all | solution.py:15
  212.4 17.7 %all-to-all-start.4 = ((f32[32,8,256]{2,1,0:T(8,128)}), f32[32,8,256]{2,1,0:T(8,128)S(1)}, u32[]{:S(2)}, u32[]{:S(2)}) async-start(f32[32,8,256]{2,1,0:T(8,128)} %broadcast_in_dim.116), calls=%async_computation.5 | async-start | bytes 524288 | tf_op jit(solution)/shard_map/all_to_all | solution.py:15
Sparse Core Ops, SparseCore 0:
  9.8 44.2 all-gather.5
  55.9 33.1 all-gather.7
  113.6 53.5 reduce-scatter.1

commit v2 on v1

v2 whole, which is shorter than its diff:
```python
import jax
import jax.numpy as jnp
from jax import lax
from jax.experimental import pallas as pl
from jax.experimental.pallas import tpu as pltpu
from jax.sharding import PartitionSpec as P

residual_scale = 128.0 ** (-0.5)
highest = lax.Precision.HIGHEST
contract_last = (((1,), (1,)), ((), ()))
contract_first = (((0,), (0,)), ((), ()))
f32, bf16, i32 = jnp.float32, jnp.bfloat16, jnp.int32
fold = 8
facts_width = 128


def dot(left, right, dims=(((1,), (0,)), ((), ()))):
    return lax.dot_general(left, right, dims, preferred_element_type=f32)


def call(kernel, shapes, cost, aliases=None, **specs):
    return pl.pallas_call(
        kernel,
        out_shape=shapes,
        input_output_aliases=aliases or {},
        cost_estimate=pl.CostEstimate(flops=cost, bytes_accessed=0, transcendentals=0),
        compiler_params=pltpu.CompilerParams(vmem_limit_bytes=48 * 2**20),
        **specs,
    )


def places(ids, experts):
    tokens = ids.shape[1]
    rows = lax.broadcasted_iota(i32, (experts, tokens), 0)
    hot = [(rows == ids[k : k + 1, :]).astype(f32) for k in range(2)]
    earlier = lax.broadcasted_iota(i32, (tokens, tokens), 0) < lax.broadcasted_iota(
        i32, (tokens, tokens), 1
    )
    counts = dot((hot[0] + hot[1]).astype(bf16), earlier.astype(f32).astype(bf16))
    slots = []
    for k in range(2):
        rank = jnp.sum(hot[k] * counts, axis=0, keepdims=True).astype(i32)
        slots.append(
            jnp.where(rank < fold, ids[k : k + 1, :] * fold + rank, -1 - ids[k : k + 1, :])
        )
    return hot, slots


def spread(slots, values, experts):
    tokens = slots[0].shape[1]
    rows = lax.broadcasted_iota(i32, (experts * fold, tokens), 0)
    ninth = -1 - rows // fold
    zero = jnp.zeros((), f32)
    main = sum(jnp.where(rows == slots[k], values[k], zero) for k in range(2))
    extra = sum(jnp.where(ninth == slots[k], values[k], zero) for k in range(2))
    return main, extra


def gather_rows(main, extra, table, scale_main, scale_extra, out):
    count, features = main.shape[0], table.shape[1]
    part = features // fold
    own = lax.broadcasted_iota(i32, extra.shape, 0) % fold
    main = main.astype(bf16)
    total = jnp.zeros((count, part), f32)
    for c in range(fold):
        piece = table[:, c * part : (c + 1) * part]
        rows = dot(main, piece)
        if scale_main is not None:
            rows = rows * scale_main
        out[:, c * part : (c + 1) * part] = rows.astype(bf16)
        total += dot(jnp.where(own == c, extra, 0.0).astype(bf16), piece)
    if scale_extra is not None:
        total = total * scale_extra
    out[:, features : features + part] = total.astype(bf16)


def send_rows_kernel(experts, ids, keep, table, out):
    _, slots = places(ids[...], experts)
    kept = keep[...].astype(f32)
    main, extra = spread(slots, (kept[:1], kept[1:]), experts)
    gather_rows(main, extra, table, None, None, out)


def send_cot_kernel(experts, ids, keep, lower, cot, router, out, mix, used):
    ids_now = ids[...]
    features = lower.shape[1]
    part = features // fold
    hot, slots = places(ids_now, experts)
    kept = keep[...].astype(f32)
    logits = lax.dot_general(
        router[...],
        lower[...].astype(f32),
        contract_last,
        precision=highest,
        preferred_element_type=f32,
    )
    gap = jnp.sum((hot[0] - hot[1]) * logits, axis=0, keepdims=True)
    share = jax.nn.sigmoid(gap)
    rest = 1.0 - share
    used_main, used_extra = spread(slots, (kept[:1], kept[1:]), experts)
    mix_main, mix_extra = spread(slots, (share * kept[:1], rest * kept[1:]), experts)
    weight_main = jnp.sum(mix_main, axis=1, keepdims=True) * residual_scale
    weight_extra = jnp.sum(mix_extra, axis=1, keepdims=True) * residual_scale
    gather_rows(used_main, used_extra, cot, weight_main, weight_extra, out)
    partner = spread(slots, (ids_now[1:].astype(f32), ids_now[:1].astype(f32)), experts)
    other = spread(slots, (rest, share), experts)
    lane = lax.broadcasted_iota(i32, (experts * fold, facts_width), 1)
    facts = jnp.zeros((experts * fold, facts_width), f32)
    for k in range(2):
        number = jnp.sum(partner[k], axis=1, keepdims=True)
        factor = jnp.sum(other[k], axis=1, keepdims=True)
        high = factor.astype(bf16).astype(f32)
        for place, value in enumerate((number, high, factor - high)):
            facts = jnp.where(lane == 3 * k + place, value, facts)
    out[:, features + part :] = facts.astype(bf16)
    width = experts * fold
    for k, value in enumerate((mix_main, mix_extra)):
        value = value.T
        high = value.astype(bf16)
        mix[:, 2 * k * width : (2 * k + 1) * width] = high
        mix[:, (2 * k + 1) * width : (2 * k + 2) * width] = (value - high.astype(f32)).astype(bf16)
    for k, value in enumerate((used_main, used_extra)):
        used[:, k * width : (k + 1) * width] = value.T.astype(bf16)


def signs(facts, change, own, column, experts):
    count = change.shape[0]
    col = lax.broadcasted_iota(i32, (count, experts * fold), 1) // fold
    partner = facts[:, column : column + 1].astype(i32)
    return jnp.where(col == own, change, 0.0) - jnp.where(col == partner, change, 0.0)


def router_kernel(experts, own, cot, rows, sent, out, grad):
    count = cot.shape[0]
    features = (rows.shape[1] * fold) // (fold + 1)
    part = features // fold
    total = jnp.zeros((count, 128), f32)
    for start in range(0, features, 128):
        total += cot[:, start : start + 128].astype(f32) * sent[:, start : start + 128].astype(f32)
    extra = jnp.zeros((count, 128), f32)
    for start in range(features, features + part, 128):
        extra += cot[:, start : start + 128].astype(f32) * sent[:, start : start + 128].astype(f32)
    extra = extra.reshape(experts, fold, 128)
    extra = jnp.broadcast_to(jnp.sum(extra, axis=1, keepdims=True), extra.shape)
    facts = cot[:, features + part :].astype(f32)
    changes = []
    for k, value in enumerate((total, extra.reshape(count, 128))):
        inner = jnp.sum(value, axis=1, keepdims=True)
        change = inner * (facts[:, 3 * k + 1 : 3 * k + 2] + facts[:, 3 * k + 2 : 3 * k + 3])
        changes.append(signs(facts, change, own[0], 3 * k, experts))
    row = lax.broadcasted_iota(i32, (count, count), 0) % fold
    lane = lax.broadcasted_iota(i32, (count, count), 1) % fold
    result = jnp.zeros((count, part), f32)
    for c in range(fold):
        left = jnp.where(lane == c, changes[0], 0.0).astype(bf16)
        result += dot(left, rows[:, c * part : (c + 1) * part], contract_first)
        left = jnp.where((lane == c) & (row == c), changes[1], 0.0).astype(bf16)
        result += dot(left, rows[:, features : features + part], contract_first)
    out[...] = result.astype(bf16)
    pick = lax.broadcasted_iota(i32, (count, 128), 0) == fold * lax.broadcasted_iota(
        i32, (count, 128), 1
    )
    pick = pick.astype(f32).astype(bf16)
    for k in range(2):
        high = changes[k].astype(bf16)
        low = (changes[k] - high.astype(f32)).astype(bf16)
        grad[k] = dot(high, pick) + dot(low, pick)


def upper_kernel(upper, back, mix, out):
    features = upper.shape[1]
    part = features // fold
    width = mix.shape[1] // 4
    lane = lax.broadcasted_iota(i32, (mix.shape[0], width), 1) % fold
    main_high, main_low = mix[:, :width], mix[:, width : 2 * width]
    extra_high = mix[:, 2 * width : 3 * width].astype(f32)
    extra_low = mix[:, 3 * width :].astype(f32)
    folded = back[:, features : features + part]
    for c in range(fold):
        piece = back[:, c * part : (c + 1) * part]
        mixed = dot(main_high, piece) + dot(main_low, piece)
        mixed += dot(jnp.where(lane == c, extra_high, 0.0).astype(bf16), folded)
        mixed += dot(jnp.where(lane == c, extra_low, 0.0).astype(bf16), folded)
        out[:, c * part : (c + 1) * part] = (
            upper[:, c * part : (c + 1) * part] - residual_scale * mixed
        )


def lower_kernel(lower_cot, back, used, out):
    features = lower_cot.shape[1]
    part = features // fold
    width = used.shape[1] // 2
    lane = lax.broadcasted_iota(i32, (used.shape[0], width), 1) % fold
    main, extra = used[:, :width], used[:, width:].astype(f32)
    folded = back[:, features : features + part]
    for c in range(fold):
        rows = dot(main, back[:, c * part : (c + 1) * part])
        rows += dot(jnp.where(lane == c, extra, 0.0).astype(bf16), folded)
        out[:, c * part : (c + 1) * part] = (
            lower_cot[:, c * part : (c + 1) * part].astype(f32) + rows
        )


def hidden_kernel(experts, cot, projected, down, joined, rows):
    features = down.shape[1]
    part = features // fold
    main = experts * fold
    units = down.shape[0]
    order = lax.broadcasted_iota(i32, (main, main), 1)
    place = lax.broadcasted_iota(i32, (main, main), 0)
    order = order == (place % experts) * fold + place // experts
    extra = dot(order.astype(f32).astype(bf16), cot[:, features : features + part]).astype(bf16)
    rows[:main, :] = cot[:, :features]
    for c in range(fold):
        rows[main:, c * part : (c + 1) * part] = extra[c * experts : (c + 1) * experts]
    back = dot(rows[...], down[...], contract_last)
    gate, up = projected[:, :units], projected[:, units:]
    gate_sig = jax.nn.sigmoid(gate)
    activated = gate * gate_sig
    joined[:, :units] = (back * up * (gate_sig * (1.0 + gate * (1.0 - gate_sig)))).astype(bf16)
    joined[:, units:] = (back * activated).astype(bf16)


def outputs_kernel(experts, hidden, down, out, total):
    step = pl.program_id(0)
    main = experts * fold

    @pl.when(step == 0)
    def _():
        total[...] = jnp.zeros_like(total)

    @pl.when(step < fold)
    def _():
        result = dot(hidden[...], down[...])
        out[...] = result[:main].astype(bf16)
        total[...] += unfolded(result[main:].astype(bf16), step, experts)

    @pl.when(step == fold)
    def _():
        out[...] = total[...].astype(bf16)

    @pl.when(step > fold)
    def _():
        out[...] = jnp.zeros_like(out)


def unfolded(extra, step, experts):
    row = lax.broadcasted_iota(i32, (experts * fold, experts), 0)
    lane = lax.broadcasted_iota(i32, (experts * fold, experts), 1)
    return dot((row == lane * fold + step).astype(f32).astype(bf16), extra)


def rows_kernel(experts, joined, gate_up, grad, router, out, total):
    step = pl.program_id(0)
    main = experts * fold

    @pl.when(step == 0)
    def _():
        total[...] = jnp.zeros_like(total)

    @pl.when(step < fold)
    def _():
        result = dot(joined[...], gate_up[...], contract_last)
        change = lax.dot_general(
            grad[...].reshape(2 * main, grad.shape[2])[:, :experts],
            router[...],
            (((1,), (0,)), ((), ())),
            precision=highest,
            preferred_element_type=f32,
        )
        out[...] = (result[:main] + change[:main]).astype(bf16)
        own = lax.broadcasted_iota(i32, (main, out.shape[1]), 0) % fold == step
        extra = result[main:]
        high = extra.astype(bf16)
        low = (extra - high.astype(f32)).astype(bf16)
        total[...] += (
            unfolded(high, step, experts)
            + unfolded(low, step, experts)
            + jnp.where(own, change[main:], 0.0)
        )

    @pl.when(step == fold)
    def _():
        out[...] = total[...].astype(bf16)


def reduce_kernel(back, out):
    folded = back[...].astype(f32).reshape(back.shape[0] // fold, *out.shape)
    out[...] = jnp.sum(folded, axis=0)


def grads_kernel(rows, joined, cot, hidden, out):
    wide = joined.shape[1]
    out[:, :wide] = dot(rows[...], joined[...], contract_first).astype(bf16)
    out[:, wide:] = dot(cot[...], hidden[...], contract_first).astype(bf16)


def exchange(array, experts):
    width = array.shape[1]
    moved = lax.all_to_all(
        array.reshape(experts, fold, width), "expert", split_axis=0, concat_axis=0, tiled=True
    )
    return moved.reshape(experts * fold, width)


def unpack(block, features, experts):
    part = features // fold
    extra = block[:, features : features + part].reshape(experts, features)
    return jnp.concatenate([block[:, :features], extra], axis=0)


def body(
    upper_out,
    lower_out,
    upper_cot,
    lower_cot,
    gate_up_weight,
    down_weight,
    router_weight,
    expert_ids,
    keep_mask,
):
    tokens, features = lower_out.shape
    experts = router_weight.shape[1]
    hidden_units = down_weight.shape[2]
    main = experts * fold
    part = features // fold
    ids, keep, router = expert_ids.T, keep_mask.T, router_weight.T
    gate_up = lax.all_gather(gate_up_weight[0], "dp", axis=0, tiled=True)
    down = lax.all_gather(down_weight[0].T, "dp", axis=1, tiled=True)
    whole = pl.BlockSpec(memory_space=pltpu.VMEM)
    scalar = pl.BlockSpec(memory_space=pltpu.SMEM)

    def shape(*dims, kind=bf16):
        return jax.ShapeDtypeStruct(dims, kind)

    packed = call(
        lambda *refs: send_rows_kernel(experts, *refs), shape(main, features + part), 10**6
    )(ids, keep, lower_out)
    arrived = exchange(packed, experts)
    cot_packed, mix, used = call(
        lambda *refs: send_cot_kernel(experts, *refs),
        (
            shape(main, features + part + facts_width),
            shape(tokens, 4 * main),
            shape(tokens, 2 * main),
        ),
        10**6,
    )(ids, keep, lower_out, upper_cot, router)
    cot_packed, gate_up, arrived = lax.optimization_barrier((cot_packed, gate_up, arrived))
    cot_arrived = exchange(cot_packed, experts)

    row_block = unpack(arrived, features, experts)
    projected = jnp.dot(row_block, gate_up, preferred_element_type=f32)
    gate_part = projected[:, :hidden_units]
    up_part = projected[:, hidden_units:]
    gate_sig = jax.nn.sigmoid(gate_part)
    activated = gate_part * gate_sig
    hidden = (activated * up_part).astype(bf16)
    slots = main + experts
    out_packed = call(
        lambda *refs: outputs_kernel(experts, *refs),
        shape(main, features + 2 * part),
        10**6,
        grid=(fold + 2,),
        in_specs=[
            pl.BlockSpec((slots, hidden_units), lambda i: (0, 0)),
            pl.BlockSpec((hidden_units, part), lambda i: (0, jnp.minimum(i, fold - 1))),
        ],
        out_specs=pl.BlockSpec((main, part), lambda i: (0, i)),
        scratch_shapes=[pltpu.VMEM((main, part), f32)],
    )(hidden, down)

    own = lax.axis_index("expert").astype(i32).reshape(1)
    block = pl.BlockSpec((main, part), lambda i: (0, fold + 1))
    out_packed, logit_grad = call(
        lambda own, cot, rows, sent, out, grad: router_kernel(
            experts, own, cot, rows, sent, out, grad
        ),
        (shape(main, features + 2 * part), shape(2, main, 128, kind=f32)),
        10**6,
        aliases={3: 0},
        grid=(1,),
        in_specs=[
            scalar,
            whole,
            whole,
            pl.BlockSpec((main, features + 2 * part), lambda i: (0, 0)),
        ],
        out_specs=(block, pl.BlockSpec((2, main, 128), lambda i: (0, 0, 0))),
    )(own, cot_arrived, arrived, out_packed)
    out_packed, cot_arrived, hidden, row_block, logit_grad = lax.optimization_barrier(
        (out_packed, cot_arrived, hidden, row_block, logit_grad)
    )
    out_back = exchange(out_packed, experts)

    joined, grads = call(
        lambda *refs: hidden_kernel(experts, *refs),
        (shape(slots, 2 * hidden_units), shape(slots, features)),
        10**6,
    )(cot_arrived, projected, down)
    both = call(
        grads_kernel,
        shape(features, 3 * hidden_units),
        10**6,
        grid=(fold,),
        in_specs=[
            pl.BlockSpec((slots, part), lambda i: (0, i)),
            pl.BlockSpec((slots, 2 * hidden_units), lambda i: (0, 0)),
            pl.BlockSpec((slots, part), lambda i: (0, i)),
            pl.BlockSpec((slots, hidden_units), lambda i: (0, 0)),
        ],
        out_specs=pl.BlockSpec((part, 3 * hidden_units), lambda i: (i, 0)),
    )(row_block, joined, grads, hidden)
    both = lax.psum_scatter(both, "dp", scatter_dimension=0, tiled=True)
    rows_packed = call(
        lambda *refs: rows_kernel(experts, *refs),
        shape(main, features + part),
        10**6,
        grid=(fold + 1,),
        in_specs=[
            pl.BlockSpec((slots, 2 * hidden_units), lambda i: (0, 0)),
            pl.BlockSpec((part, 2 * hidden_units), lambda i: (jnp.minimum(i, fold - 1), 0)),
            pl.BlockSpec((2, main, 128), lambda i: (0, 0, 0)),
            pl.BlockSpec((experts, part), lambda i: (0, jnp.minimum(i, fold - 1))),
        ],
        out_specs=pl.BlockSpec((main, part), lambda i: (0, i)),
        scratch_shapes=[pltpu.VMEM((main, part), f32)],
    )(joined, gate_up, logit_grad, router)
    router_row = call(
        reduce_kernel,
        shape(fold, part, kind=f32),
        3 * 10**11,
        grid=(1,),
        in_specs=[pl.BlockSpec((main, part), lambda i: (0, fold + 1))],
        out_specs=pl.BlockSpec((fold, part), lambda i: (0, 0)),
    )(out_back)
    rows_packed, router_row = lax.optimization_barrier((rows_packed, router_row))
    rows_back = exchange(rows_packed, experts)
    step, copies = 1, lax.axis_size("dp")
    while step < copies:
        pairs = [(d, d ^ step) for d in range(copies)]
        router_row = router_row + lax.ppermute(router_row, "dp", pairs)
        step *= 2
    upper_input = call(upper_kernel, shape(tokens, features, kind=f32), 10**6)(
        upper_out, out_back, mix
    )
    router_all = jnp.broadcast_to(router_row, (experts, fold, part))
    router_all, both, rows_back = lax.optimization_barrier((router_all, both, rows_back))
    router_all = exchange(router_all.reshape(main, part), experts)
    router_grad = router_all.reshape(experts, features).T
    lower_grad = call(lower_kernel, shape(tokens, features, kind=f32), 10**6)(
        lower_cot, rows_back, used
    )
    return (
        upper_input,
        lower_grad,
        both[None, :, : 2 * hidden_units],
        both[None, :, 2 * hidden_units :],
        router_grad,
    )


def solution(mesh):
    blocks = P(("expert", "dp"), None)
    split = P("expert", "dp", None)
    return jax.shard_map(
        body,
        mesh=mesh,
        in_specs=(blocks, blocks, blocks, blocks, split, split, P(), blocks, blocks),
        out_specs=(blocks, blocks, split, split, P()),
        check_vma=False,
    )
```

time: 244 us -> 215 us (0.88)
  Pallas kernels: 0 us -> 40.8 us
  waiting for transfers between devices: 121 us -> 85.4 us
  matrix products: 36.3 us -> 5.13 us
  starting transfers between devices: 35.4 us -> 51.8 us
  blocking collectives: 13.3 us -> 0 us
  other arithmetic: 10.7 us -> 1.43 us
  local copies, waits for them, and re-layouts: 10.9 us -> 14.5 us
    all_to_all x5, waiting for transfers between devices: 119 us -> 62.9 us  [exchange(): lax.all_to_all(array.reshape(experts, fold, width), 'expert', split_axis=...]
    pallas_call x0 -> x10, Pallas kernels: none -> 40.8 us  [the longest x1 10.1 us: body(): call(lambda *refs: rows_kernel(experts, *refs), shape(main, features + pa...]
    dot_general x13 -> x0, matrix products: 30.5 us -> none  [the longest x1 4.71 us: body(): lax.dot_general(joined, gate_up, contract_last, preferred_element_type=f32)]
    all_gather x1, waiting for transfers between devices: 0.01 us -> 17.1 us  [body(): down = lax.all_gather(down_weight[0].T, 'dp', axis=1, tiled=True)]
    all_gather x1 -> x0, blocking collectives: 13.3 us -> none  [body(): lax.all_gather(router_row.reshape(fold, -1), 'dp')]
    all_to_all x5, starting transfers between devices: 35.1 us -> 47.6 us  [exchange(): lax.all_to_all(array.reshape(experts, fold, width), 'expert', split_axis=...]
    concatenate x6 -> x1, other arithmetic: 8.8 us -> 1.12 us  [unpack(): return jnp.concatenate([block[:, :features], extra], axis=0)]
    unnamed x34 -> x48, local copies, waits for them, and re-layouts: 3.22 us -> 10.7 us
  transfers between devices with their start and end apart: 8 -> 11, of which waited for: 5 -> 8; matrix products, arithmetic and copies ran while one was open for 16% -> 5% of each run, Pallas kernels for 0% -> 17%
where the time goes in v2:
time: 215 us; the launch traced here: 213 us
  waiting for transfers between devices  85.4 us (40%)
  starting transfers between devices  51.8 us (24%)
  Pallas kernels  40.8 us (19%)
  local copies, waits for them, and re-layouts  14.5 us (7%)
  between operations  14 us (7%)
  matrix products  5.13 us (2%)
    all_to_all x5, waiting for transfers between devices, exchange(): lax.all_to_all(array.reshape(experts, fold, width), 'expert', split_axis=...  62.9 us
    all_to_all x5, starting transfers between devices, exchange(): lax.all_to_all(array.reshape(experts, fold, width), 'expert', split_axis=...  47.6 us
    all_gather x1, waiting for transfers between devices, body(): down = lax.all_gather(down_weight[0].T, 'dp', axis=1, tiled=True)  17.1 us
    unnamed x48, local copies, waits for them, and re-layouts  10.7 us
    pallas_call x1, Pallas kernels, body(): call(lambda *refs: rows_kernel(experts, *refs), shape(main, features + pa...  10.1 us
    pallas_call x1, Pallas kernels, body(): call(grads_kernel, shape(features, 3 * hidden_units), 10 ** 6, grid=(fold...  8.46 us
    pallas_call x1, Pallas kernels, body(): call(lambda *refs: outputs_kernel(experts, *refs), shape(main, features +...  6.24 us
    dot_general x1, matrix products, body(): projected = jnp.dot(row_block, gate_up, preferred_element_type=f32)  5.13 us
  transfers between devices with their start and end apart: 11, of which 8 were waited for; matrix products, arithmetic and copies ran while one was open for 5% of the time, Pallas kernels for 17%

profile of v2, /device:TPU:2, one launch (start us, length us, event | category | flops | bytes accessed | tf_op | source)
XLA Modules:
  0.0 213.1 jit_solution(12874816290503193655)
XLA Ops:
  7.2 0.7 all-gather.6.cloned.1.call-update
  8.0 0.7 all-gather.4.cloned.1.call-update
  8.7 0.7 copy-done.17
  9.4 0.7 copy-done.19
  10.0 1.9 shard_map.129
  11.9 11.8 %all-to-all-start = ((bf16[32,8,2304]{2,1,0:T(8,128)(2,1)}), bf16[32,8,2304]{2,1,0:T(8,128)(2,1)S(1)}, u32[]{:S(2)}, u32[]{:S(2)}) async-start(bf16[32,8,2304]{2,1,0:T(8,128)(2,1)} %bitcast.5), calls=%async_computation | async-start | bytes 2359296 | tf_op jit(solution)/shard_map/all_to_all | solution.py:300
  23.7 2.0 shard_map.128
  25.7 1.1 copy-done.7
  26.8 0.7 copy-done.13
  27.5 27.1 %all-to-all-done = bf16[32,8,2304]{2,1,0:T(8,128)(2,1)S(1)} async-done(((bf16[32,8,2304]{2,1,0:T(8,128)(2,1)}), bf16[32,8,2304]{2,1,0:T(8,128)(2,1)S(1)}, u32[]{:S(2)}, u32[]{:S(2)}) %all-to-all-start) | async-done | bytes 1179680 | tf_op jit(solution)/shard_map/all_to_all | solution.py:300
  54.6 9.7 %all-to-all-start.1 = ((bf16[32,8,2432]{2,1,0:T(8,128)(2,1)}), bf16[32,8,2432]{2,1,0:T(8,128)(2,1)S(1)}, u32[]{:S(2)}, u32[]{:S(2)}) async-start(bf16[32,8,2432]{2,1,0:T(8,128)(2,1)} %bitcast.31), calls=%async_computation.1 | async-start | bytes 2490368 | tf_op jit(solution)/shard_map/all_to_all | solution.py:300
  64.3 1.1 slice.18
  65.4 0.1 reshape.45
  65.4 5.1 %fusion.1.refs_1_ = f32[288,1408]{1,0:T(8,128)S(1)} fusion(bf16[2048,1408]{1,0:T(8,128)(2,1)} %bitcast.38, bf16[32,2048]{1,0:T(8,128)(2,1)S(1)} %reshape.45, bf16[256,2048]{1,0:T(8,128)(2,1)} %slice.18), kind=kOutput, calls=%fused_computation.5 | convolution fusion | flops 1663303680 | bytes 8568832 | tf_op jit(solution)/shard_map/dot_general | solution.py:354
  70.6 0.3 fusion.refs_0_.hidden
  70.9 1.2 copy-done.1
  72.1 17.1 %all-gather.4.cloned.1.call-done.refs_1_.refs_2_ = bf16[704,2048]{1,0:T(8,128)(2,1)} async-done(((bf16[704,256]{1,0:T(8,128)(2,1)}), bf16[704,2048]{1,0:T(8,128)(2,1)}) %all-gather.4.cloned.1.call-update) | async-done | bytes 2883600 | tf_op jit(solution)/shard_map/all_gather | solution.py:330
  89.1 1.8 copy-done
  91.0 6.2 %shard_map.130.sent = bf16[256,2560]{1,0:T(8,128)(2,1)} custom-call(bf16[288,704]{1,0:T(8,128)(2,1)S(1)} %fusion.refs_0_.hidden, bf16[704,2048]{1,0:T(8,128)(2,1)S(1)} %copy-done), custom_call_target="tpu_custom_call" | custom-call | flops 1000000 | tf_op jit(solution)/shard_map/pallas_call | solution.py:361
  97.2 1.1 pad_maximum_fusion.rows
  98.3 3.6 %shard_map.131 = (bf16[256,2560]{1,0:T(8,128)(2,1)}, f32[2,256,128]{2,1,0:T(8,128)S(1)}) custom-call(s32[1]{0:T(128)} %bitcast.own, bf16[256,2432]{1,0:T(8,128)(2,1)S(1)} %bitcast.25, bf16[256,2304]{1,0:T(8,128)(2,1)S(1)} %bitcast.29, bf16[256,2560]{1,0:T(8,128)(2,1)} %shard_map.130.sent), custom_call_target="tpu_custom_call", output_to_operand_aliasing={{0}: (3, {})} | custom-call | flops 1000000 | tf_op jit(solution)/shard_map/pallas_call | solution.py:376
  101.9 0.7 copy-done.15
  102.6 10.3 %all-to-all-start.2 = ((bf16[32,8,2560]{2,1,0:T(8,128)(2,1)}), bf16[32,8,2560]{2,1,0:T(8,128)(2,1)}, u32[]{:S(2)}, u32[]{:S(2)}) async-start(bf16[32,8,2560]{2,1,0:T(8,128)(2,1)} %bitcast.11), calls=%async_computation.2 | async-start | bytes 2621440 | tf_op jit(solution)/shard_map/all_to_all | solution.py:300
  113.0 3.2 %shard_map.133 = (bf16[288,1408]{1,0:T(8,128)(2,1)S(1)}, bf16[288,2048]{1,0:T(8,128)(2,1)S(1)}) custom-call(bf16[256,2432]{1,0:T(8,128)(2,1)S(1)} %bitcast.26, f32[288,1408]{1,0:T(8,128)S(1)} %copy-done.2, bf16[704,2048]{1,0:T(8,128)(2,1)} %all-gather.4.cloned.1.call-done.refs_1_.refs_2_), custom_call_target="tpu_custom_call" | custom-call | flops 1000000 | tf_op jit(solution)/shard_map/pallas_call | solution.py:397
  116.2 8.5 %shard_map.136 = bf16[2048,2112]{1,0:T(8,128)(2,1)} custom-call(bf16[288,2048]{1,0:T(8,128)(2,1)S(1)} %copy-done.3, bf16[288,1408]{1,0:T(8,128)(2,1)S(1)} %get-tuple-element.34.refs_0_.joined, bf16[288,2048]{1,0:T(8,128)(2,1)S(1)} %get-tuple-element.38.cot, bf16[288,704]{1,0:T(8,128)(2,1)S(1)} %fusion.refs_0_.hidden), custom_call_target="tpu_custom_call" | custom-call | flops 1000000 | tf_op jit(solution)/shard_map/pallas_call | solution.py:402
  124.7 0.9 copy-done.4
  125.6 1.1 copy-done.5
  126.8 0.1 copy-done.16
  126.9 10.1 %shard_map.134 = bf16[256,2304]{1,0:T(8,128)(2,1)} custom-call(bf16[288,1408]{1,0:T(8,128)(2,1)S(1)} %copy-done.5, bf16[2048,1408]{1,0:T(8,128)(2,1)} %bitcast.39, f32[2,256,128]{2,1,0:T(8,128)S(1)} %copy-done.16, f32[32,2048]{1,0:T(8,128)S(1)} %bitcast.33), custom_call_target="tpu_custom_call" | custom-call | flops 1000000 | tf_op jit(solution)/shard_map/pallas_call | solution.py:416
  136.9 10.2 %all-to-all-done.2 = bf16[32,8,2560]{2,1,0:T(8,128)(2,1)} async-done(((bf16[32,8,2560]{2,1,0:T(8,128)(2,1)}), bf16[32,8,2560]{2,1,0:T(8,128)(2,1)}, u32[]{:S(2)}, u32[]{:S(2)}) %all-to-all-start.2) | async-done | bytes 1310752 | tf_op jit(solution)/shard_map/all_to_all | solution.py:300
  147.1 0.9 shard_map.135
  148.1 5.7 %all-to-all-start.3 = ((bf16[32,8,2304]{2,1,0:T(8,128)(2,1)}), bf16[32,8,2304]{2,1,0:T(8,128)(2,1)S(1)}, u32[]{:S(2)}, u32[]{:S(2)}) async-start(bf16[32,8,2304]{2,1,0:T(8,128)(2,1)} %bitcast.13), calls=%async_computation.4 | async-start | bytes 2359296 | tf_op jit(solution)/shard_map/all_to_all | solution.py:300
  153.8 0.3 collective-permute-start
  154.1 1.2 collective-permute-done
  155.2 1.0 collective-permute-start.1
  156.3 2.8 %collective-permute-done.1 = f32[8,256]{1,0:T(8,128)S(1)} collective-permute-done((f32[8,256]{1,0:T(8,128)S(1)}, f32[8,256]{1,0:T(8,128)S(1)}, u32[]{:S(2)}, u32[]{:S(2)}) %collective-permute-start.1) | collective-permute-done | bytes 8224 | tf_op jit(solution)/shard_map/ppermute | solution.py:443
  159.0 2.7 %collective-permute-start.2 = (f32[8,256]{1,0:T(8,128)S(1)}, f32[8,256]{1,0:T(8,128)S(1)}, u32[]{:S(2)}, u32[]{:S(2)}) collective-permute-start(f32[8,256]{1,0:T(8,128)S(1)} %add.16), channel_id=1, source_target_pairs={{0,4},{1,5},{2,6},{3,7},{4,0},{5,1},{6,2},{7,3},{8,12},{9,13},{10,... | collective-permute-start | bytes 24584 | tf_op jit(solution)/shard_map/ppermute | solution.py:443
  161.8 3.0 %shard_map.132 = f32[128,2048]{1,0:T(8,128)} custom-call(f32[128,2048]{1,0:T(8,128)S(1)} %copy-done.8, bf16[256,2560]{1,0:T(8,128)(2,1)} %bitcast.12.back, bf16[128,1024]{1,0:T(8,128)(2,1)S(1)} %copy-done.14), custom_call_target="tpu_custom_call" | custom-call | flops 1000000 | tf_op jit(solution)/shard_map/pallas_call | solution.py:445
  164.8 19.1 %all-to-all-done.3 = bf16[32,8,2304]{2,1,0:T(8,128)(2,1)S(1)} async-done(((bf16[32,8,2304]{2,1,0:T(8,128)(2,1)}), bf16[32,8,2304]{2,1,0:T(8,128)(2,1)S(1)}, u32[]{:S(2)}, u32[]{:S(2)}) %all-to-all-start.3) | async-done | bytes 1179680 | tf_op jit(solution)/shard_map/all_to_all | solution.py:300
  183.9 0.2 reduce-scatter.2.cloned.1.call-done
  184.1 0.7 broadcast_in_dim.9
  184.8 10.1 %all-to-all-start.4 = ((f32[32,8,256]{2,1,0:T(8,128)}), f32[32,8,256]{2,1,0:T(8,128)S(1)}, u32[]{:S(2)}, u32[]{:S(2)}) async-start(f32[32,8,256]{2,1,0:T(8,128)} %broadcast_in_dim.9), calls=%async_computation.5 | async-start | bytes 524288 | tf_op jit(solution)/shard_map/all_to_all | solution.py:300
  194.9 1.0 slice_bitcast_fusion.1
  196.0 0.9 copy.15
  196.9 1.4 shard_map.137
  198.3 0.9 slice_bitcast_fusion
  199.2 6.5 %all-to-all-done.4 = f32[32,8,256]{2,1,0:T(8,128)S(1)} async-done(((f32[32,8,256]{2,1,0:T(8,128)}), f32[32,8,256]{2,1,0:T(8,128)S(1)}, u32[]{:S(2)}, u32[]{:S(2)}) %all-to-all-start.4) | async-done | bytes 262176 | tf_op jit(solution)/shard_map/all_to_all | solution.py:300
  205.8 0.8 copy.16
  (47 shorter events, 0.3 us)
Async XLA Ops:
  7.2 1.5 copy-start.6
  7.2 47.4 %all-gather.6.cloned.1.call-start = ((), (), s32[]{:S(2)}) async-start(), calls=%async_computation.8 | async-start | bytes 6488064 | tf_op jit(solution)/shard_map/all_gather | solution.py:329
  7.9 81.2 %all-gather.4.cloned.1.call-start = ((), (), s32[]{:S(2)}) async-start(), calls=%async_computation.6 | async-start | bytes 3244032 | tf_op jit(solution)/shard_map/all_gather | solution.py:330
  8.7 0.7 copy-start.17
  9.4 0.7 copy-start.19
  11.9 11.8 %copy-start.9 = (f32[2048,32]{0,1:T(8,128)S(1)}, f32[2048,32]{0,1:T(8,128)}, u32[]{:S(2)}) copy-start(f32[2048,32]{0,1:T(8,128)} %param.15) | copy-start | bytes 786436
  11.9 11.8 %copy-start.11 = (bf16[128,2048]{1,0:T(8,128)(2,1)S(1)}, bf16[128,2048]{1,0:T(8,128)(2,1)}, u32[]{:S(2)}) copy-start(bf16[128,2048]{1,0:T(8,128)(2,1)} %refs_3_.1) | copy-start | bytes 1572868
  11.9 11.8 %copy-start.18 = (s32[128,2]{0,1:T(2,128)S(1)}, s32[128,2]{0,1:T(2,128)}, u32[]{:S(2)}) copy-start(s32[128,2]{0,1:T(2,128)} %param.16) | copy-start | bytes 3076
  11.9 11.8 %copy-start.20 = (s32[128,2]{0,1:T(2,128)S(1)}, s32[128,2]{0,1:T(2,128)}, u32[]{:S(2)}) copy-start(s32[128,2]{0,1:T(2,128)} %param.17) | copy-start | bytes 3076
  11.9 42.6 %all-to-all-start = ((bf16[32,8,2304]{2,1,0:T(8,128)(2,1)}), bf16[32,8,2304]{2,1,0:T(8,128)(2,1)S(1)}, u32[]{:S(2)}, u32[]{:S(2)}) async-start(bf16[32,8,2304]{2,1,0:T(8,128)(2,1)} %bitcast.5), calls=%async_computation | async-start | bytes 2359296 | tf_op jit(solution)/shard_map/all_to_all | solution.py:300
  25.7 1.1 copy-start.7
  26.8 0.7 copy-start.13
  54.6 43.8 %all-to-all-start.1 = ((bf16[32,8,2432]{2,1,0:T(8,128)(2,1)}), bf16[32,8,2432]{2,1,0:T(8,128)(2,1)S(1)}, u32[]{:S(2)}, u32[]{:S(2)}) async-start(bf16[32,8,2432]{2,1,0:T(8,128)(2,1)} %bitcast.31), calls=%async_computation.1 | async-start | bytes 2490368 | tf_op jit(solution)/shard_map/all_to_all | solution.py:300
  70.9 1.2 copy-start.1
  89.1 1.8 copy-start
  91.0 6.2 %copy-start.21 = (bf16[256,2048]{1,0:T(8,128)(2,1)S(1)}, bf16[256,2048]{1,0:T(8,128)(2,1)}, u32[]{:S(2)}) copy-start(bf16[256,2048]{1,0:T(8,128)(2,1)} %slice.18) | copy-start | bytes 3145732
  101.9 0.7 copy-start.15
  102.6 10.4 %copy-start.2 = (f32[288,1408]{1,0:T(8,128)S(1)}, f32[288,1408]{1,0:T(8,128)}, u32[]{:S(2)}) copy-start(f32[288,1408]{1,0:T(8,128)} %copy-done.1) | copy-start | bytes 4866052
  102.6 44.5 %all-to-all-start.2 = ((bf16[32,8,2560]{2,1,0:T(8,128)(2,1)}), bf16[32,8,2560]{2,1,0:T(8,128)(2,1)}, u32[]{:S(2)}, u32[]{:S(2)}) async-start(bf16[32,8,2560]{2,1,0:T(8,128)(2,1)} %bitcast.11), calls=%async_computation.2 | async-start | bytes 2621440 | tf_op jit(solution)/shard_map/all_to_all | solution.py:300
  112.9 71.1 %reduce-scatter.2.cloned.1.call-start = ((), (), s32[]{:S(2)}) async-start(), calls=%async_computation.7 | async-start | bytes 10027008 | tf_op jit(solution)/shard_map/reduce_scatter | solution.py:415
  113.0 3.2 %copy-start.3 = (bf16[288,2048]{1,0:T(8,128)(2,1)S(1)}, bf16[288,2048]{1,0:T(8,128)(2,1)}, u32[]{:S(2)}) copy-start(bf16[288,2048]{1,0:T(8,128)(2,1)} %pad_maximum_fusion.rows) | copy-start | bytes 3538948
  124.7 0.9 copy-start.4
  125.6 1.1 copy-start.5
  125.6 1.2 copy-start.10
  125.6 1.3 copy-start.16
  148.0 13.7 %copy-start.8 = (f32[128,2048]{1,0:T(8,128)S(1)}, f32[128,2048]{1,0:T(8,128)}, u32[]{:S(2)}) copy-start(f32[128,2048]{1,0:T(8,128)} %upper.1) | copy-start | bytes 3145732
  148.0 13.7 %copy-start.14 = (bf16[128,1024]{1,0:T(8,128)(2,1)S(1)}, bf16[128,1024]{1,0:T(8,128)(2,1)}, u32[]{:S(2)}) copy-start(bf16[128,1024]{1,0:T(8,128)(2,1)} %copy-done.13) | copy-start | bytes 786436
  148.1 35.8 %all-to-all-start.3 = ((bf16[32,8,2304]{2,1,0:T(8,128)(2,1)}), bf16[32,8,2304]{2,1,0:T(8,128)(2,1)S(1)}, u32[]{:S(2)}, u32[]{:S(2)}) async-start(bf16[32,8,2304]{2,1,0:T(8,128)(2,1)} %bitcast.13), calls=%async_computation.4 | async-start | bytes 2359296 | tf_op jit(solution)/shard_map/all_to_all | solution.py:300
  153.8 1.4 collective-permute-start
  155.2 3.8 %collective-permute-start.1 = (f32[8,256]{1,0:T(8,128)S(1)}, f32[8,256]{1,0:T(8,128)S(1)}, u32[]{:S(2)}, u32[]{:S(2)}) collective-permute-start(f32[8,256]{1,0:T(8,128)S(1)} %add.15), channel_id=1, source_target_pairs={{0,2},{1,3},{2,0},{3,1},{4,6},{5,7},{6,4},{7,5},{8,10},{9,11},{10,... | collective-permute-start | bytes 24584 | tf_op jit(solution)/shard_map/ppermute | solution.py:443
  159.0 5.7 %collective-permute-start.2 = (f32[8,256]{1,0:T(8,128)S(1)}, f32[8,256]{1,0:T(8,128)S(1)}, u32[]{:S(2)}, u32[]{:S(2)}) collective-permute-start(f32[8,256]{1,0:T(8,128)S(1)} %add.16), channel_id=1, source_target_pairs={{0,4},{1,5},{2,6},{3,7},{4,0},{5,1},{6,2},{7,3},{8,12},{9,13},{10,... | collective-permute-start | bytes 24584 | tf_op jit(solution)/shard_map/ppermute | solution.py:443
  164.8 32.1 %copy-start.12 = (bf16[128,2048]{1,0:T(8,128)(2,1)S(1)}, bf16[128,2048]{1,0:T(8,128)(2,1)}, u32[]{:S(2)}) copy-start(bf16[128,2048]{1,0:T(8,128)(2,1)} %lower_cot.1) | copy-start | bytes 1572868
  184.8 21.0 %all-to-all-start.4 = ((f32[32,8,256]{2,1,0:T(8,128)}), f32[32,8,256]{2,1,0:T(8,128)S(1)}, u32[]{:S(2)}, u32[]{:S(2)}) async-start(f32[32,8,256]{2,1,0:T(8,128)} %broadcast_in_dim.9), calls=%async_computation.5 | async-start | bytes 524288 | tf_op jit(solution)/shard_map/all_to_all | solution.py:300
  196.9 1.4 copy-start.22
Sparse Core Ops, SparseCore 0:
  9.8 44.2 all-gather.5
  55.9 33.1 all-gather.3
  125.7 58.2 reduce-scatter.1

commit v3 on v2

--- a/solution.py
+++ b/solution.py
@@ -72,6 +72,12 @@
     if scale_extra is not None:
         total = total * scale_extra
     out[:, features : features + part] = total.astype(bf16)
+
+
+def weights_kernel(gate_up, down, out):
+    wide = gate_up.shape[1]
+    out[:, :wide] = gate_up[...]
+    out[:, wide:] = down[...].astype(f32).T.astype(bf16)
 
 
 def send_rows_kernel(experts, ids, keep, table, out):
@@ -202,10 +208,9 @@
 
 
 def hidden_kernel(experts, cot, projected, down, joined, rows):
-    features = down.shape[1]
+    features, units = down.shape
     part = features // fold
     main = experts * fold
-    units = down.shape[0]
     order = lax.broadcasted_iota(i32, (main, main), 1)
     place = lax.broadcasted_iota(i32, (main, main), 0)
     order = order == (place % experts) * fold + place // experts
@@ -213,7 +218,7 @@
     rows[:main, :] = cot[:, :features]
     for c in range(fold):
         rows[main:, c * part : (c + 1) * part] = extra[c * experts : (c + 1) * experts]
-    back = dot(rows[...], down[...], contract_last)
+    back = dot(rows[...], down[...])
     gate, up = projected[:, :units], projected[:, units:]
     gate_sig = jax.nn.sigmoid(gate)
     activated = gate * gate_sig
@@ -221,7 +226,31 @@
     joined[:, units:] = (back * activated).astype(bf16)
 
 
-def outputs_kernel(experts, hidden, down, out, total):
+def outputs_kernel(experts, hidden, down, out):
+    main = experts * fold
+    features = down.shape[0]
+    part = features // fold
+    total = jnp.zeros((main, part), f32)
+    for c in range(fold):
+        result = dot(hidden[...], down[c * part : (c + 1) * part, :], contract_last)
+        out[:, c * part : (c + 1) * part] = result[:main].astype(bf16)
+        total += unfolded(result[main:].astype(bf16), c, experts)
+    out[:, features : features + part] = total.astype(bf16)
+    out[:, features + part :] = jnp.zeros((main, part), bf16)
+
+
+def halves(value):
+    high = value.astype(bf16)
+    return high, (value - high.astype(f32)).astype(bf16)
+
+
+def unfolded(extra, step, experts):
+    row = lax.broadcasted_iota(i32, (experts * fold, extra.shape[0]), 0)
+    lane = lax.broadcasted_iota(i32, (experts * fold, extra.shape[0]), 1) % experts
+    return dot((row == lane * fold + step).astype(f32).astype(bf16), extra)
+
+
+def rows_kernel(experts, joined, gate_up, grad, router, out, total):
     step = pl.program_id(0)
     main = experts * fold
 
@@ -231,53 +260,19 @@
 
     @pl.when(step < fold)
     def _():
-        result = dot(hidden[...], down[...])
-        out[...] = result[:main].astype(bf16)
-        total[...] += unfolded(result[main:].astype(bf16), step, experts)
-
-    @pl.when(step == fold)
-    def _():
-        out[...] = total[...].astype(bf16)
-
-    @pl.when(step > fold)
-    def _():
-        out[...] = jnp.zeros_like(out)
-
-
-def unfolded(extra, step, experts):
-    row = lax.broadcasted_iota(i32, (experts * fold, experts), 0)
-    lane = lax.broadcasted_iota(i32, (experts * fold, experts), 1)
-    return dot((row == lane * fold + step).astype(f32).astype(bf16), extra)
-
-
-def rows_kernel(experts, joined, gate_up, grad, router, out, total):
-    step = pl.program_id(0)
-    main = experts * fold
-
-    @pl.when(step == 0)
-    def _():
-        total[...] = jnp.zeros_like(total)
-
-    @pl.when(step < fold)
-    def _():
         result = dot(joined[...], gate_up[...], contract_last)
-        change = lax.dot_general(
-            grad[...].reshape(2 * main, grad.shape[2])[:, :experts],
-            router[...],
-            (((1,), (0,)), ((), ())),
-            precision=highest,
-            preferred_element_type=f32,
+        left = grad[...].reshape(2 * main, grad.shape[2])[:, :experts]
+        left_high, left_low = halves(left)
+        right_high, right_low = halves(router[...])
+        change = dot(
+            jnp.concatenate([left_high, left_low, left_high], axis=1),
+            jnp.concatenate([right_high, right_high, right_low], axis=0),
         )
         out[...] = (result[:main] + change[:main]).astype(bf16)
         own = lax.broadcasted_iota(i32, (main, out.shape[1]), 0) % fold == step
         extra = result[main:]
-        high = extra.astype(bf16)
-        low = (extra - high.astype(f32)).astype(bf16)
-        total[...] += (
-            unfolded(high, step, experts)
-            + unfolded(low, step, experts)
-            + jnp.where(own, change[main:], 0.0)
-        )
+        total[...] += unfolded(jnp.concatenate(halves(extra), axis=0), step, experts)
+        total[...] += jnp.where(own, change[main:], 0.0)
 
     @pl.when(step == fold)
     def _():
@@ -287,6 +282,14 @@
 def reduce_kernel(back, out):
     folded = back[...].astype(f32).reshape(back.shape[0] // fold, *out.shape)
     out[...] = jnp.sum(folded, axis=0)
+
+
+def order_kernel(experts, own, parts, out):
+    part = parts.shape[2]
+    for e in range(experts):
+        piece = parts[own[0] ^ e]
+        for c in range(fold):
+            out[e : e + 1, c * part : (c + 1) * part] = piece[c : c + 1]
 
 
 def grads_kernel(rows, joined, cot, hidden, out):
@@ -326,14 +329,17 @@
     main = experts * fold
     part = features // fold
     ids, keep, router = expert_ids.T, keep_mask.T, router_weight.T
-    gate_up = lax.all_gather(gate_up_weight[0], "dp", axis=0, tiled=True)
-    down = lax.all_gather(down_weight[0].T, "dp", axis=1, tiled=True)
     whole = pl.BlockSpec(memory_space=pltpu.VMEM)
     scalar = pl.BlockSpec(memory_space=pltpu.SMEM)
 
     def shape(*dims, kind=bf16):
         return jax.ShapeDtypeStruct(dims, kind)
 
+    weights = call(weights_kernel, shape(gate_up_weight.shape[1], 3 * hidden_units), 10**6)(
+        gate_up_weight[0], down_weight[0].T
+    )
+    weights = lax.all_gather(weights, "dp", axis=0, tiled=True)
+    gate_up, down = weights[:, : 2 * hidden_units], weights[:, 2 * hidden_units :]
     packed = call(
         lambda *refs: send_rows_kernel(experts, *refs), shape(main, features + part), 10**6
     )(ids, keep, lower_out)
@@ -345,9 +351,9 @@
             shape(tokens, 4 * main),
             shape(tokens, 2 * main),
         ),
-        10**6,
+        3 * 10**11,
     )(ids, keep, lower_out, upper_cot, router)
-    cot_packed, gate_up, arrived = lax.optimization_barrier((cot_packed, gate_up, arrived))
+    cot_packed, arrived = lax.optimization_barrier((cot_packed, arrived))
     cot_arrived = exchange(cot_packed, experts)
 
     row_block = unpack(arrived, features, experts)
@@ -362,13 +368,6 @@
         lambda *refs: outputs_kernel(experts, *refs),
         shape(main, features + 2 * part),
         10**6,
-        grid=(fold + 2,),
-        in_specs=[
-            pl.BlockSpec((slots, hidden_units), lambda i: (0, 0)),
-            pl.BlockSpec((hidden_units, part), lambda i: (0, jnp.minimum(i, fold - 1))),
-        ],
-        out_specs=pl.BlockSpec((main, part), lambda i: (0, i)),
-        scratch_shapes=[pltpu.VMEM((main, part), f32)],
     )(hidden, down)
 
     own = lax.axis_index("expert").astype(i32).reshape(1)
@@ -426,7 +425,7 @@
         ],
         out_specs=pl.BlockSpec((main, part), lambda i: (0, i)),
         scratch_shapes=[pltpu.VMEM((main, part), f32)],
-    )(joined, gate_up, logit_grad, router)
+    )(joined, weights, logit_grad, router)
     router_row = call(
         reduce_kernel,
         shape(fold, part, kind=f32),
@@ -445,10 +444,20 @@
     upper_input = call(upper_kernel, shape(tokens, features, kind=f32), 10**6)(
         upper_out, out_back, mix
     )
-    router_all = jnp.broadcast_to(router_row, (experts, fold, part))
-    router_all, both, rows_back = lax.optimization_barrier((router_all, both, rows_back))
-    router_all = exchange(router_all.reshape(main, part), experts)
-    router_grad = router_all.reshape(experts, features).T
+    router_all = router_row[None]
+    step = 1
+    while step < experts:
+        pairs = [(e, e ^ step) for e in range(experts)]
+        theirs = lax.ppermute(router_all, "expert", pairs)
+        router_all = jnp.concatenate([router_all, theirs], axis=0)
+        step *= 2
+    router_grad = call(
+        lambda own, parts, out: order_kernel(experts, own, parts, out),
+        shape(experts, features, kind=f32),
+        10**6,
+        in_specs=[scalar, whole],
+        out_specs=whole,
+    )(own, router_all).T
     lower_grad = call(lower_kernel, shape(tokens, features, kind=f32), 10**6)(
         lower_cot, rows_back, used
     )

time: 215 us -> 196 us (0.912)
  starting transfers between devices: 51.8 us -> 42.3 us
  waiting for transfers between devices: 85.4 us -> 76.5 us
    ppermute x0 -> x5, waiting for transfers between devices: none -> 19.6 us  [body(): theirs = lax.ppermute(router_all, 'expert', pairs)]
    all_to_all x5 -> x4, starting transfers between devices: 47.6 us -> 29.5 us  [exchange(): lax.all_to_all(array.reshape(experts, fold, width), 'expert', split_axis=...]
    all_to_all x5 -> x4, waiting for transfers between devices: 62.9 us -> 47.6 us  [exchange(): lax.all_to_all(array.reshape(experts, fold, width), 'expert', split_axis=...]
    all_gather x2 -> x1, waiting for transfers between devices: 17.1 us -> 3.81 us  [body(): weights = lax.all_gather(weights, 'dp', axis=0, tiled=True)]
    ppermute x0 -> x5, starting transfers between devices: none -> 7.63 us  [body(): theirs = lax.ppermute(router_all, 'expert', pairs)]
    unnamed x48 -> x49, local copies, waits for them, and re-layouts: 10.7 us -> 6.63 us
    pallas_call x1, Pallas kernels: 6.24 us -> 2.93 us  [body(): call(lambda *refs: outputs_kernel(experts, *refs), shape(main, features +...]
    slice x0 -> x1, local copies, waits for them, and re-layouts: none -> 2.18 us  [body(): weights[:, 2 * hidden_units:]]
  transfers between devices with their start and end apart: 11 -> 14, of which waited for: 8 -> 12; matrix products, arithmetic and copies ran while one was open for 5% -> 6% of each run, Pallas kernels for 17% -> 18%
where the time goes in v3:
time: 196 us; the launch traced here: 194 us
  waiting for transfers between devices  76.5 us (39%)
  starting transfers between devices  42.3 us (22%)
  Pallas kernels  40.1 us (20%)
  between operations  14.3 us (7%)
  local copies, waits for them, and re-layouts  13.1 us (7%)
  matrix products  5.82 us (3%)
    all_to_all x4, waiting for transfers between devices, exchange(): lax.all_to_all(array.reshape(experts, fold, width), 'expert', split_axis=...  47.6 us
    all_to_all x4, starting transfers between devices, exchange(): lax.all_to_all(array.reshape(experts, fold, width), 'expert', split_axis=...  29.5 us
    ppermute x5, waiting for transfers between devices, body(): theirs = lax.ppermute(router_all, 'expert', pairs)  19.6 us
    pallas_call x1, Pallas kernels, body(): call(lambda *refs: rows_kernel(experts, *refs), shape(main, features + pa...  9.13 us
    pallas_call x1, Pallas kernels, body(): call(grads_kernel, shape(features, 3 * hidden_units), 10 ** 6, grid=(fold...  8.37 us
    ppermute x5, starting transfers between devices, body(): theirs = lax.ppermute(router_all, 'expert', pairs)  7.63 us
    unnamed x49, local copies, waits for them, and re-layouts  6.63 us
    dot_general x1, matrix products, body(): projected = jnp.dot(row_block, gate_up, preferred_element_type=f32)  5.82 us
  transfers between devices with their start and end apart: 14, of which 12 were waited for; matrix products, arithmetic and copies ran while one was open for 6% of the time, Pallas kernels for 18%

profile of v3, /device:TPU:2, one launch (start us, length us, event | category | flops | bytes accessed | tf_op | source)
XLA Modules:
  0.0 193.6 jit_solution(6427867043051920097)
XLA Ops:
  7.2 1.1 copy-done.5
  8.3 1.0 copy-done.8
  9.3 1.2 shard_map.130
  10.6 1.9 shard_map.129
  12.4 11.8 %all-to-all-start = ((bf16[32,8,2304]{2,1,0:T(8,128)(2,1)}), bf16[32,8,2304]{2,1,0:T(8,128)(2,1)}, u32[]{:S(2)}, u32[]{:S(2)}) async-start(bf16[32,8,2304]{2,1,0:T(8,128)(2,1)} %bitcast.4), calls=%async_computation | async-start | bytes 2359296 | tf_op jit(solution)/shard_map/all_to_all | solution.py:303
  24.2 3.0 %shard_map.128 = (bf16[256,2432]{1,0:T(8,128)(2,1)}, bf16[128,1024]{1,0:T(8,128)(2,1)S(1)}, bf16[128,512]{1,0:T(8,128)(2,1)S(1)}) custom-call(s32[2,128]{1,0:T(2,128)S(1)} %bitcast.32, s32[2,128]{1,0:T(2,128)S(1)} %bitcast.34, bf16[128,2048]{1,0:T(8,128)(2,1)S(1)} %copy-done.6, bf16[128,2048]{1,0:T(8,128)(2,1)S(1)} %copy-done.17, f32[32,2048]{1,0:T(8,128)S(1)} %bitcast.29), custom_call_target="tpu_custom_call" | custom-call | flops 299999985664 | tf_op jit(solution)/shard_map/pallas_call | solution.py:347
  27.3 0.7 copy-done.9
  28.0 27.2 %all-to-all-done = bf16[32,8,2304]{2,1,0:T(8,128)(2,1)} async-done(((bf16[32,8,2304]{2,1,0:T(8,128)(2,1)}), bf16[32,8,2304]{2,1,0:T(8,128)(2,1)}, u32[]{:S(2)}, u32[]{:S(2)}) %all-to-all-start) | async-done | bytes 1179680 | tf_op jit(solution)/shard_map/all_to_all | solution.py:303
  55.2 5.6 %all-to-all-start.1 = ((bf16[32,8,2432]{2,1,0:T(8,128)(2,1)}), bf16[32,8,2432]{2,1,0:T(8,128)(2,1)S(1)}, u32[]{:S(2)}, u32[]{:S(2)}) async-start(bf16[32,8,2432]{2,1,0:T(8,128)(2,1)} %bitcast.6), calls=%async_computation.1 | async-start | bytes 2490368 | tf_op jit(solution)/shard_map/all_to_all | solution.py:303
  60.7 0.9 slice.25
  61.7 1.3 slice.24
  63.1 1.2 pad_maximum_fusion.rows
  64.3 3.8 %all-gather.2.cloned.1.call-done.refs_1_ = bf16[2048,2112]{1,0:T(8,128)(2,1)} async-done(((bf16[256,2112]{1,0:T(8,128)(2,1)}), bf16[2048,2112]{1,0:T(8,128)(2,1)}) %all-gather.2.cloned.1.call-update) | async-done | bytes 8650768 | tf_op jit(solution)/shard_map/all_gather | solution.py:341
  68.1 2.2 %slice.35.refs_1_.refs_2_ = bf16[2048,704]{1,0:T(8,128)(2,1)S(1)} slice(bf16[2048,2112]{1,0:T(8,128)(2,1)} %all-gather.2.cloned.1.call-done.refs_1_), slice={[0:2048], [1408:2112]} | slice | bytes 5767168 | tf_op jit(solution)/shard_map/slice | solution.py:342
  70.3 5.8 %fusion.refs_1_ = f32[288,1408]{1,0:T(8,128)S(1)} fusion(bf16[2048,2112]{1,0:T(8,128)(2,1)} %all-gather.2.cloned.1.call-done.refs_1_, bf16[32,2048]{1,0:T(8,128)(2,1)} %copy-done.21, bf16[256,2048]{1,0:T(8,128)(2,1)S(1)} %copy-done.19), kind=kOutput, calls=%fused_computation | convolution fusion | flops 1663303680 | bytes 8568832 | tf_op jit(solution)/shard_map/dot_general | solution.py:360
  76.2 0.3 fusion.2.refs_0_.hidden
  76.5 2.9 %shard_map.131.sent = bf16[256,2560]{1,0:T(8,128)(2,1)} custom-call(bf16[288,704]{1,0:T(8,128)(2,1)S(1)} %fusion.2.refs_0_.hidden, bf16[2048,704]{1,0:T(8,128)(2,1)S(1)} %slice.35.refs_1_.refs_2_), custom_call_target="tpu_custom_call" | custom-call | flops 1000000 | tf_op jit(solution)/shard_map/pallas_call | solution.py:367
  79.4 12.0 %all-to-all-done.1 = bf16[32,8,2432]{2,1,0:T(8,128)(2,1)S(1)} async-done(((bf16[32,8,2432]{2,1,0:T(8,128)(2,1)}), bf16[32,8,2432]{2,1,0:T(8,128)(2,1)S(1)}, u32[]{:S(2)}, u32[]{:S(2)}) %all-to-all-start.1) | async-done | bytes 1245216 | tf_op jit(solution)/shard_map/all_to_all | solution.py:303
  91.4 4.0 %shard_map.132 = (bf16[256,2560]{1,0:T(8,128)(2,1)}, f32[2,256,128]{2,1,0:T(8,128)S(1)}) custom-call(s32[1]{0:T(128)} %bitcast.own, bf16[256,2432]{1,0:T(8,128)(2,1)S(1)} %bitcast.24, bf16[256,2304]{1,0:T(8,128)(2,1)} %bitcast.5.rows, bf16[256,2560]{1,0:T(8,128)(2,1)} %shard_map.131.sent), custom_call_target="tpu_custom_call", output_to_operand_aliasing={{0}: (3, {})} | custom-call | flops 1000000 | tf_op jit(solution)/shard_map/pallas_call | solution.py:375
  95.4 0.7 copy-done.13
  96.1 6.0 %all-to-all-start.2 = ((bf16[32,8,2560]{2,1,0:T(8,128)(2,1)}), bf16[32,8,2560]{2,1,0:T(8,128)(2,1)}, u32[]{:S(2)}, u32[]{:S(2)}) async-start(bf16[32,8,2560]{2,1,0:T(8,128)(2,1)} %bitcast.11), calls=%async_computation.2 | async-start | bytes 2621440 | tf_op jit(solution)/shard_map/all_to_all | solution.py:303
  102.3 3.4 %shard_map.134 = (bf16[288,1408]{1,0:T(8,128)(2,1)S(1)}, bf16[288,2048]{1,0:T(8,128)(2,1)S(1)}) custom-call(bf16[256,2432]{1,0:T(8,128)(2,1)S(1)} %bitcast.25, f32[288,1408]{1,0:T(8,128)S(1)} %fusion.refs_1_, bf16[2048,704]{1,0:T(8,128)(2,1)} %copy-done), custom_call_target="tpu_custom_call" | custom-call | flops 1000000 | tf_op jit(solution)/shard_map/pallas_call | solution.py:396
  105.7 8.4 %shard_map.138 = bf16[2048,2112]{1,0:T(8,128)(2,1)} custom-call(bf16[288,2048]{1,0:T(8,128)(2,1)S(1)} %copy-done.1, bf16[288,1408]{1,0:T(8,128)(2,1)S(1)} %get-tuple-element.29.refs_0_.joined, bf16[288,2048]{1,0:T(8,128)(2,1)S(1)} %get-tuple-element.34.cot, bf16[288,704]{1,0:T(8,128)(2,1)S(1)} %fusion.2.refs_0_.hidden), custom_call_target="tpu_custom_call" | custom-call | flops 1000000 | tf_op jit(solution)/shard_map/pallas_call | solution.py:401
  114.1 0.9 copy-done.2
  115.0 1.1 copy-done.3
  116.2 9.1 %shard_map.135 = bf16[256,2304]{1,0:T(8,128)(2,1)} custom-call(bf16[288,1408]{1,0:T(8,128)(2,1)S(1)} %copy-done.3, bf16[2048,2112]{1,0:T(8,128)(2,1)} %all-gather.2.cloned.1.call-done.refs_1_, f32[2,256,128]{2,1,0:T(8,128)S(1)} %copy-done.14, f32[32,2048]{1,0:T(8,128)S(1)} %bitcast.30), custom_call_target="tpu_custom_call" | custom-call | flops 1000000 | tf_op jit(solution)/shard_map/pallas_call | solution.py:415
  125.4 8.4 %all-to-all-done.2 = bf16[32,8,2560]{2,1,0:T(8,128)(2,1)} async-done(((bf16[32,8,2560]{2,1,0:T(8,128)(2,1)}), bf16[32,8,2560]{2,1,0:T(8,128)(2,1)}, u32[]{:S(2)}, u32[]{:S(2)}) %all-to-all-start.2) | async-done | bytes 1310752 | tf_op jit(solution)/shard_map/all_to_all | solution.py:303
  133.8 0.9 shard_map.136
  134.7 6.1 %all-to-all-start.3 = ((bf16[32,8,2304]{2,1,0:T(8,128)(2,1)}), bf16[32,8,2304]{2,1,0:T(8,128)(2,1)S(1)}, u32[]{:S(2)}, u32[]{:S(2)}) async-start(bf16[32,8,2304]{2,1,0:T(8,128)(2,1)} %bitcast.13), calls=%async_computation.3 | async-start | bytes 2359296 | tf_op jit(solution)/shard_map/all_to_all | solution.py:303
  141.0 1.2 collective-permute-done
  142.1 1.6 collective-permute-start.1
  143.7 2.2 %collective-permute-done.1 = f32[8,256]{1,0:T(8,128)S(1)} collective-permute-done((f32[8,256]{1,0:T(8,128)S(1)}, f32[8,256]{1,0:T(8,128)S(1)}, u32[]{:S(2)}, u32[]{:S(2)}) %collective-permute-start.1) | collective-permute-done | bytes 8224 | tf_op jit(solution)/shard_map/ppermute | solution.py:442
  145.9 3.2 %collective-permute-start.2 = (f32[8,256]{1,0:T(8,128)S(1)}, f32[8,256]{1,0:T(8,128)S(1)}, u32[]{:S(2)}, u32[]{:S(2)}) collective-permute-start(f32[8,256]{1,0:T(8,128)S(1)} %add.16), channel_id=1, source_target_pairs={{0,4},{1,5},{2,6},{3,7},{4,0},{5,1},{6,2},{7,3},{8,12},{9,13},{10,... | collective-permute-start | bytes 24584 | tf_op jit(solution)/shard_map/ppermute | solution.py:442
  149.1 2.1 %collective-permute-done.2 = f32[8,256]{1,0:T(8,128)S(1)} collective-permute-done((f32[8,256]{1,0:T(8,128)S(1)}, f32[8,256]{1,0:T(8,128)S(1)}, u32[]{:S(2)}, u32[]{:S(2)}) %collective-permute-start.2) | collective-permute-done | bytes 8224 | tf_op jit(solution)/shard_map/ppermute | solution.py:442
  151.5 4.2 %collective-permute-done.3 = f32[1,8,256]{2,1,0:T(8,128)S(1)} collective-permute-done((f32[1,8,256]{2,1,0:T(8,128)S(1)}, f32[1,8,256]{2,1,0:T(8,128)S(1)}, u32[]{:S(2)}, u32[]{:S(2)}) %collective-permute-start.3) | collective-permute-done | bytes 8224 | tf_op jit(solution)/shard_map/ppermute | solution.py:451
  155.7 1.3 collective-permute-start.4
  157.0 5.1 %collective-permute-done.4 = f32[2,8,256]{2,1,0:T(8,128)S(1)} collective-permute-done((f32[2,8,256]{2,1,0:T(8,128)S(1)}, f32[2,8,256]{2,1,0:T(8,128)S(1)}, u32[]{:S(2)}, u32[]{:S(2)}) %collective-permute-start.4) | collective-permute-done | bytes 16416 | tf_op jit(solution)/shard_map/ppermute | solution.py:451
  162.1 4.4 %collective-permute-done.5 = f32[4,8,256]{2,1,0:T(8,128)S(1)} collective-permute-done((f32[4,8,256]{2,1,0:T(8,128)S(1)}, f32[4,8,256]{2,1,0:T(8,128)S(1)}, u32[]{:S(2)}, u32[]{:S(2)}) %collective-permute-start.5) | collective-permute-done | bytes 32800 | tf_op jit(solution)/shard_map/ppermute | solution.py:451
  166.5 1.6 collective-permute-start.6
  168.2 4.0 %collective-permute-done.6 = f32[8,8,256]{2,1,0:T(8,128)S(1)} collective-permute-done((f32[8,8,256]{2,1,0:T(8,128)S(1)}, f32[8,8,256]{2,1,0:T(8,128)S(1)}, u32[]{:S(2)}, u32[]{:S(2)}) %collective-permute-start.6) | collective-permute-done | bytes 65568 | tf_op jit(solution)/shard_map/ppermute | solution.py:451
  172.2 4.4 %collective-permute-start.7 = (f32[16,8,256]{2,1,0:T(8,128)S(1)}, f32[16,8,256]{2,1,0:T(8,128)S(1)}, u32[]{:S(2)}, u32[]{:S(2)}) collective-permute-start(f32[16,8,256]{2,1,0:T(8,128)S(1)} %get-tuple-element.44), channel_id=1, source_target_pairs={{0,128},{8,136},{16,144},{24,152},{32,160},{40,168},{48,176},{56,1... | collective-permute-start | bytes 393224 | tf_op jit(solution)/shard_map/ppermute | solution.py:451
  176.6 3.1 %shard_map.133 = f32[128,2048]{1,0:T(8,128)} custom-call(f32[128,2048]{1,0:T(8,128)S(1)} %copy-done.4, bf16[256,2560]{1,0:T(8,128)(2,1)} %bitcast.12.back, bf16[128,1024]{1,0:T(8,128)(2,1)S(1)} %copy-done.10), custom_call_target="tpu_custom_call" | custom-call | flops 1000000 | tf_op jit(solution)/shard_map/pallas_call | solution.py:444
  179.7 1.9 collective-permute-done.7
  181.6 0.8 shard_map.139
  182.4 1.4 shard_map.137
  183.8 1.1 slice_bitcast_fusion.1
  184.9 0.9 copy.15
  185.9 0.9 slice_bitcast_fusion
  (60 shorter events, 1.0 us)
Async XLA Ops:
  7.2 61.0 %all-gather.2.cloned.1.call-start = ((), (), s32[]{:S(2)}) async-start(), calls=%async_computation.5 | async-start | bytes 10027008 | tf_op jit(solution)/shard_map/all_gather | solution.py:341
  7.2 1.1 copy-start.5
  8.3 1.0 copy-start.8
  9.3 1.2 copy-start.6
  9.3 1.2 copy-start.15
  9.3 1.2 copy-start.16
  12.4 11.8 %copy-start.11 = (f32[2048,32]{0,1:T(8,128)S(1)}, f32[2048,32]{0,1:T(8,128)}, u32[]{:S(2)}) copy-start(f32[2048,32]{0,1:T(8,128)} %param.15) | copy-start | bytes 786436
  12.4 11.8 %copy-start.17 = (bf16[128,2048]{1,0:T(8,128)(2,1)S(1)}, bf16[128,2048]{1,0:T(8,128)(2,1)}, u32[]{:S(2)}) copy-start(bf16[128,2048]{1,0:T(8,128)(2,1)} %refs_3_.1) | copy-start | bytes 1572868
  12.4 42.7 %all-to-all-start = ((bf16[32,8,2304]{2,1,0:T(8,128)(2,1)}), bf16[32,8,2304]{2,1,0:T(8,128)(2,1)}, u32[]{:S(2)}, u32[]{:S(2)}) async-start(bf16[32,8,2304]{2,1,0:T(8,128)(2,1)} %bitcast.4), calls=%async_computation | async-start | bytes 2359296 | tf_op jit(solution)/shard_map/all_to_all | solution.py:303
  27.3 0.7 copy-start.9
  55.2 36.2 %all-to-all-start.1 = ((bf16[32,8,2432]{2,1,0:T(8,128)(2,1)}), bf16[32,8,2432]{2,1,0:T(8,128)(2,1)S(1)}, u32[]{:S(2)}, u32[]{:S(2)}) async-start(bf16[32,8,2432]{2,1,0:T(8,128)(2,1)} %bitcast.6), calls=%async_computation.1 | async-start | bytes 2490368 | tf_op jit(solution)/shard_map/all_to_all | solution.py:303
  63.0 1.4 copy-start.18
  63.0 5.1 %copy-start.21 = (bf16[32,2048]{1,0:T(8,128)(2,1)}, bf16[32,2048]{1,0:T(8,128)(2,1)S(1)}, u32[]{:S(2)}) copy-start(bf16[32,2048]{1,0:T(8,128)(2,1)S(1)} %reshape.45) | copy-start | bytes 393220
  68.1 2.2 %copy-start.19 = (bf16[256,2048]{1,0:T(8,128)(2,1)S(1)}, bf16[256,2048]{1,0:T(8,128)(2,1)}, u32[]{:S(2)}) copy-start(bf16[256,2048]{1,0:T(8,128)(2,1)} %copy-done.18) | copy-start | bytes 3145732
  70.3 6.1 %copy-start = (bf16[2048,704]{1,0:T(8,128)(2,1)}, bf16[2048,704]{1,0:T(8,128)(2,1)S(1)}, u32[]{:S(2)}) copy-start(bf16[2048,704]{1,0:T(8,128)(2,1)S(1)} %slice.35.refs_1_.refs_2_) | copy-start | bytes 8650756
  95.4 0.7 copy-start.13
  96.1 37.7 %all-to-all-start.2 = ((bf16[32,8,2560]{2,1,0:T(8,128)(2,1)}), bf16[32,8,2560]{2,1,0:T(8,128)(2,1)}, u32[]{:S(2)}, u32[]{:S(2)}) async-start(bf16[32,8,2560]{2,1,0:T(8,128)(2,1)} %bitcast.11), calls=%async_computation.2 | async-start | bytes 2621440 | tf_op jit(solution)/shard_map/all_to_all | solution.py:303
  102.1 81.7 %reduce-scatter.2.cloned.1.call-start = ((), (), s32[]{:S(2)}) async-start(), calls=%async_computation.6 | async-start | bytes 10027008 | tf_op jit(solution)/shard_map/reduce_scatter | solution.py:414
  102.3 3.4 %copy-start.1 = (bf16[288,2048]{1,0:T(8,128)(2,1)S(1)}, bf16[288,2048]{1,0:T(8,128)(2,1)}, u32[]{:S(2)}) copy-start(bf16[288,2048]{1,0:T(8,128)(2,1)} %pad_maximum_fusion.rows) | copy-start | bytes 3538948
  114.1 0.9 copy-start.2
  114.9 1.1 copy-start.3
  115.0 1.2 copy-start.12
  115.0 1.3 copy-start.14
  134.7 41.9 %copy-start.4 = (f32[128,2048]{1,0:T(8,128)S(1)}, f32[128,2048]{1,0:T(8,128)}, u32[]{:S(2)}) copy-start(f32[128,2048]{1,0:T(8,128)} %upper.1) | copy-start | bytes 3145732
  134.7 41.9 %copy-start.10 = (bf16[128,1024]{1,0:T(8,128)(2,1)S(1)}, bf16[128,1024]{1,0:T(8,128)(2,1)}, u32[]{:S(2)}) copy-start(bf16[128,1024]{1,0:T(8,128)(2,1)} %copy-done.9) | copy-start | bytes 786436
  134.7 47.7 %all-to-all-start.3 = ((bf16[32,8,2304]{2,1,0:T(8,128)(2,1)}), bf16[32,8,2304]{2,1,0:T(8,128)(2,1)S(1)}, u32[]{:S(2)}, u32[]{:S(2)}) async-start(bf16[32,8,2304]{2,1,0:T(8,128)(2,1)} %bitcast.13), calls=%async_computation.3 | async-start | bytes 2359296 | tf_op jit(solution)/shard_map/all_to_all | solution.py:303
  140.9 1.3 collective-permute-start
  142.1 3.8 %collective-permute-start.1 = (f32[8,256]{1,0:T(8,128)S(1)}, f32[8,256]{1,0:T(8,128)S(1)}, u32[]{:S(2)}, u32[]{:S(2)}) collective-permute-start(f32[8,256]{1,0:T(8,128)S(1)} %add.15), channel_id=1, source_target_pairs={{0,2},{1,3},{2,0},{3,1},{4,6},{5,7},{6,4},{7,5},{8,10},{9,11},{10,... | collective-permute-start | bytes 24584 | tf_op jit(solution)/shard_map/ppermute | solution.py:442
  145.9 5.3 %collective-permute-start.2 = (f32[8,256]{1,0:T(8,128)S(1)}, f32[8,256]{1,0:T(8,128)S(1)}, u32[]{:S(2)}, u32[]{:S(2)}) collective-permute-start(f32[8,256]{1,0:T(8,128)S(1)} %add.16), channel_id=1, source_target_pairs={{0,4},{1,5},{2,6},{3,7},{4,0},{5,1},{6,2},{7,3},{8,12},{9,13},{10,... | collective-permute-start | bytes 24584 | tf_op jit(solution)/shard_map/ppermute | solution.py:442
  151.3 4.4 %collective-permute-start.3 = (f32[1,8,256]{2,1,0:T(8,128)S(1)}, f32[1,8,256]{2,1,0:T(8,128)S(1)}, u32[]{:S(2)}, u32[]{:S(2)}) collective-permute-start(f32[1,8,256]{2,1,0:T(8,128)S(1)} %get-tuple-element.43), channel_id=1, source_target_pairs={{0,8},{8,0},{16,24},{24,16},{32,40},{40,32},{48,56},{56,48},{64,72... | collective-permute-start | bytes 24584 | tf_op jit(solution)/shard_map/ppermute | solution.py:451
  155.7 6.4 %collective-permute-start.4 = (f32[2,8,256]{2,1,0:T(8,128)S(1)}, f32[2,8,256]{2,1,0:T(8,128)S(1)}, u32[]{:S(2)}, u32[]{:S(2)}) collective-permute-start(f32[2,8,256]{2,1,0:T(8,128)S(1)} %pad_maximum_fusion.3), channel_id=1, source_target_pairs={{0,16},{8,24},{16,0},{24,8},{32,48},{40,56},{48,32},{56,40},{64,80... | collective-permute-start | bytes 49160 | tf_op jit(solution)/shard_map/ppermute | solution.py:451
  162.1 4.4 %collective-permute-start.5 = (f32[4,8,256]{2,1,0:T(8,128)S(1)}, f32[4,8,256]{2,1,0:T(8,128)S(1)}, u32[]{:S(2)}, u32[]{:S(2)}) collective-permute-start(f32[4,8,256]{2,1,0:T(8,128)S(1)} %pad_maximum_fusion.2), channel_id=1, source_target_pairs={{0,32},{8,40},{16,48},{24,56},{32,0},{40,8},{48,16},{56,24},{64,96... | collective-permute-start | bytes 98312 | tf_op jit(solution)/shard_map/ppermute | solution.py:451
  166.5 5.6 %collective-permute-start.6 = (f32[8,8,256]{2,1,0:T(8,128)S(1)}, f32[8,8,256]{2,1,0:T(8,128)S(1)}, u32[]{:S(2)}, u32[]{:S(2)}) collective-permute-start(f32[8,8,256]{2,1,0:T(8,128)S(1)} %pad_maximum_fusion.1), channel_id=1, source_target_pairs={{0,64},{8,72},{16,80},{24,88},{32,96},{40,104},{48,112},{56,120},{... | collective-permute-start | bytes 196616 | tf_op jit(solution)/shard_map/ppermute | solution.py:451
  172.2 9.4 %collective-permute-start.7 = (f32[16,8,256]{2,1,0:T(8,128)S(1)}, f32[16,8,256]{2,1,0:T(8,128)S(1)}, u32[]{:S(2)}, u32[]{:S(2)}) collective-permute-start(f32[16,8,256]{2,1,0:T(8,128)S(1)} %get-tuple-element.44), channel_id=1, source_target_pairs={{0,128},{8,136},{16,144},{24,152},{32,160},{40,168},{48,176},{56,1... | collective-permute-start | bytes 393224 | tf_op jit(solution)/shard_map/ppermute | solution.py:451
  176.6 5.8 %copy-start.7 = (bf16[128,2048]{1,0:T(8,128)(2,1)S(1)}, bf16[128,2048]{1,0:T(8,128)(2,1)}, u32[]{:S(2)}) copy-start(bf16[128,2048]{1,0:T(8,128)(2,1)} %lower_cot.1) | copy-start | bytes 1572868
  183.8 2.0 %copy-start.20 = (bf16[256,2112]{1,0:T(8,128)(2,1)S(1)}, bf16[256,2112]{1,0:T(8,128)(2,1)}, u32[]{:S(2)}) copy-start(bf16[256,2112]{1,0:T(8,128)(2,1)} %reduce-scatter.2.cloned.1.call-done) | copy-start | bytes 3244036
Sparse Core Ops, SparseCore 0:
  10.6 57.4 all-gather.1
  115.1 58.7 reduce-scatter.1

commit v4 on v3

--- a/solution.py
+++ b/solution.py
@@ -74,13 +74,10 @@
     out[:, features : features + part] = total.astype(bf16)
 
 
-def weights_kernel(gate_up, down, out):
+def send_rows_kernel(experts, ids, keep, table, gate_up, down, weights, out):
     wide = gate_up.shape[1]
-    out[:, :wide] = gate_up[...]
-    out[:, wide:] = down[...].astype(f32).T.astype(bf16)
-
-
-def send_rows_kernel(experts, ids, keep, table, out):
+    weights[:, :wide] = gate_up[...]
+    weights[:, wide:] = down[...].astype(f32).T.astype(bf16)
     _, slots = places(ids[...], experts)
     kept = keep[...].astype(f32)
     main, extra = spread(slots, (kept[:1], kept[1:]), experts)
@@ -129,11 +126,11 @@
         used[:, k * width : (k + 1) * width] = value.T.astype(bf16)
 
 
-def signs(facts, change, own, column, experts):
-    count = change.shape[0]
-    col = lax.broadcasted_iota(i32, (count, experts * fold), 1) // fold
-    partner = facts[:, column : column + 1].astype(i32)
-    return jnp.where(col == own, change, 0.0) - jnp.where(col == partner, change, 0.0)
+def reverse(number, experts):
+    result, bits = number * 0, experts.bit_length() - 1
+    for bit in range(bits):
+        result = result | (((number >> bit) & 1) << (bits - 1 - bit))
+    return result
 
 
 def router_kernel(experts, own, cot, rows, sent, out, grad):
@@ -149,28 +146,26 @@
     extra = extra.reshape(experts, fold, 128)
     extra = jnp.broadcast_to(jnp.sum(extra, axis=1, keepdims=True), extra.shape)
     facts = cot[:, features + part :].astype(f32)
-    changes = []
+    me = own[0]
+    column = lax.broadcasted_iota(i32, (count, 128), 1)
+    lane = lax.broadcasted_iota(i32, (count, count), 1)
+    row = lax.broadcasted_iota(i32, (count, count), 0) % fold
+    lefts = []
     for k, value in enumerate((total, extra.reshape(count, 128))):
         inner = jnp.sum(value, axis=1, keepdims=True)
         change = inner * (facts[:, 3 * k + 1 : 3 * k + 2] + facts[:, 3 * k + 2 : 3 * k + 3])
-        changes.append(signs(facts, change, own[0], 3 * k, experts))
-    row = lax.broadcasted_iota(i32, (count, count), 0) % fold
-    lane = lax.broadcasted_iota(i32, (count, count), 1) % fold
-    result = jnp.zeros((count, part), f32)
-    for c in range(fold):
-        left = jnp.where(lane == c, changes[0], 0.0).astype(bf16)
-        result += dot(left, rows[:, c * part : (c + 1) * part], contract_first)
-        left = jnp.where((lane == c) & (row == c), changes[1], 0.0).astype(bf16)
-        result += dot(left, rows[:, features : features + part], contract_first)
-    out[...] = result.astype(bf16)
-    pick = lax.broadcasted_iota(i32, (count, 128), 0) == fold * lax.broadcasted_iota(
-        i32, (count, 128), 1
-    )
-    pick = pick.astype(f32).astype(bf16)
-    for k in range(2):
-        high = changes[k].astype(bf16)
-        low = (changes[k] - high.astype(f32)).astype(bf16)
-        grad[k] = dot(high, pick) + dot(low, pick)
+        partner = facts[:, 3 * k : 3 * k + 1].astype(i32)
+        grad[k] = jnp.where(column == me, change, 0.0) - jnp.where(column == partner, change, 0.0)
+        away = reverse(partner ^ me, experts)
+        at = column if k == 0 else lane % experts
+        left = jnp.where(at == 0, change, 0.0) - jnp.where(at == away, change, 0.0)
+        if k == 1:
+            left = jnp.where(lane // experts == row, left, 0.0)
+        lefts.append(left.astype(bf16))
+    ninth = dot(lefts[1], rows[:, features:], contract_first)
+    for c in range(fold):
+        piece = dot(lefts[0], rows[:, c * part : (c + 1) * part], contract_first)
+        out[:, c, :] = piece[:experts] + ninth[c * experts : (c + 1) * experts]
 
 
 def upper_kernel(upper, back, mix, out):
@@ -235,8 +230,7 @@
         result = dot(hidden[...], down[c * part : (c + 1) * part, :], contract_last)
         out[:, c * part : (c + 1) * part] = result[:main].astype(bf16)
         total += unfolded(result[main:].astype(bf16), c, experts)
-    out[:, features : features + part] = total.astype(bf16)
-    out[:, features + part :] = jnp.zeros((main, part), bf16)
+    out[:, features:] = total.astype(bf16)
 
 
 def halves(value):
@@ -250,44 +244,46 @@
     return dot((row == lane * fold + step).astype(f32).astype(bf16), extra)
 
 
-def rows_kernel(experts, joined, gate_up, grad, router, out, total):
+def rows_kernel(experts, joined, gate_up, grad, router, out, total, left):
     step = pl.program_id(0)
     main = experts * fold
 
     @pl.when(step == 0)
     def _():
         total[...] = jnp.zeros_like(total)
+        high, low = halves(grad[...].reshape(2 * main, grad.shape[2])[:, :experts])
+        left[...] = jnp.concatenate([high, low, high], axis=1)
 
     @pl.when(step < fold)
     def _():
         result = dot(joined[...], gate_up[...], contract_last)
-        left = grad[...].reshape(2 * main, grad.shape[2])[:, :experts]
-        left_high, left_low = halves(left)
-        right_high, right_low = halves(router[...])
-        change = dot(
-            jnp.concatenate([left_high, left_low, left_high], axis=1),
-            jnp.concatenate([right_high, right_high, right_low], axis=0),
-        )
+        high, low = halves(router[...])
+        change = dot(left[...], jnp.concatenate([high, high, low], axis=0))
         out[...] = (result[:main] + change[:main]).astype(bf16)
         own = lax.broadcasted_iota(i32, (main, out.shape[1]), 0) % fold == step
-        extra = result[main:]
-        total[...] += unfolded(jnp.concatenate(halves(extra), axis=0), step, experts)
-        total[...] += jnp.where(own, change[main:], 0.0)
+        extra = unfolded(jnp.concatenate(halves(result[main:]), axis=0), step, experts)
+        total[...] = jnp.where(own, extra + change[main:], total[...])
 
     @pl.when(step == fold)
     def _():
         out[...] = total[...].astype(bf16)
 
 
-def reduce_kernel(back, out):
-    folded = back[...].astype(f32).reshape(back.shape[0] // fold, *out.shape)
-    out[...] = jnp.sum(folded, axis=0)
+def add_kernel(*refs):
+    *parts, out = refs
+    out[...] = sum([ref[...] for ref in parts[1:]], parts[0][...])
+
+
+def split_kernel(both, gate_up, down):
+    wide = gate_up.shape[1]
+    gate_up[...] = both[:, :wide]
+    down[...] = both[:, wide:].astype(f32).T.astype(bf16)
 
 
 def order_kernel(experts, own, parts, out):
     part = parts.shape[2]
     for e in range(experts):
-        piece = parts[own[0] ^ e]
+        piece = parts[reverse(own[0] ^ e, experts)]
         for c in range(fold):
             out[e : e + 1, c * part : (c + 1) * part] = piece[c : c + 1]
 
@@ -304,6 +300,22 @@
         array.reshape(experts, fold, width), "expert", split_axis=0, concat_axis=0, tiled=True
     )
     return moved.reshape(experts * fold, width)
+
+
+def rounds(size):
+    result, bit = [], 1
+    while bit < size:
+        if 2 * bit < size:
+            result.append((2 * bit, bit, 3 * bit))
+            bit *= 4
+        else:
+            result.append((bit,))
+            bit *= 2
+    return result
+
+
+def swap(array, axis, flip):
+    return lax.ppermute(array, axis, [(i, i ^ flip) for i in range(lax.axis_size(axis))])
 
 
 def unpack(block, features, experts):
@@ -335,14 +347,16 @@
     def shape(*dims, kind=bf16):
         return jax.ShapeDtypeStruct(dims, kind)
 
-    weights = call(weights_kernel, shape(gate_up_weight.shape[1], 3 * hidden_units), 10**6)(
-        gate_up_weight[0], down_weight[0].T
-    )
+    weights, packed = call(
+        lambda *refs: send_rows_kernel(experts, *refs),
+        (
+            shape(gate_up_weight.shape[1], 3 * hidden_units),
+            shape(main, features + part),
+        ),
+        10**6,
+    )(ids, keep, lower_out, gate_up_weight[0], down_weight[0].T)
     weights = lax.all_gather(weights, "dp", axis=0, tiled=True)
     gate_up, down = weights[:, : 2 * hidden_units], weights[:, 2 * hidden_units :]
-    packed = call(
-        lambda *refs: send_rows_kernel(experts, *refs), shape(main, features + part), 10**6
-    )(ids, keep, lower_out)
     arrived = exchange(packed, experts)
     cot_packed, mix, used = call(
         lambda *refs: send_cot_kernel(experts, *refs),
@@ -366,33 +380,12 @@
     slots = main + experts
     out_packed = call(
         lambda *refs: outputs_kernel(experts, *refs),
-        shape(main, features + 2 * part),
+        shape(main, features + part),
         10**6,
     )(hidden, down)
 
     own = lax.axis_index("expert").astype(i32).reshape(1)
-    block = pl.BlockSpec((main, part), lambda i: (0, fold + 1))
-    out_packed, logit_grad = call(
-        lambda own, cot, rows, sent, out, grad: router_kernel(
-            experts, own, cot, rows, sent, out, grad
-        ),
-        (shape(main, features + 2 * part), shape(2, main, 128, kind=f32)),
-        10**6,
-        aliases={3: 0},
-        grid=(1,),
-        in_specs=[
-            scalar,
-            whole,
-            whole,
-            pl.BlockSpec((main, features + 2 * part), lambda i: (0, 0)),
-        ],
-        out_specs=(block, pl.BlockSpec((2, main, 128), lambda i: (0, 0, 0))),
-    )(own, cot_arrived, arrived, out_packed)
-    out_packed, cot_arrived, hidden, row_block, logit_grad = lax.optimization_barrier(
-        (out_packed, cot_arrived, hidden, row_block, logit_grad)
-    )
     out_back = exchange(out_packed, experts)
-
     joined, grads = call(
         lambda *refs: hidden_kernel(experts, *refs),
         (shape(slots, 2 * hidden_units), shape(slots, features)),
@@ -411,6 +404,14 @@
         ],
         out_specs=pl.BlockSpec((part, 3 * hidden_units), lambda i: (i, 0)),
     )(row_block, joined, grads, hidden)
+    both, cot_arrived = lax.optimization_barrier((both, cot_arrived))
+    router_part, logit_grad = call(
+        lambda *refs: router_kernel(experts, *refs),
+        (shape(experts, fold, part, kind=f32), shape(2, main, 128, kind=f32)),
+        10**6,
+        in_specs=[scalar, whole, whole, whole],
+        out_specs=(whole, whole),
+    )(own, cot_arrived, arrived, out_packed)
     both = lax.psum_scatter(both, "dp", scatter_dimension=0, tiled=True)
     rows_packed = call(
         lambda *refs: rows_kernel(experts, *refs),
@@ -424,33 +425,34 @@
             pl.BlockSpec((experts, part), lambda i: (0, jnp.minimum(i, fold - 1))),
         ],
         out_specs=pl.BlockSpec((main, part), lambda i: (0, i)),
-        scratch_shapes=[pltpu.VMEM((main, part), f32)],
+        scratch_shapes=[
+            pltpu.VMEM((main, part), f32),
+            pltpu.VMEM((2 * main, 3 * experts), bf16),
+        ],
     )(joined, weights, logit_grad, router)
-    router_row = call(
-        reduce_kernel,
-        shape(fold, part, kind=f32),
-        3 * 10**11,
-        grid=(1,),
-        in_specs=[pl.BlockSpec((main, part), lambda i: (0, fold + 1))],
-        out_specs=pl.BlockSpec((fold, part), lambda i: (0, 0)),
-    )(out_back)
-    rows_packed, router_row = lax.optimization_barrier((rows_packed, router_row))
-    rows_back = exchange(rows_packed, experts)
-    step, copies = 1, lax.axis_size("dp")
-    while step < copies:
-        pairs = [(d, d ^ step) for d in range(copies)]
-        router_row = router_row + lax.ppermute(router_row, "dp", pairs)
-        step *= 2
+    for count, flips in enumerate(rounds(experts)):
+        piece = router_part.shape[0] // (len(flips) + 1)
+        parts = [router_part[:piece]]
+        for place, flip in enumerate(flips, 1):
+            parts.append(swap(router_part[place * piece : (place + 1) * piece], "expert", flip))
+        if count == 0:
+            *parts, out_back = lax.optimization_barrier((*parts, out_back))
+            router_part = call(add_kernel, shape(piece, fold, part, kind=f32), 149500 * 10**6)(*parts)
+            rows_packed, router_part = lax.optimization_barrier((rows_packed, router_part))
+            rows_back = exchange(rows_packed, experts)
+        else:
+            router_part = sum(parts[1:], parts[0])
+    copies = lax.axis_size("dp")
+    flips = [1] + [flip for flip in range(2, copies, 2)]
+    router_part = router_part + (swap(router_part, "dp", 1) if copies > 1 else 0.0)
+    parts = [swap(router_part, "dp", flip) for flip in flips[1:]]
+    router_all = sum(parts, router_part)
     upper_input = call(upper_kernel, shape(tokens, features, kind=f32), 10**6)(
         upper_out, out_back, mix
     )
-    router_all = router_row[None]
-    step = 1
-    while step < experts:
-        pairs = [(e, e ^ step) for e in range(experts)]
-        theirs = lax.ppermute(router_all, "expert", pairs)
-        router_all = jnp.concatenate([router_all, theirs], axis=0)
-        step *= 2
+    for flips in reversed(rounds(experts)):
+        parts = [swap(router_all, "expert", flip) for flip in flips]
+        router_all = jnp.concatenate([router_all, *parts], axis=0)
     router_grad = call(
         lambda own, parts, out: order_kernel(experts, own, parts, out),
         shape(experts, features, kind=f32),
@@ -461,13 +463,13 @@
     lower_grad = call(lower_kernel, shape(tokens, features, kind=f32), 10**6)(
         lower_cot, rows_back, used
     )
-    return (
-        upper_input,
-        lower_grad,
-        both[None, :, : 2 * hidden_units],
-        both[None, :, 2 * hidden_units :],
-        router_grad,
-    )
+    lower_grad, both = lax.optimization_barrier((lower_grad, both))
+    gate_up_grad, down_grad = call(
+        split_kernel,
+        (shape(both.shape[0], 2 * hidden_units), shape(hidden_units, both.shape[0])),
+        10**6,
+    )(both)
+    return upper_input, lower_grad, gate_up_grad[None], down_grad.T[None], router_grad
 
 
 def solution(mesh):

time: 196 us -> 221 us (1.13)
  starting transfers between devices: 42.3 us -> 63 us
  waiting for transfers between devices: 76.5 us -> 82.2 us
  Pallas kernels: 40.1 us -> 37.5 us
    ppermute x8 -> x18, starting transfers between devices: 12.5 us -> 28.6 us  [swap(): lax.ppermute(array, axis, [(i, i ^ flip) for i in range(lax.axis_size(axi...]
    ppermute x8 -> x18, waiting for transfers between devices: 25.1 us -> 38.4 us  [swap(): lax.ppermute(array, axis, [(i, i ^ flip) for i in range(lax.axis_size(axi...]
    all_to_all x4, waiting for transfers between devices: 47.6 us -> 37 us  [exchange(): lax.all_to_all(array.reshape(experts, fold, width), 'expert', split_axis=...]
    all_to_all x4, starting transfers between devices: 29.5 us -> 34.3 us  [exchange(): lax.all_to_all(array.reshape(experts, fold, width), 'expert', split_axis=...]
    all_gather x1, waiting for transfers between devices: 3.81 us -> 6.82 us  [body(): weights = lax.all_gather(weights, 'dp', axis=0, tiled=True)]
    unnamed x49 -> x50, local copies, waits for them, and re-layouts: 6.63 us -> 9.29 us
  transfers between devices with their start and end apart: 14 -> 24, of which waited for: 12 -> 12; matrix products, arithmetic and copies ran while one was open for 6% -> 5% of each run, Pallas kernels for 18% -> 16%
where the time goes in v4:
time: 221 us; the launch traced here: 218 us
  waiting for transfers between devices  82.2 us (37%)
  starting transfers between devices  63 us (29%)
  Pallas kernels  37.5 us (17%)
  between operations  14.4 us (7%)
  local copies, waits for them, and re-layouts  13.8 us (6%)
  matrix products  5.75 us (3%)
    ppermute x18, waiting for transfers between devices, swap(): lax.ppermute(array, axis, [(i, i ^ flip) for i in range(lax.axis_size(axi...  38.4 us
    all_to_all x4, waiting for transfers between devices, exchange(): lax.all_to_all(array.reshape(experts, fold, width), 'expert', split_axis=...  37 us
    all_to_all x4, starting transfers between devices, exchange(): lax.all_to_all(array.reshape(experts, fold, width), 'expert', split_axis=...  34.3 us
    ppermute x18, starting transfers between devices, swap(): lax.ppermute(array, axis, [(i, i ^ flip) for i in range(lax.axis_size(axi...  28.6 us
    unnamed x50, local copies, waits for them, and re-layouts  9.29 us
    pallas_call x1, Pallas kernels, body(): call(lambda *refs: rows_kernel(experts, *refs), shape(main, features + pa...  9.05 us
    pallas_call x1, Pallas kernels, body(): call(grads_kernel, shape(features, 3 * hidden_units), 10 ** 6, grid=(fold...  8.43 us
    all_gather x1, waiting for transfers between devices, body(): weights = lax.all_gather(weights, 'dp', axis=0, tiled=True)  6.82 us
  transfers between devices with their start and end apart: 24, of which 12 were waited for; matrix products, arithmetic and copies ran while one was open for 5% of the time, Pallas kernels for 16%

profile of v4, /device:TPU:2, one launch (start us, length us, event | category | flops | bytes accessed | tf_op | source)
XLA Modules:
  0.0 218.4 jit_solution(1094865524944495723)
XLA Ops:
  7.2 1.1 copy-done.5
  8.3 1.0 copy-done.6
  9.4 1.0 copy-done.9
  11.7 2.2 %shard_map.129 = (bf16[256,2112]{1,0:T(8,128)(2,1)}, bf16[256,2304]{1,0:T(8,128)(2,1)}) custom-call(s32[2,128]{1,0:T(2,128)S(1)} %bitcast.27, s32[2,128]{1,0:T(2,128)S(1)} %bitcast.29, bf16[128,2048]{1,0:T(8,128)(2,1)S(1)} %copy-done.6, bf16[256,1408]{1,0:T(8,128)(2,1)S(1)} %bitcast.23, bf16[704,256]{1,0:T(8,128)(2,1)S(1)} %bitcast.24), custom_call_target="tpu_custom_call" | custom-call | flops 1000000 | tf_op jit(solution)/shard_map/pallas_call | solution.py:350
  14.0 11.8 %all-to-all-start = ((bf16[32,8,2304]{2,1,0:T(8,128)(2,1)}), bf16[32,8,2304]{2,1,0:T(8,128)(2,1)}, u32[]{:S(2)}, u32[]{:S(2)}) async-start(bf16[32,8,2304]{2,1,0:T(8,128)(2,1)} %bitcast.7), calls=%async_computation | async-start | bytes 2359296 | tf_op jit(solution)/shard_map/all_to_all | solution.py:299
  25.9 3.0 %shard_map.128 = (bf16[256,2432]{1,0:T(8,128)(2,1)}, bf16[128,1024]{1,0:T(8,128)(2,1)S(1)}, bf16[128,512]{1,0:T(8,128)(2,1)S(1)}) custom-call(s32[2,128]{1,0:T(2,128)S(1)} %bitcast.28, s32[2,128]{1,0:T(2,128)S(1)} %bitcast.30, bf16[128,2048]{1,0:T(8,128)(2,1)S(1)} %copy-done.7, bf16[128,2048]{1,0:T(8,128)(2,1)S(1)} %copy-done.19, f32[32,2048]{1,0:T(8,128)S(1)} %bitcast.25), custom_call_target="tpu_custom_call" | custom-call | flops 299999985664 | tf_op jit(solution)/shard_map/pallas_call | solution.py:361
  30.2 26.6 %all-to-all-done = bf16[32,8,2304]{2,1,0:T(8,128)(2,1)} async-done(((bf16[32,8,2304]{2,1,0:T(8,128)(2,1)}), bf16[32,8,2304]{2,1,0:T(8,128)(2,1)}, u32[]{:S(2)}, u32[]{:S(2)}) %all-to-all-start) | async-done | bytes 1179680 | tf_op jit(solution)/shard_map/all_to_all | solution.py:299
  56.8 5.6 %all-to-all-start.1 = ((bf16[32,8,2432]{2,1,0:T(8,128)(2,1)}), bf16[32,8,2432]{2,1,0:T(8,128)(2,1)}, u32[]{:S(2)}, u32[]{:S(2)}) async-start(bf16[32,8,2432]{2,1,0:T(8,128)(2,1)} %bitcast.9), calls=%async_computation.1 | async-start | bytes 2490368 | tf_op jit(solution)/shard_map/all_to_all | solution.py:299
  62.4 0.9 slice.49
  63.3 1.3 slice.48
  64.7 6.8 %all-gather.2.cloned.1.call-done.refs_1_ = bf16[2048,2112]{1,0:T(8,128)(2,1)} async-done(((bf16[256,2112]{1,0:T(8,128)(2,1)}), bf16[2048,2112]{1,0:T(8,128)(2,1)}) %all-gather.2.cloned.1.call-update) | async-done | bytes 8650768 | tf_op jit(solution)/shard_map/all_gather | solution.py:358
  71.5 2.1 slice.65.refs_2_.refs_1_
  73.7 5.8 %fusion.refs_1_ = f32[288,1408]{1,0:T(8,128)S(1)} fusion(bf16[2048,2112]{1,0:T(8,128)(2,1)} %all-gather.2.cloned.1.call-done.refs_1_, bf16[32,2048]{1,0:T(8,128)(2,1)S(1)} %reshape.43, bf16[256,2048]{1,0:T(8,128)(2,1)S(1)} %slice.48), kind=kOutput, calls=%fused_computation | convolution fusion | flops 1663303680 | bytes 8568832 | tf_op jit(solution)/shard_map/dot_general | solution.py:374
  79.8 2.9 %shard_map.132.refs_3_ = bf16[256,2304]{1,0:T(8,128)(2,1)} custom-call(bf16[288,704]{1,0:T(8,128)(2,1)S(1)} %fusion.2.hidden.refs_0_, bf16[2048,704]{1,0:T(8,128)(2,1)S(1)} %slice.65.refs_2_.refs_1_), custom_call_target="tpu_custom_call" | custom-call | flops 1000000 | tf_op jit(solution)/shard_map/pallas_call | solution.py:381
  82.7 10.4 %all-to-all-done.1 = bf16[32,8,2432]{2,1,0:T(8,128)(2,1)} async-done(((bf16[32,8,2432]{2,1,0:T(8,128)(2,1)}), bf16[32,8,2432]{2,1,0:T(8,128)(2,1)}, u32[]{:S(2)}, u32[]{:S(2)}) %all-to-all-start.1) | async-done | bytes 1245216 | tf_op jit(solution)/shard_map/all_to_all | solution.py:299
  93.1 6.0 %all-to-all-start.2 = ((bf16[32,8,2304]{2,1,0:T(8,128)(2,1)}), bf16[32,8,2304]{2,1,0:T(8,128)(2,1)S(1)}, u32[]{:S(2)}, u32[]{:S(2)}) async-start(bf16[32,8,2304]{2,1,0:T(8,128)(2,1)} %bitcast.11), calls=%async_computation.2 | async-start | bytes 2359296 | tf_op jit(solution)/shard_map/all_to_all | solution.py:299
  99.1 1.4 pad_maximum_fusion.rows
  100.6 3.6 %shard_map.130 = (bf16[288,1408]{1,0:T(8,128)(2,1)S(1)}, bf16[288,2048]{1,0:T(8,128)(2,1)S(1)}) custom-call(bf16[256,2432]{1,0:T(8,128)(2,1)} %bitcast.10.refs_0_.refs_1_, f32[288,1408]{1,0:T(8,128)S(1)} %fusion.refs_1_, bf16[2048,704]{1,0:T(8,128)(2,1)} %copy-done), custom_call_target="tpu_custom_call" | custom-call | flops 1000000 | tf_op jit(solution)/shard_map/pallas_call | solution.py:389
  104.2 8.4 %shard_map.131 = bf16[2048,2112]{1,0:T(8,128)(2,1)} custom-call(bf16[288,2048]{1,0:T(8,128)(2,1)S(1)} %pad_maximum_fusion.rows, bf16[288,1408]{1,0:T(8,128)(2,1)S(1)} %get-tuple-element.34.joined.refs_0_, bf16[288,2048]{1,0:T(8,128)(2,1)S(1)} %get-tuple-element.35.cot, bf16[288,704]{1,0:T(8,128)(2,1)S(1)} %fusion.2.hidden.refs_0_), custom_call_target="tpu_custom_call" | custom-call | flops 1000000 | tf_op jit(solution)/shard_map/pallas_call | solution.py:394
  112.6 0.9 copy-done.1
  113.6 3.2 %shard_map.133 = (f32[32,8,256]{2,1,0:T(8,128)S(1)}, f32[2,256,128]{2,1,0:T(8,128)S(1)}) custom-call(s32[1]{0:T(128)} %bitcast.refs_0_.own, bf16[256,2432]{1,0:T(8,128)(2,1)} %bitcast.10.refs_0_.refs_1_, bf16[256,2304]{1,0:T(8,128)(2,1)} %bitcast.8.refs_2_, bf16[256,2304]{1,0:T(8,128)(2,1)} %shard_map.132.refs_3_), custom_call_target="tpu_custom_call" | custom-call | flops 1000000 | tf_op jit(solution)/shard_map/pallas_call | solution.py:408
  116.8 1.5 collective-permute-start.2
  118.3 1.8 collective-permute-start.1
  120.4 9.1 %shard_map.135 = bf16[256,2304]{1,0:T(8,128)(2,1)} custom-call(bf16[288,1408]{1,0:T(8,128)(2,1)S(1)} %copy-done.2, bf16[2048,2112]{1,0:T(8,128)(2,1)} %all-gather.2.cloned.1.call-done.refs_1_, f32[2,256,128]{2,1,0:T(8,128)S(1)} %get-tuple-element.40.refs_2_, f32[32,2048]{1,0:T(8,128)S(1)} %bitcast.26), custom_call_target="tpu_custom_call" | custom-call | flops 1000000 | tf_op jit(solution)/shard_map/pallas_call | solution.py:416
  129.5 10.9 %all-to-all-start.3 = ((bf16[32,8,2304]{2,1,0:T(8,128)(2,1)}), bf16[32,8,2304]{2,1,0:T(8,128)(2,1)S(1)}, u32[]{:S(2)}, u32[]{:S(2)}) async-start(bf16[32,8,2304]{2,1,0:T(8,128)(2,1)} %bitcast.13), calls=%async_computation.3 | async-start | bytes 2359296 | tf_op jit(solution)/shard_map/all_to_all | solution.py:299
  140.4 2.5 %collective-permute-start.3 = (f32[2,8,256]{2,1,0:T(8,128)S(1)}, f32[2,8,256]{2,1,0:T(8,128)S(1)}, u32[]{:S(2)}, u32[]{:S(2)}) collective-permute-start(f32[2,8,256]{2,1,0:T(8,128)S(1)} %get-tuple-element.59), channel_id=1, source_target_pairs={{0,64},{8,72},{16,80},{24,88},{32,96},{40,104},{48,112},{56,120},{... | collective-permute-start | bytes 49160 | tf_op jit(solution)/shard_map/ppermute | solution.py:318
  142.9 1.5 collective-permute-start.5
  144.4 20.0 %collective-permute-done.3 = f32[2,8,256]{2,1,0:T(8,128)S(1)} collective-permute-done((f32[2,8,256]{2,1,0:T(8,128)S(1)}, f32[2,8,256]{2,1,0:T(8,128)S(1)}, u32[]{:S(2)}, u32[]{:S(2)}) %collective-permute-start.3) | collective-permute-done | bytes 16416 | tf_op jit(solution)/shard_map/ppermute | solution.py:318
  164.4 1.7 collective-permute-done.5
  166.1 3.9 %collective-permute-start.6 = (f32[1,8,256]{2,1,0:T(8,128)S(1)}, f32[1,8,256]{2,1,0:T(8,128)S(1)}, u32[]{:S(2)}, u32[]{:S(2)}) collective-permute-start(f32[1,8,256]{2,1,0:T(8,128)S(1)} %slice.69), channel_id=1, source_target_pairs={{0,128},{8,136},{16,144},{24,152},{32,160},{40,168},{48,176},{56,1... | collective-permute-start | bytes 24584 | tf_op jit(solution)/shard_map/ppermute | solution.py:318
  170.1 3.7 %collective-permute-done.6 = f32[1,8,256]{2,1,0:T(8,128)S(1)} collective-permute-done((f32[1,8,256]{2,1,0:T(8,128)S(1)}, f32[1,8,256]{2,1,0:T(8,128)S(1)}, u32[]{:S(2)}, u32[]{:S(2)}) %collective-permute-start.6) | collective-permute-done | bytes 8224 | tf_op jit(solution)/shard_map/ppermute | solution.py:318
  173.8 1.2 collective-permute-done.7
  175.0 3.0 %collective-permute-start.10 = (f32[1,8,256]{2,1,0:T(8,128)S(1)}, f32[1,8,256]{2,1,0:T(8,128)S(1)}, u32[]{:S(2)}, u32[]{:S(2)}) collective-permute-start(f32[1,8,256]{2,1,0:T(8,128)S(1)} %add.34), channel_id=1, source_target_pairs={{0,6},{1,7},{2,4},{3,5},{4,2},{5,3},{6,0},{7,1},{8,14},{9,15},{10,... | collective-permute-start | bytes 24584 | tf_op jit(solution)/shard_map/ppermute | solution.py:318
  179.8 3.3 %collective-permute-done.9 = f32[1,8,256]{2,1,0:T(8,128)S(1)} collective-permute-done((f32[1,8,256]{2,1,0:T(8,128)S(1)}, f32[1,8,256]{2,1,0:T(8,128)S(1)}, u32[]{:S(2)}, u32[]{:S(2)}) %collective-permute-start.9) | collective-permute-done | bytes 8224 | tf_op jit(solution)/shard_map/ppermute | solution.py:318
  183.1 3.9 %collective-permute-start.11 = (f32[1,8,256]{2,1,0:T(8,128)S(1)}, f32[1,8,256]{2,1,0:T(8,128)S(1)}, u32[]{:S(2)}, u32[]{:S(2)}) collective-permute-start(f32[1,8,256]{2,1,0:T(8,128)S(1)} %get-tuple-element.54), channel_id=1, source_target_pairs={{0,128},{8,136},{16,144},{24,152},{32,160},{40,168},{48,176},{56,1... | collective-permute-start | bytes 24584 | tf_op jit(solution)/shard_map/ppermute | solution.py:318
  187.0 3.7 %collective-permute-done.11 = f32[1,8,256]{2,1,0:T(8,128)S(1)} collective-permute-done((f32[1,8,256]{2,1,0:T(8,128)S(1)}, f32[1,8,256]{2,1,0:T(8,128)S(1)}, u32[]{:S(2)}, u32[]{:S(2)}) %collective-permute-start.11) | collective-permute-done | bytes 8224 | tf_op jit(solution)/shard_map/ppermute | solution.py:318
  190.7 1.5 collective-permute-start.14
  192.2 2.9 %collective-permute-start.12 = (f32[2,8,256]{2,1,0:T(8,128)S(1)}, f32[2,8,256]{2,1,0:T(8,128)S(1)}, u32[]{:S(2)}, u32[]{:S(2)}) collective-permute-start(f32[2,8,256]{2,1,0:T(8,128)S(1)} %pad_maximum_fusion.1), channel_id=1, source_target_pairs={{0,64},{8,72},{16,80},{24,88},{32,96},{40,104},{48,112},{56,120},{... | collective-permute-start | bytes 49160 | tf_op jit(solution)/shard_map/ppermute | solution.py:318
  195.1 1.7 collective-permute-done.12
  196.9 2.4 %collective-permute-start.15 = (f32[8,8,256]{2,1,0:T(8,128)S(1)}, f32[8,8,256]{2,1,0:T(8,128)S(1)}, u32[]{:S(2)}, u32[]{:S(2)}) collective-permute-start(f32[8,8,256]{2,1,0:T(8,128)S(1)} %get-tuple-element.62), channel_id=1, source_target_pairs={{0,16},{8,24},{16,0},{24,8},{32,48},{40,56},{48,32},{56,40},{64,80... | collective-permute-start | bytes 196616 | tf_op jit(solution)/shard_map/ppermute | solution.py:318
  199.3 1.2 copy-done.4
  200.5 1.7 shard_map.134
  202.2 2.4 %collective-permute-start.16 = (f32[8,8,256]{2,1,0:T(8,128)S(1)}, f32[8,8,256]{2,1,0:T(8,128)S(1)}, u32[]{:S(2)}, u32[]{:S(2)}) collective-permute-start(f32[8,8,256]{2,1,0:T(8,128)S(1)} %get-tuple-element.62), channel_id=1, source_target_pairs={{0,8},{8,0},{16,24},{24,16},{32,40},{40,32},{48,56},{56,48},{64,72... | collective-permute-start | bytes 196616 | tf_op jit(solution)/shard_map/ppermute | solution.py:318
  204.6 2.2 %collective-permute-done.16 = f32[8,8,256]{2,1,0:T(8,128)S(1)} collective-permute-done((f32[8,8,256]{2,1,0:T(8,128)S(1)}, f32[8,8,256]{2,1,0:T(8,128)S(1)}, u32[]{:S(2)}, u32[]{:S(2)}) %collective-permute-start.16) | collective-permute-done | bytes 65568 | tf_op jit(solution)/shard_map/ppermute | solution.py:318
  206.9 0.9 shard_map.139
  207.8 1.4 shard_map.137
  209.2 1.2 copy-done.3
  210.5 1.1 shard_map.138
  (81 shorter events, 5.6 us)
Async XLA Ops:
  7.2 64.4 %all-gather.2.cloned.1.call-start = ((), (), s32[]{:S(2)}) async-start(), calls=%async_computation.5 | async-start | bytes 10027008 | tf_op jit(solution)/shard_map/all_gather | solution.py:358
  7.2 1.1 copy-start.5
  8.3 1.0 copy-start.6
  9.4 1.0 copy-start.9
  10.3 0.7 copy-start.15
  11.0 0.7 copy-start.17
  13.9 11.9 %copy-start.7 = (bf16[128,2048]{1,0:T(8,128)(2,1)S(1)}, bf16[128,2048]{1,0:T(8,128)(2,1)}, u32[]{:S(2)}) copy-start(bf16[128,2048]{1,0:T(8,128)(2,1)} %refs_2_.3) | copy-start | bytes 1572868
  14.0 11.9 %copy-start.10 = (f32[2048,32]{0,1:T(8,128)S(1)}, f32[2048,32]{0,1:T(8,128)}, u32[]{:S(2)}) copy-start(f32[2048,32]{0,1:T(8,128)} %param.15) | copy-start | bytes 786436
  14.0 11.9 %copy-start.16 = (s32[128,2]{0,1:T(2,128)S(1)}, s32[128,2]{0,1:T(2,128)}, u32[]{:S(2)}) copy-start(s32[128,2]{0,1:T(2,128)} %param.16) | copy-start | bytes 3076
  14.0 11.9 %copy-start.18 = (s32[128,2]{0,1:T(2,128)S(1)}, s32[128,2]{0,1:T(2,128)}, u32[]{:S(2)}) copy-start(s32[128,2]{0,1:T(2,128)} %param.17) | copy-start | bytes 3076
  14.0 11.9 %copy-start.19 = (bf16[128,2048]{1,0:T(8,128)(2,1)S(1)}, bf16[128,2048]{1,0:T(8,128)(2,1)}, u32[]{:S(2)}) copy-start(bf16[128,2048]{1,0:T(8,128)(2,1)} %refs_3_.1) | copy-start | bytes 1572868
  14.0 42.7 %all-to-all-start = ((bf16[32,8,2304]{2,1,0:T(8,128)(2,1)}), bf16[32,8,2304]{2,1,0:T(8,128)(2,1)}, u32[]{:S(2)}, u32[]{:S(2)}) async-start(bf16[32,8,2304]{2,1,0:T(8,128)(2,1)} %bitcast.7), calls=%async_computation | async-start | bytes 2359296 | tf_op jit(solution)/shard_map/all_to_all | solution.py:299
  28.8 0.7 copy-start.11
  29.5 0.7 copy-start.13
  56.8 36.3 %all-to-all-start.1 = ((bf16[32,8,2432]{2,1,0:T(8,128)(2,1)}), bf16[32,8,2432]{2,1,0:T(8,128)(2,1)}, u32[]{:S(2)}, u32[]{:S(2)}) async-start(bf16[32,8,2432]{2,1,0:T(8,128)(2,1)} %bitcast.9), calls=%async_computation.1 | async-start | bytes 2490368 | tf_op jit(solution)/shard_map/all_to_all | solution.py:299
  64.6 9.1 %copy-start.20 = (bf16[256,2048]{1,0:T(8,128)(2,1)}, bf16[256,2048]{1,0:T(8,128)(2,1)S(1)}, u32[]{:S(2)}) copy-start(bf16[256,2048]{1,0:T(8,128)(2,1)S(1)} %slice.48) | copy-start | bytes 3145732
  64.7 9.0 %copy-start.21 = (bf16[32,2048]{1,0:T(8,128)(2,1)}, bf16[32,2048]{1,0:T(8,128)(2,1)S(1)}, u32[]{:S(2)}) copy-start(bf16[32,2048]{1,0:T(8,128)(2,1)S(1)} %reshape.43) | copy-start | bytes 393220
  73.7 6.1 %copy-start = (bf16[2048,704]{1,0:T(8,128)(2,1)}, bf16[2048,704]{1,0:T(8,128)(2,1)S(1)}, u32[]{:S(2)}) copy-start(bf16[2048,704]{1,0:T(8,128)(2,1)S(1)} %slice.65.refs_2_.refs_1_) | copy-start | bytes 8650756
  93.1 36.3 %all-to-all-start.2 = ((bf16[32,8,2304]{2,1,0:T(8,128)(2,1)}), bf16[32,8,2304]{2,1,0:T(8,128)(2,1)S(1)}, u32[]{:S(2)}, u32[]{:S(2)}) async-start(bf16[32,8,2304]{2,1,0:T(8,128)(2,1)} %bitcast.11), calls=%async_computation.2 | async-start | bytes 2359296 | tf_op jit(solution)/shard_map/all_to_all | solution.py:299
  99.1 110.1 %reduce-scatter.2.cloned.1.call-start = ((), (), s32[]{:S(2)}) async-start(), calls=%async_computation.6 | async-start | bytes 10027008 | tf_op jit(solution)/shard_map/reduce_scatter | solution.py:415
  112.6 0.9 copy-start.1
  113.6 6.8 %copy-start.2 = (bf16[288,1408]{1,0:T(8,128)(2,1)S(1)}, bf16[288,1408]{1,0:T(8,128)(2,1)}, u32[]{:S(2)}) copy-start(bf16[288,1408]{1,0:T(8,128)(2,1)} %copy-done.1) | copy-start | bytes 2433028
  116.8 12.6 %collective-permute-start.2 = (f32[8,8,256]{2,1,0:T(8,128)S(1)}, f32[8,8,256]{2,1,0:T(8,128)S(1)}, u32[]{:S(2)}, u32[]{:S(2)}) collective-permute-start(f32[8,8,256]{2,1,0:T(8,128)S(1)} %get-tuple-element.55), channel_id=1, source_target_pairs={{0,24},{8,16},{16,8},{24,0},{32,56},{40,48},{48,40},{56,32},{64,88... | collective-permute-start | bytes 196616 | tf_op jit(solution)/shard_map/ppermute | solution.py:318
  118.3 11.1 %collective-permute-start.1 = (f32[8,8,256]{2,1,0:T(8,128)S(1)}, f32[8,8,256]{2,1,0:T(8,128)S(1)}, u32[]{:S(2)}, u32[]{:S(2)}) collective-permute-start(f32[8,8,256]{2,1,0:T(8,128)S(1)} %get-tuple-element.56), channel_id=1, source_target_pairs={{0,8},{8,0},{16,24},{24,16},{32,40},{40,32},{48,56},{56,48},{64,72... | collective-permute-start | bytes 196616 | tf_op jit(solution)/shard_map/ppermute | solution.py:318
  120.1 9.3 %collective-permute-start = (f32[8,8,256]{2,1,0:T(8,128)S(1)}, f32[8,8,256]{2,1,0:T(8,128)S(1)}, u32[]{:S(2)}, u32[]{:S(2)}) collective-permute-start(f32[8,8,256]{2,1,0:T(8,128)S(1)} %get-tuple-element.57), channel_id=1, source_target_pairs={{0,16},{8,24},{16,0},{24,8},{32,48},{40,56},{48,32},{56,40},{64,80... | collective-permute-start | bytes 196616 | tf_op jit(solution)/shard_map/ppermute | solution.py:318
  129.5 69.8 %copy-start.12 = (bf16[128,1024]{1,0:T(8,128)(2,1)S(1)}, bf16[128,1024]{1,0:T(8,128)(2,1)}, u32[]{:S(2)}) copy-start(bf16[128,1024]{1,0:T(8,128)(2,1)} %copy-done.11) | copy-start | bytes 786436
  129.5 78.3 %all-to-all-start.3 = ((bf16[32,8,2304]{2,1,0:T(8,128)(2,1)}), bf16[32,8,2304]{2,1,0:T(8,128)(2,1)S(1)}, u32[]{:S(2)}, u32[]{:S(2)}) async-start(bf16[32,8,2304]{2,1,0:T(8,128)(2,1)} %bitcast.13), calls=%async_computation.3 | async-start | bytes 2359296 | tf_op jit(solution)/shard_map/all_to_all | solution.py:299
  140.4 23.9 %collective-permute-start.3 = (f32[2,8,256]{2,1,0:T(8,128)S(1)}, f32[2,8,256]{2,1,0:T(8,128)S(1)}, u32[]{:S(2)}, u32[]{:S(2)}) collective-permute-start(f32[2,8,256]{2,1,0:T(8,128)S(1)} %get-tuple-element.59), channel_id=1, source_target_pairs={{0,64},{8,72},{16,80},{24,88},{32,96},{40,104},{48,112},{56,120},{... | collective-permute-start | bytes 49160 | tf_op jit(solution)/shard_map/ppermute | solution.py:318
  142.9 23.2 %collective-permute-start.5 = (f32[2,8,256]{2,1,0:T(8,128)S(1)}, f32[2,8,256]{2,1,0:T(8,128)S(1)}, u32[]{:S(2)}, u32[]{:S(2)}) collective-permute-start(f32[2,8,256]{2,1,0:T(8,128)S(1)} %get-tuple-element.60), channel_id=1, source_target_pairs={{0,96},{8,104},{16,112},{24,120},{32,64},{40,72},{48,80},{56,88},{... | collective-permute-start | bytes 49160 | tf_op jit(solution)/shard_map/ppermute | solution.py:318
  144.3 21.8 %collective-permute-start.4 = (f32[2,8,256]{2,1,0:T(8,128)S(1)}, f32[2,8,256]{2,1,0:T(8,128)S(1)}, u32[]{:S(2)}, u32[]{:S(2)}) collective-permute-start(f32[2,8,256]{2,1,0:T(8,128)S(1)} %get-tuple-element.61), channel_id=1, source_target_pairs={{0,32},{8,40},{16,48},{24,56},{32,0},{40,8},{48,16},{56,24},{64,96... | collective-permute-start | bytes 49160 | tf_op jit(solution)/shard_map/ppermute | solution.py:318
  166.1 7.6 %collective-permute-start.6 = (f32[1,8,256]{2,1,0:T(8,128)S(1)}, f32[1,8,256]{2,1,0:T(8,128)S(1)}, u32[]{:S(2)}, u32[]{:S(2)}) collective-permute-start(f32[1,8,256]{2,1,0:T(8,128)S(1)} %slice.69), channel_id=1, source_target_pairs={{0,128},{8,136},{16,144},{24,152},{32,160},{40,168},{48,176},{56,1... | collective-permute-start | bytes 24584 | tf_op jit(solution)/shard_map/ppermute | solution.py:318
  173.8 1.2 collective-permute-start.7
  175.0 4.9 %collective-permute-start.10 = (f32[1,8,256]{2,1,0:T(8,128)S(1)}, f32[1,8,256]{2,1,0:T(8,128)S(1)}, u32[]{:S(2)}, u32[]{:S(2)}) collective-permute-start(f32[1,8,256]{2,1,0:T(8,128)S(1)} %add.34), channel_id=1, source_target_pairs={{0,6},{1,7},{2,4},{3,5},{4,2},{5,3},{6,0},{7,1},{8,14},{9,15},{10,... | collective-permute-start | bytes 24584 | tf_op jit(solution)/shard_map/ppermute | solution.py:318
  177.9 5.2 %collective-permute-start.9 = (f32[1,8,256]{2,1,0:T(8,128)S(1)}, f32[1,8,256]{2,1,0:T(8,128)S(1)}, u32[]{:S(2)}, u32[]{:S(2)}) collective-permute-start(f32[1,8,256]{2,1,0:T(8,128)S(1)} %add.34), channel_id=1, source_target_pairs={{0,4},{1,5},{2,6},{3,7},{4,0},{5,1},{6,2},{7,3},{8,12},{9,13},{10,... | collective-permute-start | bytes 24584 | tf_op jit(solution)/shard_map/ppermute | solution.py:318
  178.5 4.5 %collective-permute-start.8 = (f32[1,8,256]{2,1,0:T(8,128)S(1)}, f32[1,8,256]{2,1,0:T(8,128)S(1)}, u32[]{:S(2)}, u32[]{:S(2)}) collective-permute-start(f32[1,8,256]{2,1,0:T(8,128)S(1)} %add.34), channel_id=1, source_target_pairs={{0,2},{1,3},{2,0},{3,1},{4,6},{5,7},{6,4},{7,5},{8,10},{9,11},{10,... | collective-permute-start | bytes 24584 | tf_op jit(solution)/shard_map/ppermute | solution.py:318
  183.1 7.6 %collective-permute-start.11 = (f32[1,8,256]{2,1,0:T(8,128)S(1)}, f32[1,8,256]{2,1,0:T(8,128)S(1)}, u32[]{:S(2)}, u32[]{:S(2)}) collective-permute-start(f32[1,8,256]{2,1,0:T(8,128)S(1)} %get-tuple-element.54), channel_id=1, source_target_pairs={{0,128},{8,136},{16,144},{24,152},{32,160},{40,168},{48,176},{56,1... | collective-permute-start | bytes 24584 | tf_op jit(solution)/shard_map/ppermute | solution.py:318
  190.7 6.1 %collective-permute-start.14 = (f32[2,8,256]{2,1,0:T(8,128)S(1)}, f32[2,8,256]{2,1,0:T(8,128)S(1)}, u32[]{:S(2)}, u32[]{:S(2)}) collective-permute-start(f32[2,8,256]{2,1,0:T(8,128)S(1)} %pad_maximum_fusion.1), channel_id=1, source_target_pairs={{0,96},{8,104},{16,112},{24,120},{32,64},{40,72},{48,80},{56,88},{... | collective-permute-start | bytes 49160 | tf_op jit(solution)/shard_map/ppermute | solution.py:318
  192.2 4.6 %collective-permute-start.13 = (f32[2,8,256]{2,1,0:T(8,128)S(1)}, f32[2,8,256]{2,1,0:T(8,128)S(1)}, u32[]{:S(2)}, u32[]{:S(2)}) collective-permute-start(f32[2,8,256]{2,1,0:T(8,128)S(1)} %pad_maximum_fusion.1), channel_id=1, source_target_pairs={{0,32},{8,40},{16,48},{24,56},{32,0},{40,8},{48,16},{56,24},{64,96... | collective-permute-start | bytes 49160 | tf_op jit(solution)/shard_map/ppermute | solution.py:318
  192.2 4.6 %collective-permute-start.12 = (f32[2,8,256]{2,1,0:T(8,128)S(1)}, f32[2,8,256]{2,1,0:T(8,128)S(1)}, u32[]{:S(2)}, u32[]{:S(2)}) collective-permute-start(f32[2,8,256]{2,1,0:T(8,128)S(1)} %pad_maximum_fusion.1), channel_id=1, source_target_pairs={{0,64},{8,72},{16,80},{24,88},{32,96},{40,104},{48,112},{56,120},{... | collective-permute-start | bytes 49160 | tf_op jit(solution)/shard_map/ppermute | solution.py:318
  196.9 7.7 %collective-permute-start.15 = (f32[8,8,256]{2,1,0:T(8,128)S(1)}, f32[8,8,256]{2,1,0:T(8,128)S(1)}, u32[]{:S(2)}, u32[]{:S(2)}) collective-permute-start(f32[8,8,256]{2,1,0:T(8,128)S(1)} %get-tuple-element.62), channel_id=1, source_target_pairs={{0,16},{8,24},{16,0},{24,8},{32,48},{40,56},{48,32},{56,40},{64,80... | collective-permute-start | bytes 196616 | tf_op jit(solution)/shard_map/ppermute | solution.py:318
  199.3 1.2 copy-start.4
  200.5 7.3 %copy-start.14 = (bf16[128,512]{1,0:T(8,128)(2,1)S(1)}, bf16[128,512]{1,0:T(8,128)(2,1)}, u32[]{:S(2)}) copy-start(bf16[128,512]{1,0:T(8,128)(2,1)} %copy-done.13) | copy-start | bytes 393220
  202.2 5.6 %copy-start.8 = (bf16[128,2048]{1,0:T(8,128)(2,1)S(1)}, bf16[128,2048]{1,0:T(8,128)(2,1)}, u32[]{:S(2)}) copy-start(bf16[128,2048]{1,0:T(8,128)(2,1)} %lower_cot.1) | copy-start | bytes 1572868
  202.2 4.7 %collective-permute-start.17 = (f32[8,8,256]{2,1,0:T(8,128)S(1)}, f32[8,8,256]{2,1,0:T(8,128)S(1)}, u32[]{:S(2)}, u32[]{:S(2)}) collective-permute-start(f32[8,8,256]{2,1,0:T(8,128)S(1)} %get-tuple-element.62), channel_id=1, source_target_pairs={{0,24},{8,16},{16,8},{24,0},{32,56},{40,48},{48,40},{56,32},{64,88... | collective-permute-start | bytes 196616 | tf_op jit(solution)/shard_map/ppermute | solution.py:318
  202.2 4.6 %collective-permute-start.16 = (f32[8,8,256]{2,1,0:T(8,128)S(1)}, f32[8,8,256]{2,1,0:T(8,128)S(1)}, u32[]{:S(2)}, u32[]{:S(2)}) collective-permute-start(f32[8,8,256]{2,1,0:T(8,128)S(1)} %get-tuple-element.62), channel_id=1, source_target_pairs={{0,8},{8,0},{16,24},{24,16},{32,40},{40,32},{48,56},{56,48},{64,72... | collective-permute-start | bytes 196616 | tf_op jit(solution)/shard_map/ppermute | solution.py:318
  209.2 1.2 copy-start.3
Sparse Core Ops, SparseCore 0:
  14.1 57.4 all-gather.1
  113.7 58.6 reduce-scatter.1

commit v5 on v4

--- a/solution.py
+++ b/solution.py
@@ -126,20 +126,13 @@
         used[:, k * width : (k + 1) * width] = value.T.astype(bf16)
 
 
-def reverse(number, experts):
-    result, bits = number * 0, experts.bit_length() - 1
-    for bit in range(bits):
-        result = result | (((number >> bit) & 1) << (bits - 1 - bit))
-    return result
-
-
-def router_kernel(experts, own, cot, rows, sent, out, grad):
+def router_kernel(experts, own, cot, rows, sent, out, grad, total):
     count = cot.shape[0]
     features = (rows.shape[1] * fold) // (fold + 1)
     part = features // fold
-    total = jnp.zeros((count, 128), f32)
+    sums = jnp.zeros((count, 128), f32)
     for start in range(0, features, 128):
-        total += cot[:, start : start + 128].astype(f32) * sent[:, start : start + 128].astype(f32)
+        sums += cot[:, start : start + 128].astype(f32) * sent[:, start : start + 128].astype(f32)
     extra = jnp.zeros((count, 128), f32)
     for start in range(features, features + part, 128):
         extra += cot[:, start : start + 128].astype(f32) * sent[:, start : start + 128].astype(f32)
@@ -151,21 +144,22 @@
     lane = lax.broadcasted_iota(i32, (count, count), 1)
     row = lax.broadcasted_iota(i32, (count, count), 0) % fold
     lefts = []
-    for k, value in enumerate((total, extra.reshape(count, 128))):
+    for k, value in enumerate((sums, extra.reshape(count, 128))):
         inner = jnp.sum(value, axis=1, keepdims=True)
         change = inner * (facts[:, 3 * k + 1 : 3 * k + 2] + facts[:, 3 * k + 2 : 3 * k + 3])
         partner = facts[:, 3 * k : 3 * k + 1].astype(i32)
-        grad[k] = jnp.where(column == me, change, 0.0) - jnp.where(column == partner, change, 0.0)
-        away = reverse(partner ^ me, experts)
-        at = column if k == 0 else lane % experts
-        left = jnp.where(at == 0, change, 0.0) - jnp.where(at == away, change, 0.0)
+        signed = jnp.where(column == me, change, 0.0) - jnp.where(column == partner, change, 0.0)
+        grad[k] = signed
         if k == 1:
-            left = jnp.where(lane // experts == row, left, 0.0)
-        lefts.append(left.astype(bf16))
+            at = lane % experts
+            signed = jnp.where(at == me, change, 0.0) - jnp.where(at == partner, change, 0.0)
+            signed = jnp.where(lane // experts == row, signed, 0.0)
+        lefts.append(signed.astype(bf16))
     ninth = dot(lefts[1], rows[:, features:], contract_first)
     for c in range(fold):
         piece = dot(lefts[0], rows[:, c * part : (c + 1) * part], contract_first)
-        out[:, c, :] = piece[:experts] + ninth[c * experts : (c + 1) * experts]
+        total[:, c, :] = piece[:experts] + ninth[c * experts : (c + 1) * experts]
+    out[...] = total[...].reshape(out.shape).astype(bf16)
 
 
 def upper_kernel(upper, back, mix, out):
@@ -202,17 +196,22 @@
         )
 
 
+def unpack(packed, rows, experts):
+    features = rows.shape[1]
+    part = features // fold
+    main = experts * fold
+    place = lax.broadcasted_iota(i32, (main, main), 0)
+    order = lax.broadcasted_iota(i32, (main, main), 1)
+    order = order == (place % experts) * fold + place // experts
+    extra = dot(order.astype(f32).astype(bf16), packed[:, features : features + part]).astype(bf16)
+    rows[:main, :] = packed[:, :features]
+    for c in range(fold):
+        rows[main:, c * part : (c + 1) * part] = extra[c * experts : (c + 1) * experts]
+
+
 def hidden_kernel(experts, cot, projected, down, joined, rows):
-    features, units = down.shape
-    part = features // fold
-    main = experts * fold
-    order = lax.broadcasted_iota(i32, (main, main), 1)
-    place = lax.broadcasted_iota(i32, (main, main), 0)
-    order = order == (place % experts) * fold + place // experts
-    extra = dot(order.astype(f32).astype(bf16), cot[:, features : features + part]).astype(bf16)
-    rows[:main, :] = cot[:, :features]
-    for c in range(fold):
-        rows[main:, c * part : (c + 1) * part] = extra[c * experts : (c + 1) * experts]
+    units = down.shape[1]
+    unpack(cot, rows, experts)
     back = dot(rows[...], down[...])
     gate, up = projected[:, :units], projected[:, units:]
     gate_sig = jax.nn.sigmoid(gate)
@@ -230,7 +229,8 @@
         result = dot(hidden[...], down[c * part : (c + 1) * part, :], contract_last)
         out[:, c * part : (c + 1) * part] = result[:main].astype(bf16)
         total += unfolded(result[main:].astype(bf16), c, experts)
-    out[:, features:] = total.astype(bf16)
+    out[:, features : features + part] = total.astype(bf16)
+    out[:, features + part :] = jnp.zeros((main, part), bf16)
 
 
 def halves(value):
@@ -269,9 +269,9 @@
         out[...] = total[...].astype(bf16)
 
 
-def add_kernel(*refs):
-    *parts, out = refs
-    out[...] = sum([ref[...] for ref in parts[1:]], parts[0][...])
+def reduce_kernel(back, out):
+    folded = back[...].astype(f32).reshape(back.shape[0] // fold, *out.shape)
+    out[...] = jnp.sum(folded, axis=0)
 
 
 def split_kernel(both, gate_up, down):
@@ -283,7 +283,7 @@
 def order_kernel(experts, own, parts, out):
     part = parts.shape[2]
     for e in range(experts):
-        piece = parts[reverse(own[0] ^ e, experts)]
+        piece = parts[own[0] ^ e]
         for c in range(fold):
             out[e : e + 1, c * part : (c + 1) * part] = piece[c : c + 1]
 
@@ -306,7 +306,7 @@
     result, bit = [], 1
     while bit < size:
         if 2 * bit < size:
-            result.append((2 * bit, bit, 3 * bit))
+            result.append((bit, 2 * bit, 3 * bit))
             bit *= 4
         else:
             result.append((bit,))
@@ -316,12 +316,6 @@
 
 def swap(array, axis, flip):
     return lax.ppermute(array, axis, [(i, i ^ flip) for i in range(lax.axis_size(axis))])
-
-
-def unpack(block, features, experts):
-    part = features // fold
-    extra = block[:, features : features + part].reshape(experts, features)
-    return jnp.concatenate([block[:, :features], extra], axis=0)
 
 
 def body(
@@ -347,14 +341,19 @@
     def shape(*dims, kind=bf16):
         return jax.ShapeDtypeStruct(dims, kind)
 
+    first = (ids, keep, lower_out, gate_up_weight[0], down_weight[0].T)
+    shapes = (
+        shape(gate_up_weight.shape[1], 3 * hidden_units),
+        shape(main, features + part),
+    )
     weights, packed = call(
         lambda *refs: send_rows_kernel(experts, *refs),
-        (
-            shape(gate_up_weight.shape[1], 3 * hidden_units),
-            shape(main, features + part),
-        ),
-        10**6,
-    )(ids, keep, lower_out, gate_up_weight[0], down_weight[0].T)
+        shapes,
+        10**6,
+        grid=(1,),
+        in_specs=[pl.BlockSpec(array.shape, lambda i: (0, 0)) for array in first],
+        out_specs=[pl.BlockSpec(array.shape, lambda i: (0, 0)) for array in shapes],
+    )(*first)
     weights = lax.all_gather(weights, "dp", axis=0, tiled=True)
     gate_up, down = weights[:, : 2 * hidden_units], weights[:, 2 * hidden_units :]
     arrived = exchange(packed, experts)
@@ -370,7 +369,9 @@
     cot_packed, arrived = lax.optimization_barrier((cot_packed, arrived))
     cot_arrived = exchange(cot_packed, experts)
 
-    row_block = unpack(arrived, features, experts)
+    row_block = call(
+        lambda packed, rows: unpack(packed, rows, experts), shape(main + experts, features), 10**6
+    )(arrived)
     projected = jnp.dot(row_block, gate_up, preferred_element_type=f32)
     gate_part = projected[:, :hidden_units]
     up_part = projected[:, hidden_units:]
@@ -380,12 +381,34 @@
     slots = main + experts
     out_packed = call(
         lambda *refs: outputs_kernel(experts, *refs),
-        shape(main, features + part),
+        shape(main, features + 2 * part),
         10**6,
     )(hidden, down)
 
     own = lax.axis_index("expert").astype(i32).reshape(1)
+    out_packed, logit_grad = call(
+        lambda *refs: router_kernel(experts, *refs),
+        (shape(main, features + 2 * part), shape(2, main, 128, kind=f32)),
+        10**6,
+        aliases={3: 0},
+        grid=(1,),
+        in_specs=[
+            scalar,
+            whole,
+            whole,
+            pl.BlockSpec((main, features + 2 * part), lambda i: (0, 0)),
+        ],
+        out_specs=(
+            pl.BlockSpec((main, part), lambda i: (0, fold + 1)),
+            pl.BlockSpec((2, main, 128), lambda i: (0, 0, 0)),
+        ),
+        scratch_shapes=[pltpu.VMEM((experts, fold, part), f32)],
+    )(own, cot_arrived, arrived, out_packed)
+    out_packed, cot_arrived, hidden, row_block, logit_grad = lax.optimization_barrier(
+        (out_packed, cot_arrived, hidden, row_block, logit_grad)
+    )
     out_back = exchange(out_packed, experts)
+
     joined, grads = call(
         lambda *refs: hidden_kernel(experts, *refs),
         (shape(slots, 2 * hidden_units), shape(slots, features)),
@@ -404,14 +427,6 @@
         ],
         out_specs=pl.BlockSpec((part, 3 * hidden_units), lambda i: (i, 0)),
     )(row_block, joined, grads, hidden)
-    both, cot_arrived = lax.optimization_barrier((both, cot_arrived))
-    router_part, logit_grad = call(
-        lambda *refs: router_kernel(experts, *refs),
-        (shape(experts, fold, part, kind=f32), shape(2, main, 128, kind=f32)),
-        10**6,
-        in_specs=[scalar, whole, whole, whole],
-        out_specs=(whole, whole),
-    )(own, cot_arrived, arrived, out_packed)
     both = lax.psum_scatter(both, "dp", scatter_dimension=0, tiled=True)
     rows_packed = call(
         lambda *refs: rows_kernel(experts, *refs),
@@ -430,27 +445,25 @@
             pltpu.VMEM((2 * main, 3 * experts), bf16),
         ],
     )(joined, weights, logit_grad, router)
-    for count, flips in enumerate(rounds(experts)):
-        piece = router_part.shape[0] // (len(flips) + 1)
-        parts = [router_part[:piece]]
-        for place, flip in enumerate(flips, 1):
-            parts.append(swap(router_part[place * piece : (place + 1) * piece], "expert", flip))
-        if count == 0:
-            *parts, out_back = lax.optimization_barrier((*parts, out_back))
-            router_part = call(add_kernel, shape(piece, fold, part, kind=f32), 149500 * 10**6)(*parts)
-            rows_packed, router_part = lax.optimization_barrier((rows_packed, router_part))
-            rows_back = exchange(rows_packed, experts)
-        else:
-            router_part = sum(parts[1:], parts[0])
+    router_part = call(
+        reduce_kernel,
+        shape(fold, part, kind=f32),
+        300000 * 10**6,
+        grid=(1,),
+        in_specs=[pl.BlockSpec((main, part), lambda i: (0, fold + 1))],
+        out_specs=pl.BlockSpec((fold, part), lambda i: (0, 0)),
+    )(out_back)
+    rows_packed, router_part = lax.optimization_barrier((rows_packed, router_part))
+    rows_back = exchange(rows_packed, experts)
     copies = lax.axis_size("dp")
     flips = [1] + [flip for flip in range(2, copies, 2)]
     router_part = router_part + (swap(router_part, "dp", 1) if copies > 1 else 0.0)
     parts = [swap(router_part, "dp", flip) for flip in flips[1:]]
-    router_all = sum(parts, router_part)
+    router_all = sum(parts, router_part)[None]
     upper_input = call(upper_kernel, shape(tokens, features, kind=f32), 10**6)(
         upper_out, out_back, mix
     )
-    for flips in reversed(rounds(experts)):
+    for flips in rounds(experts):
         parts = [swap(router_all, "expert", flip) for flip in flips]
         router_all = jnp.concatenate([router_all, *parts], axis=0)
     router_grad = call(

time: 221 us -> 194 us (0.88)
  starting transfers between devices: 63 us -> 46.3 us
  waiting for transfers between devices: 82.2 us -> 72.9 us
  Pallas kernels: 37.5 us -> 41.1 us
    ppermute x18 -> x11, waiting for transfers between devices: 38.4 us -> 20.1 us  [swap(): lax.ppermute(array, axis, [(i, i ^ flip) for i in range(lax.axis_size(axi...]
    ppermute x18 -> x11, starting transfers between devices: 28.6 us -> 16.7 us  [swap(): lax.ppermute(array, axis, [(i, i ^ flip) for i in range(lax.axis_size(axi...]
    all_to_all x4, waiting for transfers between devices: 37 us -> 46.1 us  [exchange(): lax.all_to_all(array.reshape(experts, fold, width), 'expert', split_axis=...]
    all_to_all x4, starting transfers between devices: 34.3 us -> 29.5 us  [exchange(): lax.all_to_all(array.reshape(experts, fold, width), 'expert', split_axis=...]
    pallas_call x3 -> x4, Pallas kernels: 5.42 us -> 8.05 us  [the longest x1 3.42 us: body(): call(lambda *refs: router_kernel(experts, *refs), (shape(main, features +...]
    slice x5 -> x0, local copies, waits for them, and re-layouts: 2.27 us -> none  [the longest x1 1.32 us: unpack(): return jnp.concatenate([block[:, :features], extra], axis=0)]
    unnamed x50 -> x54, local copies, waits for them, and re-layouts: 9.29 us -> 10.4 us
  transfers between devices with their start and end apart: 24 -> 17, of which waited for: 12 -> 11; matrix products, arithmetic and copies ran while one was open for 5% -> 4% of each run, Pallas kernels for 16% -> 18%
where the time goes in v5:
time: 194 us; the launch traced here: 193 us
  waiting for transfers between devices  72.9 us (38%)
  starting transfers between devices  46.3 us (24%)
  Pallas kernels  41.1 us (21%)
  between operations  14.3 us (7%)
  local copies, waits for them, and re-layouts  12.6 us (6%)
  matrix products  5.75 us (3%)
    all_to_all x4, waiting for transfers between devices, exchange(): lax.all_to_all(array.reshape(experts, fold, width), 'expert', split_axis=...  46.1 us
    all_to_all x4, starting transfers between devices, exchange(): lax.all_to_all(array.reshape(experts, fold, width), 'expert', split_axis=...  29.5 us
    ppermute x11, waiting for transfers between devices, swap(): lax.ppermute(array, axis, [(i, i ^ flip) for i in range(lax.axis_size(axi...  20.1 us
    ppermute x11, starting transfers between devices, swap(): lax.ppermute(array, axis, [(i, i ^ flip) for i in range(lax.axis_size(axi...  16.7 us
    unnamed x54, local copies, waits for them, and re-layouts  10.4 us
    pallas_call x1, Pallas kernels, body(): call(lambda *refs: rows_kernel(experts, *refs), shape(main, features + pa...  8.99 us
    pallas_call x1, Pallas kernels, body(): call(grads_kernel, shape(features, 3 * hidden_units), 10 ** 6, grid=(fold...  8.42 us
    all_gather x1, waiting for transfers between devices, body(): weights = lax.all_gather(weights, 'dp', axis=0, tiled=True)  6.67 us
  transfers between devices with their start and end apart: 17, of which 11 were waited for; matrix products, arithmetic and copies ran while one was open for 4% of the time, Pallas kernels for 18%

profile of v5, /device:TPU:2, one launch (start us, length us, event | category | flops | bytes accessed | tf_op | source)
XLA Modules:
  0.0 193.2 jit_solution(3980012273367434799)
XLA Ops:
  7.2 1.1 copy-done.8
  8.3 1.0 copy-done.9
  9.4 1.0 copy-done.12
  10.4 0.7 copy-done.19
  11.0 0.7 copy-done.21
  11.7 2.2 %shard_map.129 = (bf16[256,2112]{1,0:T(8,128)(2,1)}, bf16[256,2304]{1,0:T(8,128)(2,1)}) custom-call(s32[2,128]{1,0:T(2,128)S(1)} %bitcast.32, s32[2,128]{1,0:T(2,128)S(1)} %bitcast.34, bf16[128,2048]{1,0:T(8,128)(2,1)S(1)} %copy-done.9, bf16[256,1408]{1,0:T(8,128)(2,1)S(1)} %bitcast.28, bf16[704,256]{1,0:T(8,128)(2,1)S(1)} %bitcast.29), custom_call_target="tpu_custom_call" | custom-call | flops 1000000 | tf_op jit(solution)/shard_map/pallas_call | solution.py:349
  14.0 11.8 %all-to-all-start = ((bf16[32,8,2304]{2,1,0:T(8,128)(2,1)}), bf16[32,8,2304]{2,1,0:T(8,128)(2,1)}, u32[]{:S(2)}, u32[]{:S(2)}) async-start(bf16[32,8,2304]{2,1,0:T(8,128)(2,1)} %bitcast.7), calls=%async_computation | async-start | bytes 2359296 | tf_op jit(solution)/shard_map/all_to_all | solution.py:299
  25.8 3.0 %shard_map.128 = (bf16[256,2432]{1,0:T(8,128)(2,1)}, bf16[128,1024]{1,0:T(8,128)(2,1)S(1)}, bf16[128,512]{1,0:T(8,128)(2,1)S(1)}) custom-call(s32[2,128]{1,0:T(2,128)S(1)} %bitcast.33, s32[2,128]{1,0:T(2,128)S(1)} %bitcast.35, bf16[128,2048]{1,0:T(8,128)(2,1)S(1)} %copy-done.10, bf16[128,2048]{1,0:T(8,128)(2,1)S(1)} %copy-done.23, f32[32,2048]{1,0:T(8,128)S(1)} %bitcast.30), custom_call_target="tpu_custom_call" | custom-call | flops 299999985664 | tf_op jit(solution)/shard_map/pallas_call | solution.py:360
  28.8 0.7 copy-done.13
  29.5 27.2 %all-to-all-done = bf16[32,8,2304]{2,1,0:T(8,128)(2,1)} async-done(((bf16[32,8,2304]{2,1,0:T(8,128)(2,1)}), bf16[32,8,2304]{2,1,0:T(8,128)(2,1)}, u32[]{:S(2)}, u32[]{:S(2)}) %all-to-all-start) | async-done | bytes 1179680 | tf_op jit(solution)/shard_map/all_to_all | solution.py:299
  56.7 5.6 %all-to-all-start.1 = ((bf16[32,8,2432]{2,1,0:T(8,128)(2,1)}), bf16[32,8,2432]{2,1,0:T(8,128)(2,1)S(1)}, u32[]{:S(2)}, u32[]{:S(2)}) async-start(bf16[32,8,2432]{2,1,0:T(8,128)(2,1)} %bitcast.9), calls=%async_computation.1 | async-start | bytes 2490368 | tf_op jit(solution)/shard_map/all_to_all | solution.py:299
  62.3 1.5 shard_map.130.rows
  63.8 1.0 copy-done.1
  64.8 6.7 %all-gather.2.cloned.1.call-done.refs_1_ = bf16[2048,2112]{1,0:T(8,128)(2,1)} async-done(((bf16[256,2112]{1,0:T(8,128)(2,1)}), bf16[2048,2112]{1,0:T(8,128)(2,1)}) %all-gather.2.cloned.1.call-update) | async-done | bytes 8650768 | tf_op jit(solution)/shard_map/all_gather | solution.py:357
  71.5 2.2 %slice.19.refs_1_.refs_2_ = bf16[2048,704]{1,0:T(8,128)(2,1)S(1)} slice(bf16[2048,2112]{1,0:T(8,128)(2,1)} %all-gather.2.cloned.1.call-done.refs_1_), slice={[0:2048], [1408:2112]} | slice | bytes 5767168 | tf_op jit(solution)/shard_map/slice | solution.py:358
  73.7 5.7 %fusion.refs_1_ = f32[288,1408]{1,0:T(8,128)S(1)} fusion(bf16[288,2048]{1,0:T(8,128)(2,1)S(1)} %copy-done.2, bf16[2048,2112]{1,0:T(8,128)(2,1)} %all-gather.2.cloned.1.call-done.refs_1_), kind=kOutput, calls=%fused_computation | convolution fusion | flops 1660944384 | bytes 8568832 | tf_op jit(solution)/shard_map/dot_general | solution.py:375
  79.8 2.9 %shard_map.131.refs_3_ = bf16[256,2560]{1,0:T(8,128)(2,1)} custom-call(bf16[288,704]{1,0:T(8,128)(2,1)S(1)} %fusion.2.refs_0_.hidden, bf16[2048,704]{1,0:T(8,128)(2,1)S(1)} %slice.19.refs_1_.refs_2_), custom_call_target="tpu_custom_call" | custom-call | flops 1000000 | tf_op jit(solution)/shard_map/pallas_call | solution.py:382
  82.7 10.2 %all-to-all-done.1 = bf16[32,8,2432]{2,1,0:T(8,128)(2,1)S(1)} async-done(((bf16[32,8,2432]{2,1,0:T(8,128)(2,1)}), bf16[32,8,2432]{2,1,0:T(8,128)(2,1)S(1)}, u32[]{:S(2)}, u32[]{:S(2)}) %all-to-all-start.1) | async-done | bytes 1245216 | tf_op jit(solution)/shard_map/all_to_all | solution.py:299
  92.9 3.4 %shard_map.132 = (bf16[256,2560]{1,0:T(8,128)(2,1)}, f32[2,256,128]{2,1,0:T(8,128)S(1)}) custom-call(s32[1]{0:T(128)} %bitcast.refs_0_.own, bf16[256,2432]{1,0:T(8,128)(2,1)S(1)} %bitcast.25, bf16[256,2304]{1,0:T(8,128)(2,1)} %bitcast.8.packed.refs_2_, bf16[256,2560]{1,0:T(8,128)(2,1)} %shard_map.131.refs_3_), custom_call_target="tpu_custom_call", output_to_operand_aliasing={{0}: (3, {})} | custom-call | flops 1000000 | tf_op jit(solution)/shard_map/pallas_call | solution.py:389
  96.4 0.7 copy-done.17
  97.1 6.0 %all-to-all-start.2 = ((bf16[32,8,2560]{2,1,0:T(8,128)(2,1)}), bf16[32,8,2560]{2,1,0:T(8,128)(2,1)}, u32[]{:S(2)}, u32[]{:S(2)}) async-start(bf16[32,8,2560]{2,1,0:T(8,128)(2,1)} %bitcast.11), calls=%async_computation.2 | async-start | bytes 2621440 | tf_op jit(solution)/shard_map/all_to_all | solution.py:299
  103.2 3.4 %shard_map.134 = (bf16[288,1408]{1,0:T(8,128)(2,1)S(1)}, bf16[288,2048]{1,0:T(8,128)(2,1)S(1)}) custom-call(bf16[256,2432]{1,0:T(8,128)(2,1)S(1)} %bitcast.26, f32[288,1408]{1,0:T(8,128)S(1)} %fusion.refs_1_, bf16[2048,704]{1,0:T(8,128)(2,1)} %copy-done), custom_call_target="tpu_custom_call" | custom-call | flops 1000000 | tf_op jit(solution)/shard_map/pallas_call | solution.py:412
  106.5 8.4 %shard_map.138 = bf16[2048,2112]{1,0:T(8,128)(2,1)} custom-call(bf16[288,2048]{1,0:T(8,128)(2,1)S(1)} %copy-done.3, bf16[288,1408]{1,0:T(8,128)(2,1)S(1)} %get-tuple-element.37.refs_0_.joined, bf16[288,2048]{1,0:T(8,128)(2,1)S(1)} %get-tuple-element.42.cot, bf16[288,704]{1,0:T(8,128)(2,1)S(1)} %fusion.2.refs_0_.hidden), custom_call_target="tpu_custom_call" | custom-call | flops 1000000 | tf_op jit(solution)/shard_map/pallas_call | solution.py:417
  114.9 0.9 copy-done.4
  115.9 1.1 copy-done.5
  117.1 9.0 %shard_map.135 = bf16[256,2304]{1,0:T(8,128)(2,1)} custom-call(bf16[288,1408]{1,0:T(8,128)(2,1)S(1)} %copy-done.5, bf16[2048,2112]{1,0:T(8,128)(2,1)} %all-gather.2.cloned.1.call-done.refs_1_, f32[2,256,128]{2,1,0:T(8,128)S(1)} %copy-done.18, f32[32,2048]{1,0:T(8,128)S(1)} %bitcast.31), custom_call_target="tpu_custom_call" | custom-call | flops 1000000 | tf_op jit(solution)/shard_map/pallas_call | solution.py:431
  126.1 8.7 %all-to-all-done.2 = bf16[32,8,2560]{2,1,0:T(8,128)(2,1)} async-done(((bf16[32,8,2560]{2,1,0:T(8,128)(2,1)}), bf16[32,8,2560]{2,1,0:T(8,128)(2,1)}, u32[]{:S(2)}, u32[]{:S(2)}) %all-to-all-start.2) | async-done | bytes 1310752 | tf_op jit(solution)/shard_map/all_to_all | solution.py:299
  134.8 0.9 shard_map.136
  135.7 6.1 %all-to-all-start.3 = ((bf16[32,8,2304]{2,1,0:T(8,128)(2,1)}), bf16[32,8,2304]{2,1,0:T(8,128)(2,1)S(1)}, u32[]{:S(2)}, u32[]{:S(2)}) async-start(bf16[32,8,2304]{2,1,0:T(8,128)(2,1)} %bitcast.13), calls=%async_computation.3 | async-start | bytes 2359296 | tf_op jit(solution)/shard_map/all_to_all | solution.py:299
  142.1 1.2 collective-permute-done
  143.3 3.0 %collective-permute-start.3 = (f32[8,256]{1,0:T(8,128)S(1)}, f32[8,256]{1,0:T(8,128)S(1)}, u32[]{:S(2)}, u32[]{:S(2)}) collective-permute-start(f32[8,256]{1,0:T(8,128)S(1)} %add.18), channel_id=1, source_target_pairs={{0,6},{1,7},{2,4},{3,5},{4,2},{5,3},{6,0},{7,1},{8,14},{9,15},{10,... | collective-permute-start | bytes 24584 | tf_op jit(solution)/shard_map/ppermute | solution.py:318
  147.4 0.9 collective-permute-done.3
  148.3 3.3 %collective-permute-done.2 = f32[8,256]{1,0:T(8,128)S(1)} collective-permute-done((f32[8,256]{1,0:T(8,128)S(1)}, f32[8,256]{1,0:T(8,128)S(1)}, u32[]{:S(2)}, u32[]{:S(2)}) %collective-permute-start.2) | collective-permute-done | bytes 8224 | tf_op jit(solution)/shard_map/ppermute | solution.py:318
  151.7 1.6 collective-permute-start.6
  153.2 0.8 collective-permute-start.5
  154.1 1.8 collective-permute-start.4
  155.9 2.6 %collective-permute-done.5 = f32[1,8,256]{2,1,0:T(8,128)S(1)} collective-permute-done((f32[1,8,256]{2,1,0:T(8,128)S(1)}, f32[1,8,256]{2,1,0:T(8,128)S(1)}, u32[]{:S(2)}, u32[]{:S(2)}) %collective-permute-start.5) | collective-permute-done | bytes 8224 | tf_op jit(solution)/shard_map/ppermute | solution.py:318
  158.4 3.3 %collective-permute-start.9 = (f32[4,8,256]{2,1,0:T(8,128)S(1)}, f32[4,8,256]{2,1,0:T(8,128)S(1)}, u32[]{:S(2)}, u32[]{:S(2)}) collective-permute-start(f32[4,8,256]{2,1,0:T(8,128)S(1)} %pad_maximum_fusion), channel_id=1, source_target_pairs={{0,96},{8,104},{16,112},{24,120},{32,64},{40,72},{48,80},{56,88},{... | collective-permute-start | bytes 98312 | tf_op jit(solution)/shard_map/ppermute | solution.py:318
  161.7 1.1 collective-permute-start.7
  162.8 5.0 %collective-permute-done.7 = f32[4,8,256]{2,1,0:T(8,128)S(1)} collective-permute-done((f32[4,8,256]{2,1,0:T(8,128)S(1)}, f32[4,8,256]{2,1,0:T(8,128)S(1)}, u32[]{:S(2)}, u32[]{:S(2)}) %collective-permute-start.7) | collective-permute-done | bytes 32800 | tf_op jit(solution)/shard_map/ppermute | solution.py:318
  167.8 3.1 %collective-permute-done.8 = f32[4,8,256]{2,1,0:T(8,128)S(1)} collective-permute-done((f32[4,8,256]{2,1,0:T(8,128)S(1)}, f32[4,8,256]{2,1,0:T(8,128)S(1)}, u32[]{:S(2)}, u32[]{:S(2)}) %collective-permute-start.8) | collective-permute-done | bytes 32800 | tf_op jit(solution)/shard_map/ppermute | solution.py:318
  170.9 3.7 %collective-permute-start.10 = (f32[16,8,256]{2,1,0:T(8,128)S(1)}, f32[16,8,256]{2,1,0:T(8,128)S(1)}, u32[]{:S(2)}, u32[]{:S(2)}) collective-permute-start(f32[16,8,256]{2,1,0:T(8,128)S(1)} %get-tuple-element.51), channel_id=1, source_target_pairs={{0,128},{8,136},{16,144},{24,152},{32,160},{40,168},{48,176},{56,1... | collective-permute-start | bytes 393224 | tf_op jit(solution)/shard_map/ppermute | solution.py:318
  174.6 3.1 %shard_map.133 = f32[128,2048]{1,0:T(8,128)} custom-call(f32[128,2048]{1,0:T(8,128)S(1)} %copy-done.7, bf16[256,2560]{1,0:T(8,128)(2,1)} %bitcast.12.back, bf16[128,1024]{1,0:T(8,128)(2,1)S(1)} %copy-done.14), custom_call_target="tpu_custom_call" | custom-call | flops 1000000 | tf_op jit(solution)/shard_map/pallas_call | solution.py:463
  177.7 4.1 %collective-permute-done.10 = f32[16,8,256]{2,1,0:T(8,128)S(1)} collective-permute-done((f32[16,8,256]{2,1,0:T(8,128)S(1)}, f32[16,8,256]{2,1,0:T(8,128)S(1)}, u32[]{:S(2)}, u32[]{:S(2)}) %collective-permute-start.10) | collective-permute-done | bytes 131104 | tf_op jit(solution)/shard_map/ppermute | solution.py:318
  181.8 0.8 shard_map.140
  182.6 1.4 shard_map.137
  184.0 1.2 copy-done.6
  185.3 1.1 shard_map.139
  (63 shorter events, 2.1 us)
Async XLA Ops:
  7.2 64.3 %all-gather.2.cloned.1.call-start = ((), (), s32[]{:S(2)}) async-start(), calls=%async_computation.5 | async-start | bytes 10027008 | tf_op jit(solution)/shard_map/all_gather | solution.py:357
  7.2 1.1 copy-start.8
  8.3 1.0 copy-start.9
  9.4 1.0 copy-start.12
  10.3 0.7 copy-start.19
  11.0 0.7 copy-start.21
  13.9 11.9 %copy-start.10 = (bf16[128,2048]{1,0:T(8,128)(2,1)S(1)}, bf16[128,2048]{1,0:T(8,128)(2,1)}, u32[]{:S(2)}) copy-start(bf16[128,2048]{1,0:T(8,128)(2,1)} %refs_2_.3) | copy-start | bytes 1572868
  13.9 11.9 %copy-start.15 = (f32[2048,32]{0,1:T(8,128)S(1)}, f32[2048,32]{0,1:T(8,128)}, u32[]{:S(2)}) copy-start(f32[2048,32]{0,1:T(8,128)} %param.15) | copy-start | bytes 786436
  13.9 11.9 %copy-start.20 = (s32[128,2]{0,1:T(2,128)S(1)}, s32[128,2]{0,1:T(2,128)}, u32[]{:S(2)}) copy-start(s32[128,2]{0,1:T(2,128)} %param.16) | copy-start | bytes 3076
  13.9 11.9 %copy-start.22 = (s32[128,2]{0,1:T(2,128)S(1)}, s32[128,2]{0,1:T(2,128)}, u32[]{:S(2)}) copy-start(s32[128,2]{0,1:T(2,128)} %param.17) | copy-start | bytes 3076
  14.0 11.9 %copy-start.23 = (bf16[128,2048]{1,0:T(8,128)(2,1)S(1)}, bf16[128,2048]{1,0:T(8,128)(2,1)}, u32[]{:S(2)}) copy-start(bf16[128,2048]{1,0:T(8,128)(2,1)} %refs_3_.1) | copy-start | bytes 1572868
  14.0 42.7 %all-to-all-start = ((bf16[32,8,2304]{2,1,0:T(8,128)(2,1)}), bf16[32,8,2304]{2,1,0:T(8,128)(2,1)}, u32[]{:S(2)}, u32[]{:S(2)}) async-start(bf16[32,8,2304]{2,1,0:T(8,128)(2,1)} %bitcast.7), calls=%async_computation | async-start | bytes 2359296 | tf_op jit(solution)/shard_map/all_to_all | solution.py:299
  28.8 0.7 copy-start.13
  56.7 36.2 %all-to-all-start.1 = ((bf16[32,8,2432]{2,1,0:T(8,128)(2,1)}), bf16[32,8,2432]{2,1,0:T(8,128)(2,1)S(1)}, u32[]{:S(2)}, u32[]{:S(2)}) async-start(bf16[32,8,2432]{2,1,0:T(8,128)(2,1)} %bitcast.9), calls=%async_computation.1 | async-start | bytes 2490368 | tf_op jit(solution)/shard_map/all_to_all | solution.py:299
  63.8 1.0 copy-start.1
  71.5 2.2 %copy-start.2 = (bf16[288,2048]{1,0:T(8,128)(2,1)S(1)}, bf16[288,2048]{1,0:T(8,128)(2,1)}, u32[]{:S(2)}) copy-start(bf16[288,2048]{1,0:T(8,128)(2,1)} %copy-done.1) | copy-start | bytes 3538948
  73.7 6.1 %copy-start = (bf16[2048,704]{1,0:T(8,128)(2,1)}, bf16[2048,704]{1,0:T(8,128)(2,1)S(1)}, u32[]{:S(2)}) copy-start(bf16[2048,704]{1,0:T(8,128)(2,1)S(1)} %slice.19.refs_1_.refs_2_) | copy-start | bytes 8650756
  96.4 0.7 copy-start.17
  97.1 37.7 %all-to-all-start.2 = ((bf16[32,8,2560]{2,1,0:T(8,128)(2,1)}), bf16[32,8,2560]{2,1,0:T(8,128)(2,1)}, u32[]{:S(2)}, u32[]{:S(2)}) async-start(bf16[32,8,2560]{2,1,0:T(8,128)(2,1)} %bitcast.11), calls=%async_computation.2 | async-start | bytes 2621440 | tf_op jit(solution)/shard_map/all_to_all | solution.py:299
  103.1 80.9 %reduce-scatter.2.cloned.1.call-start = ((), (), s32[]{:S(2)}) async-start(), calls=%async_computation.6 | async-start | bytes 10027008 | tf_op jit(solution)/shard_map/reduce_scatter | solution.py:430
  103.1 3.4 %copy-start.3 = (bf16[288,2048]{1,0:T(8,128)(2,1)S(1)}, bf16[288,2048]{1,0:T(8,128)(2,1)}, u32[]{:S(2)}) copy-start(bf16[288,2048]{1,0:T(8,128)(2,1)} %copy-done.1) | copy-start | bytes 3538948
  114.9 0.9 copy-start.4
  115.8 1.1 copy-start.5
  115.8 1.2 copy-start.16
  115.8 1.3 copy-start.18
  135.7 38.9 %copy-start.7 = (f32[128,2048]{1,0:T(8,128)S(1)}, f32[128,2048]{1,0:T(8,128)}, u32[]{:S(2)}) copy-start(f32[128,2048]{1,0:T(8,128)} %upper.1) | copy-start | bytes 3145732
  135.7 38.9 %copy-start.14 = (bf16[128,1024]{1,0:T(8,128)(2,1)S(1)}, bf16[128,1024]{1,0:T(8,128)(2,1)}, u32[]{:S(2)}) copy-start(bf16[128,1024]{1,0:T(8,128)(2,1)} %copy-done.13) | copy-start | bytes 786436
  135.7 46.9 %all-to-all-start.3 = ((bf16[32,8,2304]{2,1,0:T(8,128)(2,1)}), bf16[32,8,2304]{2,1,0:T(8,128)(2,1)S(1)}, u32[]{:S(2)}, u32[]{:S(2)}) async-start(bf16[32,8,2304]{2,1,0:T(8,128)(2,1)} %bitcast.13), calls=%async_computation.3 | async-start | bytes 2359296 | tf_op jit(solution)/shard_map/all_to_all | solution.py:299
  141.9 1.4 collective-permute-start
  143.3 5.0 %collective-permute-start.3 = (f32[8,256]{1,0:T(8,128)S(1)}, f32[8,256]{1,0:T(8,128)S(1)}, u32[]{:S(2)}, u32[]{:S(2)}) collective-permute-start(f32[8,256]{1,0:T(8,128)S(1)} %add.18), channel_id=1, source_target_pairs={{0,6},{1,7},{2,4},{3,5},{4,2},{5,3},{6,0},{7,1},{8,14},{9,15},{10,... | collective-permute-start | bytes 24584 | tf_op jit(solution)/shard_map/ppermute | solution.py:318
  146.3 5.3 %collective-permute-start.2 = (f32[8,256]{1,0:T(8,128)S(1)}, f32[8,256]{1,0:T(8,128)S(1)}, u32[]{:S(2)}, u32[]{:S(2)}) collective-permute-start(f32[8,256]{1,0:T(8,128)S(1)} %add.18), channel_id=1, source_target_pairs={{0,4},{1,5},{2,6},{3,7},{4,0},{5,1},{6,2},{7,3},{8,12},{9,13},{10,... | collective-permute-start | bytes 24584 | tf_op jit(solution)/shard_map/ppermute | solution.py:318
  147.0 4.7 %collective-permute-start.1 = (f32[8,256]{1,0:T(8,128)S(1)}, f32[8,256]{1,0:T(8,128)S(1)}, u32[]{:S(2)}, u32[]{:S(2)}) collective-permute-start(f32[8,256]{1,0:T(8,128)S(1)} %add.18), channel_id=1, source_target_pairs={{0,2},{1,3},{2,0},{3,1},{4,6},{5,7},{6,4},{7,5},{8,10},{9,11},{10,... | collective-permute-start | bytes 24584 | tf_op jit(solution)/shard_map/ppermute | solution.py:318
  151.7 4.2 %collective-permute-start.6 = (f32[1,8,256]{2,1,0:T(8,128)S(1)}, f32[1,8,256]{2,1,0:T(8,128)S(1)}, u32[]{:S(2)}, u32[]{:S(2)}) collective-permute-start(f32[1,8,256]{2,1,0:T(8,128)S(1)} %get-tuple-element.50), channel_id=1, source_target_pairs={{0,24},{8,16},{16,8},{24,0},{32,56},{40,48},{48,40},{56,32},{64,88... | collective-permute-start | bytes 24584 | tf_op jit(solution)/shard_map/ppermute | solution.py:318
  153.2 5.2 %collective-permute-start.5 = (f32[1,8,256]{2,1,0:T(8,128)S(1)}, f32[1,8,256]{2,1,0:T(8,128)S(1)}, u32[]{:S(2)}, u32[]{:S(2)}) collective-permute-start(f32[1,8,256]{2,1,0:T(8,128)S(1)} %get-tuple-element.50), channel_id=1, source_target_pairs={{0,16},{8,24},{16,0},{24,8},{32,48},{40,56},{48,32},{56,40},{64,80... | collective-permute-start | bytes 24584 | tf_op jit(solution)/shard_map/ppermute | solution.py:318
  154.1 4.4 %collective-permute-start.4 = (f32[1,8,256]{2,1,0:T(8,128)S(1)}, f32[1,8,256]{2,1,0:T(8,128)S(1)}, u32[]{:S(2)}, u32[]{:S(2)}) collective-permute-start(f32[1,8,256]{2,1,0:T(8,128)S(1)} %get-tuple-element.50), channel_id=1, source_target_pairs={{0,8},{8,0},{16,24},{24,16},{32,40},{40,32},{48,56},{56,48},{64,72... | collective-permute-start | bytes 24584 | tf_op jit(solution)/shard_map/ppermute | solution.py:318
  158.4 12.5 %collective-permute-start.9 = (f32[4,8,256]{2,1,0:T(8,128)S(1)}, f32[4,8,256]{2,1,0:T(8,128)S(1)}, u32[]{:S(2)}, u32[]{:S(2)}) collective-permute-start(f32[4,8,256]{2,1,0:T(8,128)S(1)} %pad_maximum_fusion), channel_id=1, source_target_pairs={{0,96},{8,104},{16,112},{24,120},{32,64},{40,72},{48,80},{56,88},{... | collective-permute-start | bytes 98312 | tf_op jit(solution)/shard_map/ppermute | solution.py:318
  161.7 9.2 %collective-permute-start.8 = (f32[4,8,256]{2,1,0:T(8,128)S(1)}, f32[4,8,256]{2,1,0:T(8,128)S(1)}, u32[]{:S(2)}, u32[]{:S(2)}) collective-permute-start(f32[4,8,256]{2,1,0:T(8,128)S(1)} %pad_maximum_fusion), channel_id=1, source_target_pairs={{0,64},{8,72},{16,80},{24,88},{32,96},{40,104},{48,112},{56,120},{... | collective-permute-start | bytes 98312 | tf_op jit(solution)/shard_map/ppermute | solution.py:318
  161.7 6.1 %collective-permute-start.7 = (f32[4,8,256]{2,1,0:T(8,128)S(1)}, f32[4,8,256]{2,1,0:T(8,128)S(1)}, u32[]{:S(2)}, u32[]{:S(2)}) collective-permute-start(f32[4,8,256]{2,1,0:T(8,128)S(1)} %pad_maximum_fusion), channel_id=1, source_target_pairs={{0,32},{8,40},{16,48},{24,56},{32,0},{40,8},{48,16},{56,24},{64,96... | collective-permute-start | bytes 98312 | tf_op jit(solution)/shard_map/ppermute | solution.py:318
  170.9 10.9 %collective-permute-start.10 = (f32[16,8,256]{2,1,0:T(8,128)S(1)}, f32[16,8,256]{2,1,0:T(8,128)S(1)}, u32[]{:S(2)}, u32[]{:S(2)}) collective-permute-start(f32[16,8,256]{2,1,0:T(8,128)S(1)} %get-tuple-element.51), channel_id=1, source_target_pairs={{0,128},{8,136},{16,144},{24,152},{32,160},{40,168},{48,176},{56,1... | collective-permute-start | bytes 393224 | tf_op jit(solution)/shard_map/ppermute | solution.py:318
  174.6 8.0 %copy-start.11 = (bf16[128,2048]{1,0:T(8,128)(2,1)S(1)}, bf16[128,2048]{1,0:T(8,128)(2,1)}, u32[]{:S(2)}) copy-start(bf16[128,2048]{1,0:T(8,128)(2,1)} %lower_cot.1) | copy-start | bytes 1572868
  184.0 1.2 copy-start.6
Sparse Core Ops, SparseCore 0:
  14.0 57.4 all-gather.1
  116.0 58.9 reduce-scatter.1
